TPU v7x, 512 devices: a whole 4x8x8 slice. The times are simulated.
512 devices in a mesh: obj: 32 (over x, z), pat: 16 (over y, core).
Axes of the slice: x: 4, y: 8, z: 8, core: 2. Of those that a mesh axis runs over, the one named last changes fastest.
Arguments:
- obj_tiles: float32 [32, 2, 512, 512], P('obj', None, 'pat'), may hold values from -5 to 5
- probe_wave: float32 [2, 256, 256], replicated, may hold values from -6 to 6
- amplitudes: bfloat16 [32, 16, 4, 256, 256], P('obj', 'pat'), may hold values from 0.25 to 4
- offsets: int32 [32, 16, 4, 2], P('obj', 'pat'), may hold values from 0 to 504, as said below
- live_count: int32 [32, 16], P('obj', 'pat'), may hold values from 1 to 4, as said below
Outputs:
- object_step: float32 [32, 2, 512, 512], P('obj', None, 'pat')
Inputs may be any that keep to these rules, and one draw needn't show every extreme that they name: `offsets`: multiples of 8; a patch starting there covers cells of its own tile and of the tiles to the right, below and below-right. Slots 0 to live_count - 1 of a device are used, the rest are not read.
All inputs are finite; a program needn't handle non-finite values.
Results may differ from a plain program's by a relative error of at most 0.012.
The roundings to bfloat16 on the way count: a program that leaves them out, or rounds other values in their place, can miss the bound.
Values sent between devices are 32-bit elements; how exact they have to be, the bound alone decides.
No kernel may reach another device: no remote copies, remote signals or barrier semaphores. Data moves between devices by JAX's collectives and lax.ppermute only.
A program may use at most 64 MiB of HBM per device.

v0:
```python
import jax
import jax.numpy as jnp
from jax import lax
from jax.sharding import PartitionSpec as P

GRID_C = 4


def passed_along(value, axis, steps):
    count = lax.axis_size(axis)
    initial, last = (max(0, -steps), min(count, count - steps))
    return lax.ppermute(value, axis, [(source, source + steps) for source in range(initial, last)])


def dft_blocks(side_len):
    index_line = jnp.arange(side_len, dtype=jnp.int32)
    products = index_line[:, None] * index_line[None, :] % side_len
    angles = 2.0 * 3.141592653589793 / side_len * products.astype(jnp.float32)
    cos_part = jnp.cos(angles) / jnp.sqrt(jnp.float32(side_len))
    sin_part = -jnp.sin(angles) / jnp.sqrt(jnp.float32(side_len))
    left_table = jnp.concatenate(
        [jnp.concatenate([cos_part, -sin_part], 1), jnp.concatenate([sin_part, cos_part], 1)], 0
    )
    right_table = jnp.concatenate(
        [jnp.concatenate([cos_part, sin_part], 1), jnp.concatenate([-sin_part, cos_part], 1)], 0
    )
    return (left_table.astype(jnp.bfloat16), right_table.astype(jnp.bfloat16))


def position_terms(extended, row_at, col_at, probe_wave, pattern, left_table, right_table):
    side_len = probe_wave.shape[1]
    zero_at = jnp.zeros((), jnp.int32)
    patch_cells = lax.dynamic_slice(extended, (zero_at, row_at, col_at), (2, side_len, side_len))
    probe_re = probe_wave[0]
    probe_im = probe_wave[1]
    wave_re = probe_re * patch_cells[0] - probe_im * patch_cells[1]
    wave_im = probe_re * patch_cells[1] + probe_im * patch_cells[0]
    wave_stack = jnp.concatenate([wave_re, wave_im], 0).astype(jnp.bfloat16)
    half_way = jnp.dot(left_table, wave_stack, preferred_element_type=jnp.float32).astype(
        jnp.bfloat16
    )
    half_side = jnp.concatenate([half_way[:side_len], half_way[side_len:]], 1)
    far_field = jnp.dot(half_side, right_table, preferred_element_type=jnp.float32)
    far_re = far_field[:, :side_len]
    far_im = far_field[:, side_len:]
    ratio_amp = pattern.astype(jnp.float32) / jnp.sqrt(far_re * far_re + far_im * far_im + 0.01)
    corrected = (far_field * jnp.concatenate([ratio_amp, ratio_amp], 1)).astype(jnp.bfloat16)
    half_back = jnp.dot(corrected, left_table, preferred_element_type=jnp.float32).astype(
        jnp.bfloat16
    )
    stacked_back = jnp.concatenate([half_back[:, :side_len], half_back[:, side_len:]], 0)
    near_field = jnp.dot(right_table, stacked_back, preferred_element_type=jnp.float32)
    delta_re = near_field[:side_len] - wave_re
    delta_im = near_field[side_len:] - wave_im
    return jnp.stack(
        [
            probe_re * delta_re + probe_im * delta_im,
            probe_re * delta_im - probe_im * delta_re,
            probe_re * probe_re + probe_im * probe_im,
        ]
    )


def gather_rows(blocks):
    return lax.all_gather(blocks, "pat", axis=2, tiled=True)


def fetch_right(cells, col_pos):
    moved = passed_along(cells, "obj", -1)
    return jnp.where(col_pos == GRID_C - 1, jnp.zeros_like(moved), moved)


def fetch_down(cells):
    return passed_along(cells, "obj", -GRID_C)


def push_down(sums):
    return passed_along(sums, "obj", GRID_C)


def push_right(sums, col_pos):
    moved = passed_along(sums, "obj", 1)
    return jnp.where(col_pos == 0, jnp.zeros_like(moved), moved)


def sum_rows(blocks):
    return lax.psum_scatter(blocks, "pat", scatter_dimension=2, tiled=True)


def local(obj_tiles, probe_wave, amplitudes, offsets, live_count):
    side_len = probe_wave.shape[1]
    own_rows = obj_tiles[0]
    tile_side = own_rows.shape[2]
    col_pos = lax.axis_index("obj") % GRID_C
    whole_tile = gather_rows(own_rows[None])[0]
    upper_cells = jnp.concatenate(
        [whole_tile, fetch_right(whole_tile[:, :, :side_len], col_pos)], 2
    )
    extended = jnp.concatenate([upper_cells, fetch_down(upper_cells[:, :side_len])], 1)
    left_table, right_table = dft_blocks(side_len)
    patterns = amplitudes[0, 0]
    corners = offsets[0, 0]
    live_now = live_count[0, 0]
    zero_at = jnp.zeros((), jnp.int32)
    channels = 3
    start = jnp.zeros((channels, tile_side + side_len, tile_side + side_len), jnp.float32)

    def place(slot, totals):
        row_at = corners[slot, 0]
        col_at = corners[slot, 1]
        terms = position_terms(
            extended, row_at, col_at, probe_wave, patterns[slot], left_table, right_table
        )
        terms = jnp.where(slot < live_now, terms, jnp.zeros_like(terms))
        current = lax.dynamic_slice(
            totals, (zero_at, row_at, col_at), (channels, side_len, side_len)
        )
        return lax.dynamic_update_slice(totals, current + terms, (zero_at, row_at, col_at))

    totals = lax.fori_loop(0, patterns.shape[0], lambda slot, totals: place(slot, totals), start)
    moved_down = push_down(totals[:, tile_side:])
    upper_sum = totals[:, :tile_side].at[:, :side_len].add(moved_down)
    moved_right = push_right(upper_sum[:, :, tile_side:], col_pos)
    own_sum = upper_sum[:, :, :tile_side].at[:, :, :side_len].add(moved_right)
    summed = sum_rows(own_sum[None])[0]
    weights = summed[2] + 1.0
    return jnp.stack([summed[0] / weights, summed[1] / weights])[None]


def solution(mesh):
    in_specs = (
        P("obj", None, "pat", None),
        P(),
        P("obj", "pat", None, None, None),
        P("obj", "pat", None, None),
        P("obj", "pat"),
    )
    out_specs = P("obj", None, "pat", None)
    return jax.shard_map(local, mesh=mesh, in_specs=in_specs, out_specs=out_specs, check_vma=False)
```

profile of v0, /device:TPU:1, one launch (start us, length us, event | category | flops | bytes accessed | tf_op | source)
XLA Modules:
  0.0 494.7 jit_solution(15200268305640823094)
XLA Ops:
  6.5 1.7 copy.13
  8.3 49.0 %all-gather.2.cloned.1.call-done = f32[1,2,512,512]{3,1,0,2:T(2,128)} async-done(((f32[1,2,32,512]{3,1,0,2:T(2,128)}), f32[1,2,512,512]{3,1,0,2:T(2,128)}) %all-gather.2.cloned.1.call-update) | async-done | bytes 2097168 | tf_op jit(solution)/shard_map/all_gather | solution.py:65
  57.3 2.7 slice.217
  60.0 1.3 collective-permute-start
  61.4 25.4 %collective-permute-done = f32[2,512,256]{2,0,1:T(2,128)} collective-permute-done((f32[2,512,256]{2,0,1:T(2,128)}, f32[2,512,256]{2,0,1:T(2,128)}, u32[]{:S(2)}, u32[]{:S(2)}) %collective-permute-start) | collective-permute-done | bytes 1048608 | tf_op jit(solution)/shard_map/ppermute | solution.py:12
  86.7 1.7 broadcast_select_fusion
  88.4 1.9 pad_maximum_fusion.1
  90.3 1.3 collective-permute-start.1
  91.8 1.0 fusion.39
  92.8 1.1 negate_convert_fusion
  94.1 37.9 %collective-permute-done.1 = f32[2,256,768]{2,0,1:T(2,128)} collective-permute-done((f32[2,256,768]{2,0,1:T(2,128)}, f32[2,256,768]{2,0,1:T(2,128)}, u32[]{:S(2)}, u32[]{:S(2)}) %collective-permute-start.1) | collective-permute-done | bytes 1572896 | tf_op jit(solution)/shard_map/ppermute | solution.py:12
  132.0 13.4 %pad_maximum_fusion = f32[2,768,768]{2,0,1:T(2,128)} fusion(f32[2,256,768]{2,0,1:T(2,128)} %collective-permute-done.1, f32[2,512,256]{2,0,1:T(2,128)S(1)} %copy-done.5, f32[2,512,512]{2,0,1:T(2,128)} %bitcast.102), kind=kLoop, calls=%fused_computation.48 | loop fusion | flops 2359296 | bytes 9437184 | tf_op jit(solution)/shard_map/concatenate | solution.py:99
  145.4 3.4 broadcast_in_dim.19.clone
  148.9 87.9 %while.17 = (s32[]{:T(128)}, f32[3,768,768]{2,1,0:T(8,128)}, s32[4,2]{0,1:T(2,128)S(1)}, s32[]{:T(128)}, f32[2,256,256]{1,2,0:T(8,128)S(1)}, /*index=5*/f32[2,76...) while((s32[]{:T(128)}, f32[3,768,768]{2,1,0:T(8,128)}, ...), condition=%wide.region_1.2_spmd, body=%wide.region_0.1_spmd.sunk | while | flops 541327360 | bytes 26083664 | solution.py:120
  149.5 0.6 constant_dynamic-slice_fusion.7
  153.7 2.6 constant_dynamic-slice_fusion.9
  157.3 1.0 fusion.80
  159.1 1.6 constant_dynamic-slice_fusion.8
  161.4 9.5 %dynamic_update_slice.10 = f32[3,768,768]{2,1,0:T(8,128)} dynamic-update-slice(f32[3,768,768]{2,1,0:T(8,128)} %get-tuple-element.414, f32[3,256,256]{2,1,0:T(8,128)S(1)} %copy.34, s32[]{:T(128)} %constant.143.clone.1..sunk, s32[]{:T(128)S(6)} %select_n.125, s32[]{:T(128)S(6)} %select_n.126) | dynamic-update-slice | bytes 1572868 | tf_op jit(solution)/shard_map/while/body/eval_jaxpr/dynamic_update_slice | solution.py:118
  171.6 0.6 constant_dynamic-slice_fusion.7
  175.7 2.6 constant_dynamic-slice_fusion.9
  179.4 1.0 fusion.80
  181.2 1.6 constant_dynamic-slice_fusion.8
  183.4 9.5 %dynamic_update_slice.10 = f32[3,768,768]{2,1,0:T(8,128)} dynamic-update-slice(f32[3,768,768]{2,1,0:T(8,128)} %get-tuple-element.414, f32[3,256,256]{2,1,0:T(8,128)S(1)} %copy.34, s32[]{:T(128)} %constant.143.clone.1..sunk, s32[]{:T(128)S(6)} %select_n.125, s32[]{:T(128)S(6)} %select_n.126) | dynamic-update-slice | bytes 1572868 | tf_op jit(solution)/shard_map/while/body/eval_jaxpr/dynamic_update_slice | solution.py:118
  193.6 0.6 constant_dynamic-slice_fusion.7
  197.8 2.6 constant_dynamic-slice_fusion.9
  201.4 1.0 fusion.80
  203.2 1.6 constant_dynamic-slice_fusion.8
  205.5 9.2 %dynamic_update_slice.10 = f32[3,768,768]{2,1,0:T(8,128)} dynamic-update-slice(f32[3,768,768]{2,1,0:T(8,128)} %get-tuple-element.414, f32[3,256,256]{2,1,0:T(8,128)S(1)} %copy.34, s32[]{:T(128)} %constant.143.clone.1..sunk, s32[]{:T(128)S(6)} %select_n.125, s32[]{:T(128)S(6)} %select_n.126) | dynamic-update-slice | bytes 1572868 | tf_op jit(solution)/shard_map/while/body/eval_jaxpr/dynamic_update_slice | solution.py:118
  215.3 0.6 constant_dynamic-slice_fusion.7
  219.5 2.6 constant_dynamic-slice_fusion.9
  223.2 1.0 fusion.80
  225.0 1.6 constant_dynamic-slice_fusion.8
  227.2 9.5 %dynamic_update_slice.10 = f32[3,768,768]{2,1,0:T(8,128)} dynamic-update-slice(f32[3,768,768]{2,1,0:T(8,128)} %get-tuple-element.414, f32[3,256,256]{2,1,0:T(8,128)S(1)} %copy.34, s32[]{:T(128)} %constant.143.clone.1..sunk, s32[]{:T(128)S(6)} %select_n.125, s32[]{:T(128)S(6)} %select_n.126) | dynamic-update-slice | bytes 1572868 | tf_op jit(solution)/shard_map/while/body/eval_jaxpr/dynamic_update_slice | solution.py:118
  236.8 1.8 slice.202
  238.6 42.7 %collective-permute-start.2 = (f32[3,256,768]{2,1,0:T(8,128)S(1)}, f32[3,256,768]{2,1,0:T(8,128)S(1)}, u32[]{:S(2)}, u32[]{:S(2)}) collective-permute-start(f32[3,256,768]{2,1,0:T(8,128)S(1)} %slice.202), channel_id=1, source_target_pairs={{0,64},{16,80},{32,96},{48,112},{64,128},{80,144},{96,160},{112,17... | collective-permute-start | bytes 7077896 | tf_op jit(solution)/shard_map/ppermute | solution.py:12
  281.2 2.6 slice.200
  283.9 92.0 %collective-permute-done.2 = f32[3,256,768]{2,1,0:T(8,128)S(1)} collective-permute-done((f32[3,256,768]{2,1,0:T(8,128)S(1)}, f32[3,256,768]{2,1,0:T(8,128)S(1)}, u32[]{:S(2)}, u32[]{:S(2)}) %collective-permute-start.2) | collective-permute-done | bytes 2359328 | tf_op jit(solution)/shard_map/ppermute | solution.py:12
  375.9 2.0 add_dynamic-update-slice_fusion
  377.9 2.1 copy-done
  380.0 1.4 slice.222
  381.4 1.4 collective-permute-start.3
  382.8 3.8 slice_bitcast_fusion
  386.6 30.0 %collective-permute-done.3 = f32[3,512,256]{2,1,0:T(8,128)S(1)} collective-permute-done((f32[3,512,256]{2,1,0:T(8,128)}, f32[3,512,256]{2,1,0:T(8,128)S(1)}, u32[]{:S(2)}, u32[]{:S(2)}) %collective-permute-start.3) | collective-permute-done | bytes 1572896 | tf_op jit(solution)/shard_map/ppermute | solution.py:12
  416.6 2.8 fusion.29
  419.4 66.8 %reduce-scatter.2.cloned.1.call-done = f32[1,3,32,512]{3,2,1,0:T(8,128)} async-done(((f32[1,3,512,512]{3,2,1,0:T(8,128)}), f32[1,3,32,512]{3,2,1,0:T(8,128)}) %reduce-scatter.2.cloned.1.call-update) | async-done | bytes 196624 | tf_op jit(solution)/shard_map/reduce_scatter | solution.py:87
  486.3 0.9 fusion.41
  487.2 0.7 maximum_bitcast_fusion
  (86 shorter events, 10.2 us)
Async XLA Ops:
  6.5 50.8 %all-gather.2.cloned.1.call-start = ((), (), s32[]{:S(2)}) async-start(), calls=%async_computation.1 | async-start | bytes 2228224 | tf_op jit(solution)/shard_map/all_gather | solution.py:65
  8.2 478.1 %reduce-scatter.2.cloned.1.call-start = ((), (), s32[]{:S(2)}) async-start(), calls=%async_computation.2 | async-start | bytes 3342336 | tf_op jit(solution)/shard_map/reduce_scatter | solution.py:87
  57.3 31.1 %copy-start.3 = (f32[1,2,512,512]{3,1,0,2:T(2,128)S(1)}, f32[1,2,512,512]{3,1,0,2:T(2,128)}, u32[]{:S(2)}) copy-start(f32[1,2,512,512]{3,1,0,2:T(2,128)} %all-gather.2.cloned.1.call-done) | copy-start | bytes 6291460
  60.0 26.7 %collective-permute-start = (f32[2,512,256]{2,0,1:T(2,128)}, f32[2,512,256]{2,0,1:T(2,128)}, u32[]{:S(2)}, u32[]{:S(2)}) collective-permute-start(f32[2,512,256]{2,0,1:T(2,128)} %slice.217), channel_id=1, source_target_pairs={{16,0},{32,16},{48,32},{64,48},{80,64},{96,80},{112,96},{128,112},... | collective-permute-start | bytes 3145736 | tf_op jit(solution)/shard_map/ppermute | solution.py:12
  61.3 30.3 %copy-start.6 = (f32[2,256,256]{2,1,0:T(8,128)S(1)}, f32[2,256,256]{2,1,0:T(8,128)}, u32[]{:S(2)}) copy-start(f32[2,256,256]{2,1,0:T(8,128)} %param.12) | copy-start | bytes 1572868
  88.4 1.9 copy-start.4
  90.3 41.7 %collective-permute-start.1 = (f32[2,256,768]{2,0,1:T(2,128)}, f32[2,256,768]{2,0,1:T(2,128)}, u32[]{:S(2)}, u32[]{:S(2)}) collective-permute-start(f32[2,256,768]{2,0,1:T(2,128)} %pad_maximum_fusion.1), channel_id=1, source_target_pairs={{64,0},{80,16},{96,32},{112,48},{128,64},{144,80},{160,96},{176,11... | collective-permute-start | bytes 4718600 | tf_op jit(solution)/shard_map/ppermute | solution.py:12
  91.6 40.4 %copy-start.5 = (f32[2,512,256]{2,0,1:T(2,128)S(1)}, f32[2,512,256]{2,0,1:T(2,128)}, u32[]{:S(2)}) copy-start(f32[2,512,256]{2,0,1:T(2,128)} %copy-done.4) | copy-start | bytes 3145732
  145.4 3.4 copy-start.7
  148.9 9.5 %copy-start.1 = (bf16[512,512]{1,0:T(8,128)(2,1)}, bf16[512,512]{1,0:T(8,128)(2,1)S(1)}, u32[]{:S(2)}) copy-start(bf16[512,512]{1,0:T(8,128)(2,1)S(1)} %get-tuple-element.433) | copy-start | bytes 1572868 | tf_op jit(solution)/shard_map/while
  161.1 9.8 %copy-start.2 = (bf16[512,512]{1,0:T(8,128)(2,1)S(1)}, bf16[512,512]{1,0:T(8,128)(2,1)}, u32[]{:S(2)}) copy-start(bf16[512,512]{1,0:T(8,128)(2,1)} %copy-done.1) | copy-start | bytes 1572868 | tf_op jit(solution)/shard_map/while
  170.9 9.5 %copy-start.1 = (bf16[512,512]{1,0:T(8,128)(2,1)}, bf16[512,512]{1,0:T(8,128)(2,1)S(1)}, u32[]{:S(2)}) copy-start(bf16[512,512]{1,0:T(8,128)(2,1)S(1)} %get-tuple-element.433) | copy-start | bytes 1572868 | tf_op jit(solution)/shard_map/while
  183.1 9.8 %copy-start.2 = (bf16[512,512]{1,0:T(8,128)(2,1)S(1)}, bf16[512,512]{1,0:T(8,128)(2,1)}, u32[]{:S(2)}) copy-start(bf16[512,512]{1,0:T(8,128)(2,1)} %copy-done.1) | copy-start | bytes 1572868 | tf_op jit(solution)/shard_map/while
  193.0 9.5 %copy-start.1 = (bf16[512,512]{1,0:T(8,128)(2,1)}, bf16[512,512]{1,0:T(8,128)(2,1)S(1)}, u32[]{:S(2)}) copy-start(bf16[512,512]{1,0:T(8,128)(2,1)S(1)} %get-tuple-element.433) | copy-start | bytes 1572868 | tf_op jit(solution)/shard_map/while
  205.2 9.5 %copy-start.2 = (bf16[512,512]{1,0:T(8,128)(2,1)S(1)}, bf16[512,512]{1,0:T(8,128)(2,1)}, u32[]{:S(2)}) copy-start(bf16[512,512]{1,0:T(8,128)(2,1)} %copy-done.1) | copy-start | bytes 1572868 | tf_op jit(solution)/shard_map/while
  214.7 9.5 %copy-start.1 = (bf16[512,512]{1,0:T(8,128)(2,1)}, bf16[512,512]{1,0:T(8,128)(2,1)S(1)}, u32[]{:S(2)}) copy-start(bf16[512,512]{1,0:T(8,128)(2,1)S(1)} %get-tuple-element.433) | copy-start | bytes 1572868 | tf_op jit(solution)/shard_map/while
  227.0 9.8 %copy-start.2 = (bf16[512,512]{1,0:T(8,128)(2,1)S(1)}, bf16[512,512]{1,0:T(8,128)(2,1)}, u32[]{:S(2)}) copy-start(bf16[512,512]{1,0:T(8,128)(2,1)} %copy-done.1) | copy-start | bytes 1572868 | tf_op jit(solution)/shard_map/while
  238.6 137.3 %collective-permute-start.2 = (f32[3,256,768]{2,1,0:T(8,128)S(1)}, f32[3,256,768]{2,1,0:T(8,128)S(1)}, u32[]{:S(2)}, u32[]{:S(2)}) collective-permute-start(f32[3,256,768]{2,1,0:T(8,128)S(1)} %slice.202), channel_id=1, source_target_pairs={{0,64},{16,80},{32,96},{48,112},{64,128},{80,144},{96,160},{112,17... | collective-permute-start | bytes 7077896 | tf_op jit(solution)/shard_map/ppermute | solution.py:12
  377.9 2.1 copy-start
  381.4 35.2 %collective-permute-start.3 = (f32[3,512,256]{2,1,0:T(8,128)}, f32[3,512,256]{2,1,0:T(8,128)S(1)}, u32[]{:S(2)}, u32[]{:S(2)}) collective-permute-start(f32[3,512,256]{2,1,0:T(8,128)} %slice.222), channel_id=1, source_target_pairs={{0,16},{16,32},{32,48},{48,64},{64,80},{80,96},{96,112},{112,128},... | collective-permute-start | bytes 4718600 | tf_op jit(solution)/shard_map/ppermute | solution.py:12
Sparse Core Ops, SparseCore 0:
  9.5 47.7 all-gather.1
  419.6 66.6 reduce-scatter.1
where the time goes:
time: 498 us; the launch traced here: 495 us
  waiting for transfers between devices  301 us (60%)
  local copies, waits for them, and re-layouts  80.1 us (16%)
  starting transfers between devices  46.6 us (9%)
  other arithmetic  30.6 us (6%)
  loops' own time  17.3 us (3%)
  between operations  13.6 us (3%)
  matrix products  5.18 us (1%)
    ppermute x4, waiting for transfers between devices, passed_along(): lax.ppermute(value, axis, [(source, source + steps) for source in range(i...  185 us
    reduce_scatter x1, waiting for transfers between devices, sum_rows(): return lax.psum_scatter(blocks, 'pat', scatter_dimension=2, tiled=True)  66.8 us
    all_gather x1, waiting for transfers between devices, gather_rows(): return lax.all_gather(blocks, 'pat', axis=2, tiled=True)  49 us
    ppermute x4, starting transfers between devices, passed_along(): lax.ppermute(value, axis, [(source, source + steps) for source in range(i...  46.6 us
    dynamic_update_slice x8, local copies, waits for them, and re-layouts, place(): lax.dynamic_update_slice(totals, current + terms, (zero_at, row_at, col_at))  38.8 us
    another operation x1, loops' own time, local(): lax.fori_loop(0, patterns.shape[0], lambda slot, totals: place(slot, tota...  17.3 us
    concatenate x1, other arithmetic, local(): jnp.concatenate([upper_cells, fetch_down(upper_cells[:, :side_len])], 1)  13.4 us
    slice x4, local copies, waits for them, and re-layouts, position_terms(): wave_re = probe_re * patch_cells[0] - probe_im * patch_cells[1]  10.4 us
  transfers between devices with their start and end apart: 6, of which 6 were waited for; matrix products, arithmetic and copies ran while one was open for 2% of the time, Pallas kernels for 0%

commit v1 on v0

v1 whole, which is shorter than its diff:
```python
import jax
import jax.numpy as jnp
from jax import lax
from jax.experimental import pallas as pl
from jax.experimental.pallas import tpu as pltpu
from jax.sharding import PartitionSpec as P

GRID_C = 4
TILES = 32
WORKERS = 16
SLOTS = 4
SIDE = 256
TILE = 512
WIDE = TILE + SIDE
OWN = TILE // WORKERS
LOW = SIDE // WORKERS
ROWS = OWN + LOW
SPAN = SIDE + 128
PAD = 48


def dft_blocks(side_len):
    index_line = jnp.arange(side_len, dtype=jnp.int32)
    products = index_line[:, None] * index_line[None, :] % side_len
    angles = 2.0 * 3.141592653589793 / side_len * products.astype(jnp.float32)
    cos_part = jnp.cos(angles) / jnp.sqrt(jnp.float32(side_len))
    sin_part = -jnp.sin(angles) / jnp.sqrt(jnp.float32(side_len))
    left_table = jnp.concatenate(
        [jnp.concatenate([cos_part, -sin_part], 1), jnp.concatenate([sin_part, cos_part], 1)], 0
    )
    right_table = jnp.concatenate(
        [jnp.concatenate([cos_part, sin_part], 1), jnp.concatenate([-sin_part, cos_part], 1)], 0
    )
    return (left_table.astype(jnp.bfloat16), right_table.astype(jnp.bfloat16))


def low_row(worker):
    return TILE + worker % 8 * (2 * LOW) + worker // 8 * LOW


def slots_kernel(
    corners, live, parity, cells_hbm, probe, pattern, left, right,
    keep_hbm, send_hbm, cells, sums, wave, half, sem,
):
    fetches = []
    for worker in range(WORKERS):
        low = low_row(worker)
        fetches.append(pltpu.make_async_copy(
            cells_hbm.at[worker, 0:OWN], cells.at[OWN * worker:OWN * (worker + 1)], sem.at[2 * worker]))
        fetches.append(pltpu.make_async_copy(
            cells_hbm.at[worker, OWN:ROWS], cells.at[low:low + LOW], sem.at[2 * worker + 1]))
    for copy in fetches:
        copy.start()

    def clear(i, _):
        sums[pl.ds(pl.multiple_of(i * 16, 16), 16), :] = jnp.zeros((16, 2 * WIDE), jnp.float32)
        return 0

    lax.fori_loop(0, WIDE // 16, clear, 0)
    for copy in fetches:
        copy.wait()

    def one(slot, _):
        row = corners[slot, 0]
        col = corners[slot, 1]
        base = pl.multiple_of(col // 128 * 128, 128)
        shift = col % 128
        back = (SPAN - shift) % SPAN
        for i in range(4):
            here = slice(64 * i, 64 * i + 64)
            rows = pl.ds(pl.multiple_of(row + 64 * i, 8), 64)
            cell_re = pltpu.roll(cells[rows, pl.ds(base, SPAN)], back, 1)[:, :SIDE]
            cell_im = pltpu.roll(cells[rows, pl.ds(pl.multiple_of(base + WIDE, 128), SPAN)], back, 1)[:, :SIDE]
            probe_re = probe[0, here, :]
            probe_im = probe[1, here, :]
            wave[here, :] = (probe_re * cell_re - probe_im * cell_im).astype(jnp.bfloat16)
            wave[64 * i + SIDE:64 * i + SIDE + 64, :] = (
                probe_re * cell_im + probe_im * cell_re).astype(jnp.bfloat16)
        half_way = jnp.dot(left[...], wave[...], preferred_element_type=jnp.float32).astype(jnp.bfloat16)
        half[:, :SIDE] = half_way[:SIDE]
        half[:, SIDE:] = half_way[SIDE:]
        far = jnp.dot(half[...], right[...], preferred_element_type=jnp.float32)
        far_re = far[:, :SIDE]
        far_im = far[:, SIDE:]
        ratio = pattern[slot].astype(jnp.float32) * lax.rsqrt(far_re * far_re + far_im * far_im + 0.01)
        half[:, :SIDE] = (far_re * ratio).astype(jnp.bfloat16)
        half[:, SIDE:] = (far_im * ratio).astype(jnp.bfloat16)
        half_back = jnp.dot(half[...], left[...], preferred_element_type=jnp.float32).astype(jnp.bfloat16)
        wave[:SIDE, :] = half_back[:, :SIDE]
        wave[SIDE:, :] = half_back[:, SIDE:]
        near = jnp.dot(right[...], wave[...], preferred_element_type=jnp.float32)
        for i in range(4):
            here = slice(64 * i, 64 * i + 64)
            rows = pl.ds(pl.multiple_of(row + 64 * i, 8), 64)
            near_re = near[64 * i:64 * i + 64]
            near_im = near[64 * i + SIDE:64 * i + SIDE + 64]
            probe_re = probe[0, here, :]
            probe_im = probe[1, here, :]
            blank = jnp.zeros((64, 128), jnp.float32)
            term_re = jnp.concatenate([probe_re * near_re + probe_im * near_im, blank], 1)
            term_im = jnp.concatenate([probe_re * near_im - probe_im * near_re, blank], 1)
            sums[rows, pl.ds(base, SPAN)] += pltpu.roll(term_re, shift, 1)
            sums[rows, pl.ds(pl.multiple_of(base + WIDE, 128), SPAN)] += pltpu.roll(term_im, shift, 1)
        return 0

    lax.fori_loop(0, live[0, 0], one, 0)

    def store(own_core):
        copies = []
        for worker in range(WORKERS):
            low = low_row(worker)
            target = keep_hbm if worker % 2 == own_core else send_hbm
            copies.append(pltpu.make_async_copy(
                sums.at[OWN * worker:OWN * (worker + 1)], target.at[worker // 2, 0:OWN], sem.at[2 * worker]))
            copies.append(pltpu.make_async_copy(
                sums.at[low:low + LOW], target.at[worker // 2, OWN:ROWS], sem.at[2 * worker + 1]))
        for copy in copies:
            copy.start()
        for copy in copies:
            copy.wait()

    @pl.when(parity[0] == 0)
    def _():
        store(0)

    @pl.when(parity[0] != 0)
    def _():
        store(1)


def weight_kernel(corners, live, me, probe, weights, padded):
    padded[...] = jnp.zeros_like(padded)
    for i in range(4):
        here = slice(64 * i, 64 * i + 64)
        probe_re = probe[0, here, :]
        probe_im = probe[1, here, :]
        padded[PAD + 64 * i:PAD + 64 * i + 64, 0:SIDE] = probe_re * probe_re + probe_im * probe_im
    weights[...] = jnp.zeros_like(weights)
    worker = me[0]
    own_first = worker * OWN
    low_first = low_row(worker)

    def one(index, _):
        other = index // SLOTS
        slot = index % SLOTS
        row = corners[other, 2 * slot]
        used = slot < live[other]
        col = jnp.where(used, corners[other, 2 * slot + 1], 0)
        base = pl.multiple_of(col // 128 * 128, 128)
        shift = col % 128

        def part(first, count, at):
            start = jnp.where(used, jnp.clip(first - row + PAD, 0, PAD + SIDE), 0)
            piece = padded[pl.ds(pl.multiple_of(start, 8), count), :]
            weights[at:at + count, pl.ds(base, SPAN)] += pltpu.roll(piece, shift, 1)

        part(own_first, OWN, 0)
        part(low_first, LOW, OWN)
        return 0

    lax.fori_loop(0, WORKERS * SLOTS, one, 0)


def smem():
    return pl.BlockSpec(memory_space=pltpu.SMEM)


def vmem():
    return pl.BlockSpec(memory_space=pltpu.VMEM)


def hbm():
    return pl.BlockSpec(memory_space=pl.ANY)


def patch_sums(corners, live, parity, cells, probe, patterns, left, right):
    chunk = jax.ShapeDtypeStruct((WORKERS // 2, ROWS, 2 * WIDE), jnp.float32)
    return pl.pallas_call(
        slots_kernel,
        out_shape=(chunk, chunk),
        in_specs=[smem(), smem(), smem(), hbm(), vmem(), vmem(), vmem(), vmem()],
        out_specs=(hbm(), hbm()),
        scratch_shapes=[
            pltpu.VMEM((WIDE, 2 * WIDE), jnp.float32),
            pltpu.VMEM((WIDE, 2 * WIDE), jnp.float32),
            pltpu.VMEM((2 * SIDE, SIDE), jnp.bfloat16),
            pltpu.VMEM((SIDE, 2 * SIDE), jnp.bfloat16),
            pltpu.SemaphoreType.DMA((2 * WORKERS,)),
        ],
        compiler_params=pltpu.CompilerParams(vmem_limit_bytes=40 * 2**20),
        cost_estimate=pl.CostEstimate(flops=2 * 10**9, bytes_accessed=12 * 10**6, transcendentals=0),
        name="patch_sums",
    )(corners, live, parity, cells, probe, patterns, left, right)


def weight_rows(corners, live, me, probe):
    return pl.pallas_call(
        weight_kernel,
        out_shape=jax.ShapeDtypeStruct((ROWS, WIDE), jnp.float32),
        in_specs=[smem(), smem(), smem(), vmem()],
        out_specs=vmem(),
        scratch_shapes=[pltpu.VMEM((SIDE + 2 * PAD, SPAN), jnp.float32)],
        compiler_params=pltpu.CompilerParams(vmem_limit_bytes=16 * 2**20),
        cost_estimate=pl.CostEstimate(flops=10**7, bytes_accessed=10**6, transcendentals=0),
        name="weight_rows",
    )(corners, live, me, probe)


def moved(value, tile_step, pick):
    pairs = []
    for tile in range(TILES):
        for worker in range(WORKERS):
            target = pick(tile, worker)
            if target is not None and 0 <= tile + tile_step < TILES:
                pairs.append((tile * WORKERS + worker, (tile + tile_step) * WORKERS + target))
    return lax.ppermute(value, ("obj", "pat"), pairs)


def local(obj_tiles, probe_wave, amplitudes, offsets, live_count):
    own = obj_tiles[0]
    me = lax.axis_index("pat").astype(jnp.int32)
    corners = offsets[0, 0]

    own_left = jnp.concatenate([own[0, :, :SIDE], own[1, :, :SIDE]], 1)
    from_right = moved(own_left, -1, lambda tile, worker: worker if tile % GRID_C else None)
    spare_re = jnp.zeros((OWN, 8), jnp.float32)
    spare_re = spare_re.at[0].set(corners.reshape(8).astype(jnp.float32))
    spare_re = spare_re.at[1].set(jnp.broadcast_to(live_count[0, 0].astype(jnp.float32), (8,)))
    upper = jnp.concatenate(
        [own[0], from_right[:, :SIDE], own[1], from_right[:, SIDE:]], 1)
    low_a = moved(upper[:LOW], -GRID_C, lambda tile, worker: worker if worker < 8 else None)
    low_b = moved(upper[LOW:], -GRID_C, lambda tile, worker: worker + 8 if worker < 8 else None)
    marked = jnp.concatenate(
        [own[0], from_right[:, :SIDE - 8], spare_re, own[1], from_right[:, SIDE:]], 1)
    shard = jnp.concatenate([marked, low_a + low_b], 0)
    cells = lax.all_gather(shard, "pat", axis=0, tiled=True).reshape(WORKERS, ROWS, 2 * WIDE)

    left_table, right_table = dft_blocks(SIDE)
    keep, send = patch_sums(
        corners, live_count, (me % 2).reshape(1), cells, probe_wave, amplitudes[0, 0],
        left_table, right_table)
    other = lax.ppermute(send, "pat", [(i, i ^ 1) for i in range(WORKERS)])
    both = (keep + other).reshape(WORKERS // 2 * ROWS, 2 * WIDE)
    summed = lax.psum_scatter(
        both, "pat", scatter_dimension=0, tiled=True,
        axis_index_groups=[list(range(0, WORKERS, 2)), list(range(1, WORKERS, 2))])

    tile_corners = cells[:, 0, WIDE - 8:WIDE].astype(jnp.int32)
    tile_live = cells[:, 1, WIDE - 8].astype(jnp.int32)
    weights = weight_rows(tile_corners, tile_live, me.reshape(1), probe_wave)

    full = jnp.concatenate([summed, weights], 1)
    down_a = moved(full[OWN:], GRID_C, lambda tile, worker: worker if worker < 8 else None)
    down_b = moved(full[OWN:], GRID_C, lambda tile, worker: worker - 8 if worker >= 8 else None)
    upper_sum = (full[:OWN] + jnp.concatenate([down_a, down_b], 0)).reshape(OWN, 3, WIDE)
    to_right = upper_sum[:, :, TILE:].reshape(OWN, 3 * SIDE)
    from_left = moved(to_right, 1, lambda tile, worker: worker if tile % GRID_C != GRID_C - 1 else None)
    total = upper_sum[:, :, :TILE] + jnp.pad(
        from_left.reshape(OWN, 3, SIDE), ((0, 0), (0, 0), (0, TILE - SIDE)))
    weight = total[:, 2]
    over = 1.0 / (weight + 1.0)
    return jnp.stack([
        (total[:, 0] - weight * own[0]) * over,
        (total[:, 1] - weight * own[1]) * over,
    ])[None]


def solution(mesh):
    in_specs = (
        P("obj", None, "pat", None),
        P(),
        P("obj", "pat", None, None, None),
        P("obj", "pat", None, None),
        P("obj", "pat"),
    )
    out_specs = P("obj", None, "pat", None)
    return jax.shard_map(local, mesh=mesh, in_specs=in_specs, out_specs=out_specs, check_vma=False)
```

time: 498 us -> 198 us (0.40)
  the two profiles are of different devices: /device:TPU:1 before, /device:TPU:84 now
where the time goes in v1:
time: 198 us; the launch traced here: 197 us
  waiting for transfers between devices  114 us (58%)
  starting transfers between devices  30.4 us (15%)
  Pallas kernels  22.9 us (12%)
  between operations  14.3 us (7%)
  other arithmetic  10.1 us (5%)
  local copies, waits for them, and re-layouts  5.5 us (3%)
    reduce_scatter x1, waiting for transfers between devices, local(): lax.psum_scatter(both, 'pat', scatter_dimension=0, tiled=True, axis_index...  39 us
    all_gather x1, waiting for transfers between devices, local(): lax.all_gather(shard, 'pat', axis=0, tiled=True)  38.6 us
    ppermute x6, waiting for transfers between devices, moved(): return lax.ppermute(value, ('obj', 'pat'), pairs)  32.4 us
    ppermute x6, starting transfers between devices, moved(): return lax.ppermute(value, ('obj', 'pat'), pairs)  28.2 us
    pallas_call x1, Pallas kernels, patch_sums(): pl.pallas_call(slots_kernel, out_shape=(chunk, chunk), in_specs=[smem(),...  15.2 us
    pallas_call x1, Pallas kernels, weight_rows(): pl.pallas_call(weight_kernel, out_shape=jax.ShapeDtypeStruct((ROWS, WIDE)...  7.77 us
    ppermute x1, waiting for transfers between devices, local(): other = lax.ppermute(send, 'pat', [(i, i ^ 1) for i in range(WORKERS)])  4.28 us
  transfers between devices with their start and end apart: 9, of which 8 were waited for; matrix products, arithmetic and copies ran while one was open for 3% of the time, Pallas kernels for 4%

profile of v1, /device:TPU:84, one launch (start us, length us, event | category | flops | bytes accessed | tf_op | source)
XLA Modules:
  0.0 197.4 jit_solution(4789292910381282386)
XLA Ops:
  6.5 0.8 slice_bitcast_fusion.4
  7.3 0.0 copy-start
  7.4 0.0 copy-start.2
  7.4 2.1 %collective-permute-start = (f32[32,512]{1,0:T(8,128)S(1)}, f32[32,512]{1,0:T(8,128)S(1)}, u32[]{:S(2)}, u32[]{:S(2)}) collective-permute-start(f32[32,512]{1,0:T(8,128)S(1)} %pad_maximum_fusion.7), channel_id=1, source_target_pairs={{16,0},{17,1},{18,2},{19,3},{20,4},{21,5},{22,6},{23,7},{24,8},{25... | collective-permute-start | bytes 196616 | tf_op jit(solution)/shard_map/ppermute | solution.py:216
  9.4 0.9 fusion.17
  10.3 3.7 %collective-permute-done = f32[32,512]{1,0:T(8,128)S(1)} collective-permute-done((f32[32,512]{1,0:T(8,128)S(1)}, f32[32,512]{1,0:T(8,128)S(1)}, u32[]{:S(2)}, u32[]{:S(2)}) %collective-permute-start) | collective-permute-done | bytes 65568 | tf_op jit(solution)/shard_map/ppermute | solution.py:216
  14.1 13.1 %collective-permute-start.2 = (f32[16,1536]{1,0:T(8,128)S(1)}, f32[16,1536]{1,0:T(8,128)S(1)}, u32[]{:S(2)}, u32[]{:S(2)}) collective-permute-start(f32[16,1536]{1,0:T(8,128)S(1)} %get-tuple-element.39), channel_id=1, source_target_pairs={{64,8},{65,9},{66,10},{67,11},{68,12},{69,13},{70,14},{71,15},{80,... | collective-permute-start | bytes 294920 | tf_op jit(solution)/shard_map/ppermute | solution.py:216
  27.2 1.9 collective-permute-start.1
  29.7 0.7 convert_element_type.48
  30.4 0.1 copy.19
  30.5 0.1 convert_element_type.49
  30.7 0.1 concatenate.47
  30.7 7.6 %collective-permute-done.1 = f32[16,1536]{1,0:T(8,128)S(1)} collective-permute-done((f32[16,1536]{1,0:T(8,128)S(1)}, f32[16,1536]{1,0:T(8,128)S(1)}, u32[]{:S(2)}, u32[]{:S(2)}) %collective-permute-start.1) | collective-permute-done | bytes 98336 | tf_op jit(solution)/shard_map/ppermute | solution.py:216
  38.3 0.7 pad_maximum_fusion.4
  39.1 0.0 all-gather.2.cloned.1.call-update
  39.1 0.0 reduce-scatter.2.cloned.1.call-start
  39.1 0.1 copy.21.corners
  39.2 1.0 fusion.10
  40.2 1.1 negate_convert_fusion
  41.3 0.1 fusion.1
  41.4 38.6 %all-gather.2.cloned.1.call-done = f32[768,1536]{1,0:T(8,128)} async-done(((f32[48,1536]{1,0:T(8,128)}), f32[768,1536]{1,0:T(8,128)}) %all-gather.2.cloned.1.call-update) | async-done | bytes 4718608 | tf_op jit(solution)/shard_map/all_gather | solution.py:236
  80.0 2.3 %copy-done.1 = f32[768,1536]{1,0:T(8,128)S(1)} copy-done((f32[768,1536]{1,0:T(8,128)S(1)}, f32[768,1536]{1,0:T(8,128)}, u32[]{:S(2)}) %copy-start.1) | copy-done | bytes 4718616
  82.3 15.2 %patch_sums.1 = (f32[8,48,1536]{2,1,0:T(8,128)S(1)}, f32[8,48,1536]{2,1,0:T(8,128)S(1)}) custom-call(s32[4,2]{1,0:T(4,128)S(1)} %copy.21.corners, s32[1,1]{1,0:T(1,128)S(6)} %copy.45.live, s32[1]{0:T(128)} %bitcast.1.parity, f32[16,48,1536]{2,1,0:T(8,128)S(1)} %bitcast.54, f32[2,256,256]{2,1,0:T(8,128)S(1)} %copy-done, bf16[4,256,256]{2,1,0:T(8,128)(2,1)S(1)} %bitcast.55, ...), custom_call_target="tpu_custom_call" | custom-call | flops 2000000000 | bytes 12000000 | tf_op jit(solution)/shard_map/patch_sums/pallas_call | solution.py:178
  97.5 2.1 %collective-permute-start.3 = (f32[8,48,1536]{2,1,0:T(8,128)S(1)}, f32[8,48,1536]{2,1,0:T(8,128)S(1)}, u32[]{:S(2)}, u32[]{:S(2)}) collective-permute-start(f32[8,48,1536]{2,1,0:T(8,128)S(1)} %get-tuple-element.32), channel_id=1, source_target_pairs={{0,1},{1,0},{2,3},{3,2},{4,5},{5,4},{6,7},{7,6},{8,9},{9,8},{10,11... | collective-permute-start | bytes 7077896 | tf_op jit(solution)/shard_map/ppermute | solution.py:242
  99.7 4.3 %collective-permute-done.3 = f32[8,48,1536]{2,1,0:T(8,128)S(1)} collective-permute-done((f32[8,48,1536]{2,1,0:T(8,128)S(1)}, f32[8,48,1536]{2,1,0:T(8,128)S(1)}, u32[]{:S(2)}, u32[]{:S(2)}) %collective-permute-start.3) | collective-permute-done | bytes 2359328 | tf_op jit(solution)/shard_map/ppermute | solution.py:242
  104.0 1.8 add.63
  105.8 0.0 reduce-scatter.2.cloned.1.call-update
  105.8 0.0 copy-start.3
  105.8 1.3 fusion.15.live
  107.1 0.9 slice_convert_fusion.1
  108.1 7.8 %weight_rows.1 = f32[48,768]{1,0:T(8,128)S(1)} custom-call(s32[16,8]{1,0:T(8,128)S(1)} %bitcast.51, s32[16]{0:T(128)S(1)} %fusion.15.live, s32[1]{0:T(128)} %bitcast.11.me, f32[2,256,256]{2,1,0:T(8,128)S(1)} %copy-done), custom_call_target="tpu_custom_call" | custom-call | flops 10000000 | bytes 1000000 | tf_op jit(solution)/shard_map/weight_rows/pallas_call | solution.py:197
  115.8 39.0 %reduce-scatter.2.cloned.1.call-done = f32[48,1536]{1,0:T(8,128)} async-done(((f32[384,1536]{1,0:T(8,128)}), f32[48,1536]{1,0:T(8,128)}) %reduce-scatter.2.cloned.1.call-update) | async-done | bytes 294928 | tf_op jit(solution)/shard_map/reduce_scatter | solution.py:244
  154.9 0.9 pad_maximum_fusion.6
  155.8 7.1 %collective-permute-start.4 = (f32[16,2304]{1,0:T(8,128)S(1)}, f32[16,2304]{1,0:T(8,128)S(1)}, u32[]{:S(2)}, u32[]{:S(2)}) collective-permute-start(f32[16,2304]{1,0:T(8,128)S(1)} %pad_maximum_fusion.6), channel_id=1, source_target_pairs={{0,64},{1,65},{2,66},{3,67},{4,68},{5,69},{6,70},{7,71},{16,80},{1... | collective-permute-start | bytes 442376 | tf_op jit(solution)/shard_map/ppermute | solution.py:216
  162.9 1.3 collective-permute-start.5
  164.2 3.5 %collective-permute-done.4 = f32[16,2304]{1,0:T(8,128)S(1)} collective-permute-done((f32[16,2304]{1,0:T(8,128)S(1)}, f32[16,2304]{1,0:T(8,128)S(1)}, u32[]{:S(2)}, u32[]{:S(2)}) %collective-permute-start.4) | collective-permute-done | bytes 147488 | tf_op jit(solution)/shard_map/ppermute | solution.py:216
  167.7 13.8 %collective-permute-done.5 = f32[16,2304]{1,0:T(8,128)S(1)} collective-permute-done((f32[16,2304]{1,0:T(8,128)S(1)}, f32[16,2304]{1,0:T(8,128)S(1)}, u32[]{:S(2)}, u32[]{:S(2)}) %collective-permute-start.5) | collective-permute-done | bytes 147488 | tf_op jit(solution)/shard_map/ppermute | solution.py:216
  181.5 1.0 fusion.3
  182.5 0.2 reshape.160
  182.7 2.7 %collective-permute-start.6 = (f32[32,768]{1,0:T(8,128)S(1)}, f32[32,768]{1,0:T(8,128)S(1)}, u32[]{:S(2)}, u32[]{:S(2)}) collective-permute-start(f32[32,768]{1,0:T(8,128)S(1)} %bitcast.59), channel_id=1, source_target_pairs={{0,16},{1,17},{2,18},{3,19},{4,20},{5,21},{6,22},{7,23},{8,24},{9,... | collective-permute-start | bytes 294920 | tf_op jit(solution)/shard_map/ppermute | solution.py:216
  185.4 3.8 %collective-permute-done.6 = f32[32,768]{1,0:T(8,128)S(1)} collective-permute-done((f32[32,768]{1,0:T(8,128)S(1)}, f32[32,768]{1,0:T(8,128)S(1)}, u32[]{:S(2)}, u32[]{:S(2)}) %collective-permute-start.6) | collective-permute-done | bytes 98336 | tf_op jit(solution)/shard_map/ppermute | solution.py:216
  189.2 0.1 reshape.162
  189.3 0.1 slice_add_fusion
  189.3 0.1 slice_bitcast_fusion.1
  189.5 0.1 copy_multiply_fusion
  189.6 0.2 fusion.12
  189.8 0.1 maximum_bitcast_fusion
  189.9 0.7 copy.27
  (20 shorter events, 0.2 us)
Async XLA Ops:
  6.5 32.6 %copy-start.4 = (s32[1,1,4,2]{2,3,1,0:T(2,128)S(1)}, s32[1,1,4,2]{2,3,1,0:T(2,128)}, u32[]{:S(2)}) copy-start(s32[1,1,4,2]{2,3,1,0:T(2,128)} %param.12) | copy-start | bytes 100
  6.5 73.5 %all-gather.2.cloned.1.call-start = ((), (), s32[]{:S(2)}) async-start(), calls=%async_computation.1 | async-start | bytes 5013504 | tf_op jit(solution)/shard_map/all_gather | solution.py:236
  7.3 72.7 %copy-start = (f32[2,256,256]{2,1,0:T(8,128)S(1)}, f32[2,256,256]{2,1,0:T(8,128)}, u32[]{:S(2)}) copy-start(f32[2,256,256]{2,1,0:T(8,128)} %probe.3) | copy-start | bytes 1572868
  7.4 72.7 %copy-start.2 = (bf16[1,1,4,256,256]{4,3,2,1,0:T(8,128)(2,1)S(1)}, bf16[1,1,4,256,256]{4,3,2,1,0:T(8,128)(2,1)}, u32[]{:S(2)}) copy-start(bf16[1,1,4,256,256]{4,3,2,1,0:T(8,128)(2,1)} %param.11) | copy-start | bytes 1572868
  7.4 6.6 %collective-permute-start = (f32[32,512]{1,0:T(8,128)S(1)}, f32[32,512]{1,0:T(8,128)S(1)}, u32[]{:S(2)}, u32[]{:S(2)}) collective-permute-start(f32[32,512]{1,0:T(8,128)S(1)} %pad_maximum_fusion.7), channel_id=1, source_target_pairs={{16,0},{17,1},{18,2},{19,3},{20,4},{21,5},{22,6},{23,7},{24,8},{25... | collective-permute-start | bytes 196616 | tf_op jit(solution)/shard_map/ppermute | solution.py:216
  14.1 16.7 %collective-permute-start.2 = (f32[16,1536]{1,0:T(8,128)S(1)}, f32[16,1536]{1,0:T(8,128)S(1)}, u32[]{:S(2)}, u32[]{:S(2)}) collective-permute-start(f32[16,1536]{1,0:T(8,128)S(1)} %get-tuple-element.39), channel_id=1, source_target_pairs={{64,8},{65,9},{66,10},{67,11},{68,12},{69,13},{70,14},{71,15},{80,... | collective-permute-start | bytes 294920 | tf_op jit(solution)/shard_map/ppermute | solution.py:216
  27.2 11.1 %collective-permute-start.1 = (f32[16,1536]{1,0:T(8,128)S(1)}, f32[16,1536]{1,0:T(8,128)S(1)}, u32[]{:S(2)}, u32[]{:S(2)}) collective-permute-start(f32[16,1536]{1,0:T(8,128)S(1)} %get-tuple-element.40), channel_id=1, source_target_pairs={{64,0},{65,1},{66,2},{67,3},{68,4},{69,5},{70,6},{71,7},{80,16},{8... | collective-permute-start | bytes 294920 | tf_op jit(solution)/shard_map/ppermute | solution.py:216
  39.1 115.8 %reduce-scatter.2.cloned.1.call-start = ((), (), s32[]{:S(2)}) async-start(), calls=%async_computation.2 | async-start | bytes 2654208 | tf_op jit(solution)/shard_map/reduce_scatter | solution.py:244
  80.0 2.3 %copy-start.1 = (f32[768,1536]{1,0:T(8,128)S(1)}, f32[768,1536]{1,0:T(8,128)}, u32[]{:S(2)}) copy-start(f32[768,1536]{1,0:T(8,128)} %all-gather.2.cloned.1.call-done) | copy-start | bytes 14155780
  97.5 6.4 %collective-permute-start.3 = (f32[8,48,1536]{2,1,0:T(8,128)S(1)}, f32[8,48,1536]{2,1,0:T(8,128)S(1)}, u32[]{:S(2)}, u32[]{:S(2)}) collective-permute-start(f32[8,48,1536]{2,1,0:T(8,128)S(1)} %get-tuple-element.32), channel_id=1, source_target_pairs={{0,1},{1,0},{2,3},{3,2},{4,5},{5,4},{6,7},{7,6},{8,9},{9,8},{10,11... | collective-permute-start | bytes 7077896 | tf_op jit(solution)/shard_map/ppermute | solution.py:242
  105.8 83.7 %copy-start.3 = (f32[1,2,32,512]{3,2,1,0:T(8,128)S(1)}, f32[1,2,32,512]{3,2,1,0:T(8,128)}, u32[]{:S(2)}) copy-start(f32[1,2,32,512]{3,2,1,0:T(8,128)} %param.9) | copy-start | bytes 393220
  155.8 11.9 %collective-permute-start.4 = (f32[16,2304]{1,0:T(8,128)S(1)}, f32[16,2304]{1,0:T(8,128)S(1)}, u32[]{:S(2)}, u32[]{:S(2)}) collective-permute-start(f32[16,2304]{1,0:T(8,128)S(1)} %pad_maximum_fusion.6), channel_id=1, source_target_pairs={{0,64},{1,65},{2,66},{3,67},{4,68},{5,69},{6,70},{7,71},{16,80},{1... | collective-permute-start | bytes 442376 | tf_op jit(solution)/shard_map/ppermute | solution.py:216
  162.9 18.6 %collective-permute-start.5 = (f32[16,2304]{1,0:T(8,128)S(1)}, f32[16,2304]{1,0:T(8,128)S(1)}, u32[]{:S(2)}, u32[]{:S(2)}) collective-permute-start(f32[16,2304]{1,0:T(8,128)S(1)} %pad_maximum_fusion.6), channel_id=1, source_target_pairs={{8,64},{9,65},{10,66},{11,67},{12,68},{13,69},{14,70},{15,71},{24,... | collective-permute-start | bytes 442376 | tf_op jit(solution)/shard_map/ppermute | solution.py:216
  182.7 6.5 %collective-permute-start.6 = (f32[32,768]{1,0:T(8,128)S(1)}, f32[32,768]{1,0:T(8,128)S(1)}, u32[]{:S(2)}, u32[]{:S(2)}) collective-permute-start(f32[32,768]{1,0:T(8,128)S(1)} %bitcast.59), channel_id=1, source_target_pairs={{0,16},{1,17},{2,18},{3,19},{4,20},{5,21},{6,22},{7,23},{8,24},{9,... | collective-permute-start | bytes 294920 | tf_op jit(solution)/shard_map/ppermute | solution.py:216
Sparse Core Ops, SparseCore 0:
  39.2 40.7 all-gather.1
  105.9 48.9 reduce-scatter.1

commit v2 on v1

--- a/solution.py
+++ b/solution.py
@@ -34,21 +34,29 @@
     return (left_table.astype(jnp.bfloat16), right_table.astype(jnp.bfloat16))
 
 
+def low_home(worker):
+    upper_half = worker // 8
+    y = worker // 2
+    return 2 * (y + upper_half * (7 - 2 * y)) + worker % 2
+
+
 def low_row(worker):
-    return TILE + worker % 8 * (2 * LOW) + worker // 8 * LOW
+    return TILE + low_home(worker) * (2 * LOW) + worker // 8 * LOW
 
 
 def slots_kernel(
-    corners, live, parity, cells_hbm, probe, pattern, left, right,
-    keep_hbm, send_hbm, cells, sums, wave, half, sem,
+    corners, live, parity, own_hbm, low_mine, low_other, probe, pattern, left, right,
+    keep_own, send_own, keep_low, send_low, cells, sums, wave, half, sem,
 ):
-    fetches = []
-    for worker in range(WORKERS):
-        low = low_row(worker)
-        fetches.append(pltpu.make_async_copy(
-            cells_hbm.at[worker, 0:OWN], cells.at[OWN * worker:OWN * (worker + 1)], sem.at[2 * worker]))
-        fetches.append(pltpu.make_async_copy(
-            cells_hbm.at[worker, OWN:ROWS], cells.at[low:low + LOW], sem.at[2 * worker + 1]))
+    core = parity[0]
+    fetches = [pltpu.make_async_copy(own_hbm, cells.at[0:TILE], sem.at[0])]
+    low_rows = []
+    for y in range(WORKERS // 2):
+        mine = pl.multiple_of(low_row(2 * y + core), LOW)
+        other = pl.multiple_of(low_row(2 * y + 1 - core), LOW)
+        low_rows.append((mine, other))
+        fetches.append(pltpu.make_async_copy(low_mine.at[y], cells.at[pl.ds(mine, LOW)], sem.at[1 + 2 * y]))
+        fetches.append(pltpu.make_async_copy(low_other.at[y], cells.at[pl.ds(other, LOW)], sem.at[2 + 2 * y]))
     for copy in fetches:
         copy.start()
 
@@ -105,27 +113,19 @@
 
     lax.fori_loop(0, live[0, 0], one, 0)
 
-    def store(own_core):
-        copies = []
-        for worker in range(WORKERS):
-            low = low_row(worker)
-            target = keep_hbm if worker % 2 == own_core else send_hbm
-            copies.append(pltpu.make_async_copy(
-                sums.at[OWN * worker:OWN * (worker + 1)], target.at[worker // 2, 0:OWN], sem.at[2 * worker]))
-            copies.append(pltpu.make_async_copy(
-                sums.at[low:low + LOW], target.at[worker // 2, OWN:ROWS], sem.at[2 * worker + 1]))
-        for copy in copies:
-            copy.start()
-        for copy in copies:
-            copy.wait()
-
-    @pl.when(parity[0] == 0)
-    def _():
-        store(0)
-
-    @pl.when(parity[0] != 0)
-    def _():
-        store(1)
+    copies = []
+    for y in range(WORKERS // 2):
+        mine, other = low_rows[y]
+        own_mine = pl.multiple_of((2 * y + core) * OWN, OWN)
+        own_other = pl.multiple_of((2 * y + 1 - core) * OWN, OWN)
+        copies.append(pltpu.make_async_copy(sums.at[pl.ds(other, LOW)], send_low.at[y], sem.at[4 * y]))
+        copies.append(pltpu.make_async_copy(sums.at[pl.ds(mine, LOW)], keep_low.at[y], sem.at[4 * y + 1]))
+        copies.append(pltpu.make_async_copy(sums.at[pl.ds(own_other, OWN)], send_own.at[y], sem.at[4 * y + 2]))
+        copies.append(pltpu.make_async_copy(sums.at[pl.ds(own_mine, OWN)], keep_own.at[y], sem.at[4 * y + 3]))
+    for copy in copies:
+        copy.start()
+    for copy in copies:
+        copy.wait()
 
 
 def weight_kernel(corners, live, me, probe, weights, padded):
@@ -173,13 +173,15 @@
     return pl.BlockSpec(memory_space=pl.ANY)
 
 
-def patch_sums(corners, live, parity, cells, probe, patterns, left, right):
-    chunk = jax.ShapeDtypeStruct((WORKERS // 2, ROWS, 2 * WIDE), jnp.float32)
+def patch_sums(corners, live, parity, own_cells, low_mine, low_other, probe, patterns, left, right):
+    own_chunk = jax.ShapeDtypeStruct((WORKERS // 2, OWN, 2 * WIDE), jnp.float32)
+    low_chunk = jax.ShapeDtypeStruct((WORKERS // 2, LOW, 2 * WIDE), jnp.float32)
     return pl.pallas_call(
         slots_kernel,
-        out_shape=(chunk, chunk),
-        in_specs=[smem(), smem(), smem(), hbm(), vmem(), vmem(), vmem(), vmem()],
-        out_specs=(hbm(), hbm()),
+        out_shape=(own_chunk, own_chunk, low_chunk, low_chunk),
+        in_specs=[smem(), smem(), smem(), pl.BlockSpec(memory_space=pltpu.HBM), hbm(), hbm(),
+                  vmem(), vmem(), vmem(), vmem()],
+        out_specs=(hbm(), hbm(), hbm(), hbm()),
         scratch_shapes=[
             pltpu.VMEM((WIDE, 2 * WIDE), jnp.float32),
             pltpu.VMEM((WIDE, 2 * WIDE), jnp.float32),
@@ -190,7 +192,7 @@
         compiler_params=pltpu.CompilerParams(vmem_limit_bytes=40 * 2**20),
         cost_estimate=pl.CostEstimate(flops=2 * 10**9, bytes_accessed=12 * 10**6, transcendentals=0),
         name="patch_sums",
-    )(corners, live, parity, cells, probe, patterns, left, right)
+    )(corners, live, parity, own_cells, low_mine, low_other, probe, patterns, left, right)
 
 
 def weight_rows(corners, live, me, probe):
@@ -226,33 +228,42 @@
     spare_re = jnp.zeros((OWN, 8), jnp.float32)
     spare_re = spare_re.at[0].set(corners.reshape(8).astype(jnp.float32))
     spare_re = spare_re.at[1].set(jnp.broadcast_to(live_count[0, 0].astype(jnp.float32), (8,)))
-    upper = jnp.concatenate(
-        [own[0], from_right[:, :SIDE], own[1], from_right[:, SIDE:]], 1)
-    low_a = moved(upper[:LOW], -GRID_C, lambda tile, worker: worker if worker < 8 else None)
-    low_b = moved(upper[LOW:], -GRID_C, lambda tile, worker: worker + 8 if worker < 8 else None)
-    marked = jnp.concatenate(
+    shard = jnp.concatenate(
         [own[0], from_right[:, :SIDE - 8], spare_re, own[1], from_right[:, SIDE:]], 1)
-    shard = jnp.concatenate([marked, low_a + low_b], 0)
-    cells = lax.all_gather(shard, "pat", axis=0, tiled=True).reshape(WORKERS, ROWS, 2 * WIDE)
+    own_cells = lax.all_gather(shard, "pat", axis=0, tiled=True)
+    mirrored = lambda worker: 2 * (7 - worker // 2) + worker % 2
+    low_a = moved(shard[:LOW], -GRID_C, lambda tile, worker: worker if worker < 8 else None)
+    low_b = moved(shard[LOW:], -GRID_C, lambda tile, worker: mirrored(worker) if worker < 8 else None)
+    same_core = [list(range(0, WORKERS, 2)), list(range(1, WORKERS, 2))]
+    sibling = [(i, i ^ 1) for i in range(WORKERS)]
+    low_mine = lax.all_to_all(
+        jnp.broadcast_to(low_a + low_b, (WORKERS // 2, LOW, 2 * WIDE)), "pat", 0, 0, axis_index_groups=same_core)
+    low_other = lax.ppermute(low_mine, "pat", sibling)
 
     left_table, right_table = dft_blocks(SIDE)
-    keep, send = patch_sums(
-        corners, live_count, (me % 2).reshape(1), cells, probe_wave, amplitudes[0, 0],
+    keep_own, send_own, keep_low, send_low = patch_sums(
+        corners, live_count, (me % 2).reshape(1), own_cells, low_mine, low_other, probe_wave, amplitudes[0, 0],
         left_table, right_table)
-    other = lax.ppermute(send, "pat", [(i, i ^ 1) for i in range(WORKERS)])
-    both = (keep + other).reshape(WORKERS // 2 * ROWS, 2 * WIDE)
-    summed = lax.psum_scatter(
-        both, "pat", scatter_dimension=0, tiled=True,
-        axis_index_groups=[list(range(0, WORKERS, 2)), list(range(1, WORKERS, 2))])
-
-    tile_corners = cells[:, 0, WIDE - 8:WIDE].astype(jnp.int32)
-    tile_live = cells[:, 1, WIDE - 8].astype(jnp.int32)
+    other_low = lax.ppermute(send_low, "pat", sibling)
+    other_own = lax.ppermute(send_own, "pat", sibling)
+    both_own = (keep_own + other_own).reshape(WORKERS // 2 * OWN, 2 * WIDE)
+    both_low = keep_low + other_low
+    both_own, both_low = lax.optimization_barrier((both_own, both_low))
+    summed_own = lax.psum_scatter(
+        both_own, "pat", scatter_dimension=0, tiled=True, axis_index_groups=same_core)
+
+    by_tile = own_cells.reshape(WORKERS, OWN, 2 * WIDE)
+    tile_corners = by_tile[:, 0, WIDE - 8:WIDE].astype(jnp.int32)
+    tile_live = by_tile[:, 1, WIDE - 8].astype(jnp.int32)
     weights = weight_rows(tile_corners, tile_live, me.reshape(1), probe_wave)
 
-    full = jnp.concatenate([summed, weights], 1)
-    down_a = moved(full[OWN:], GRID_C, lambda tile, worker: worker if worker < 8 else None)
-    down_b = moved(full[OWN:], GRID_C, lambda tile, worker: worker - 8 if worker >= 8 else None)
-    upper_sum = (full[:OWN] + jnp.concatenate([down_a, down_b], 0)).reshape(OWN, 3, WIDE)
+    summed_low = jnp.sum(lax.all_to_all(both_low, "pat", 0, 0, axis_index_groups=same_core), 0)
+    low = jnp.concatenate([summed_low, weights[OWN:]], 1)
+    down_a = moved(low, GRID_C, lambda tile, worker: worker if worker < 8 else None)
+    down_b = moved(low, GRID_C, lambda tile, worker: mirrored(worker) if worker >= 8 else None)
+    upper_sum = (
+        jnp.concatenate([summed_own, weights[:OWN]], 1) + jnp.concatenate([down_a, down_b], 0)
+    ).reshape(OWN, 3, WIDE)
     to_right = upper_sum[:, :, TILE:].reshape(OWN, 3 * SIDE)
     from_left = moved(to_right, 1, lambda tile, worker: worker if tile % GRID_C != GRID_C - 1 else None)
     total = upper_sum[:, :, :TILE] + jnp.pad(

time: 198 us -> 173 us (0.87)
  the two profiles are of different devices: /device:TPU:84 before, /device:TPU:68 now
where the time goes in v2:
time: 173 us; the launch traced here: 172 us
  waiting for transfers between devices  49.1 us (28%)
  blocking collectives  35.4 us (20%)
  starting transfers between devices  32.2 us (19%)
  Pallas kernels  25.5 us (15%)
  between operations  14.3 us (8%)
  local copies, waits for them, and re-layouts  8.82 us (5%)
  other arithmetic  7 us (4%)
    all_to_all x1, blocking collectives, local(): lax.all_to_all(jnp.broadcast_to(low_a + low_b, (WORKERS // 2, LOW, 2 * WI...  35.4 us
    ppermute x6, waiting for transfers between devices, moved(): return lax.ppermute(value, ('obj', 'pat'), pairs)  27.4 us
    ppermute x6, starting transfers between devices, moved(): return lax.ppermute(value, ('obj', 'pat'), pairs)  22.4 us
    all_to_all x1, waiting for transfers between devices, local(): lax.all_to_all(both_low, 'pat', 0, 0, axis_index_groups=same_core)  18.1 us
    pallas_call x1, Pallas kernels, patch_sums(): pl.pallas_call(slots_kernel, out_shape=(own_chunk, own_chunk, low_chunk,...  17.7 us
    pallas_call x1, Pallas kernels, weight_rows(): pl.pallas_call(weight_kernel, out_shape=jax.ShapeDtypeStruct((ROWS, WIDE)...  7.78 us
    all_to_all x1, starting transfers between devices, local(): lax.all_to_all(both_low, 'pat', 0, 0, axis_index_groups=same_core)  3.56 us
  transfers between devices with their start and end apart: 12, of which 9 were waited for; matrix products, arithmetic and copies ran while one was open for 5% of the time, Pallas kernels for 5%

profile of v2, /device:TPU:68, one launch (start us, length us, event | category | flops | bytes accessed | tf_op | source)
XLA Modules:
  0.0 172.3 jit_solution(13546814609357556402)
XLA Ops:
  6.5 0.8 slice_bitcast_fusion.7
  7.3 1.9 %collective-permute-start = (f32[32,512]{1,0:T(8,128)S(1)}, f32[32,512]{1,0:T(8,128)S(1)}, u32[]{:S(2)}, u32[]{:S(2)}) collective-permute-start(f32[32,512]{1,0:T(8,128)S(1)} %pad_maximum_fusion.6), channel_id=1, source_target_pairs={{16,0},{17,1},{18,2},{19,3},{20,4},{21,5},{22,6},{23,7},{24,8},{25... | collective-permute-start | bytes 196616 | tf_op jit(solution)/shard_map/ppermute | solution.py:218
  9.3 0.9 slice_bitcast_fusion.4
  10.8 0.7 convert_element_type.48
  11.5 0.1 copy.11
  11.6 0.1 convert_element_type.49
  11.7 2.1 %collective-permute-done = f32[32,512]{1,0:T(8,128)S(1)} collective-permute-done((f32[32,512]{1,0:T(8,128)S(1)}, f32[32,512]{1,0:T(8,128)S(1)}, u32[]{:S(2)}, u32[]{:S(2)}) %collective-permute-start) | collective-permute-done | bytes 65568 | tf_op jit(solution)/shard_map/ppermute | solution.py:218
  13.9 0.7 concatenate.51
  14.6 0.0 reduce-scatter.2.cloned.1.call-start
  14.7 1.0 fusion.13
  15.6 9.6 %collective-permute-start.1 = (f32[16,1536]{1,0:T(8,128)S(1)}, f32[16,1536]{1,0:T(8,128)S(1)}, u32[]{:S(2)}, u32[]{:S(2)}) collective-permute-start(f32[16,1536]{1,0:T(8,128)S(1)} %get-tuple-element.46), channel_id=1, source_target_pairs={{64,0},{65,1},{66,2},{67,3},{68,4},{69,5},{70,6},{71,7},{80,16},{8... | collective-permute-start | bytes 294920 | tf_op jit(solution)/shard_map/ppermute | solution.py:218
  25.3 3.6 %collective-permute-start.2 = (f32[16,1536]{1,0:T(8,128)S(1)}, f32[16,1536]{1,0:T(8,128)S(1)}, u32[]{:S(2)}, u32[]{:S(2)}) collective-permute-start(f32[16,1536]{1,0:T(8,128)S(1)} %get-tuple-element.45), channel_id=1, source_target_pairs={{64,14},{65,15},{66,12},{67,13},{68,10},{69,11},{70,8},{71,9},{80,... | collective-permute-start | bytes 294920 | tf_op jit(solution)/shard_map/ppermute | solution.py:218
  28.9 0.7 collective-permute-done.1
  29.6 1.9 %collective-permute-done.2 = f32[16,1536]{1,0:T(8,128)S(1)} collective-permute-done((f32[16,1536]{1,0:T(8,128)S(1)}, f32[16,1536]{1,0:T(8,128)S(1)}, u32[]{:S(2)}, u32[]{:S(2)}) %collective-permute-start.2) | collective-permute-done | bytes 98336 | tf_op jit(solution)/shard_map/ppermute | solution.py:218
  31.5 0.1 broadcast_in_dim.4
  31.6 35.4 %all_to_all.10.low_mine = f32[8,16,1536]{2,1,0:T(8,128)S(1)} all-to-all(f32[8,16,1536]{2,1,0:T(8,128)S(1)} %broadcast_in_dim.4), channel_id=1, replica_groups={{0,2,4,6,8,10,12,14},{1,3,5,7,9,11,13,15},{16,18,20,22,24,26,28,30},{17..., dimensions={0} | all-to-all | bytes 1572864 | tf_op jit(solution)/shard_map/all_to_all | solution.py:239
  66.9 1.9 %collective-permute-start.3 = (f32[8,16,1536]{2,1,0:T(8,128)S(1)}, f32[8,16,1536]{2,1,0:T(8,128)S(1)}, u32[]{:S(2)}, u32[]{:S(2)}) collective-permute-start(f32[8,16,1536]{2,1,0:T(8,128)S(1)} %all_to_all.10.low_mine), channel_id=1, source_target_pairs={{0,1},{1,0},{2,3},{3,2},{4,5},{5,4},{6,7},{7,6},{8,9},{9,8},{10,11... | collective-permute-start | bytes 2359304 | tf_op jit(solution)/shard_map/ppermute | solution.py:241
  68.9 0.1 copy.12.corners
  68.9 1.0 fusion.8
  69.9 1.1 negate_convert_fusion
  71.1 0.1 fusion.1
  71.2 1.5 all-gather.2.cloned.1.call-done.own_hbm
  72.7 1.9 %copy-done.1 = f32[512,1536]{1,0:T(8,128)S(1)} copy-done((f32[512,1536]{1,0:T(8,128)S(1)}, f32[512,1536]{1,0:T(8,128)}, u32[]{:S(2)}) %copy-start.1) | copy-done | bytes 3145752
  74.6 1.0 copy-done.2
  75.6 17.7 %patch_sums.1 = (f32[8,32,1536]{2,1,0:T(8,128)S(1)}, f32[8,32,1536]{2,1,0:T(8,128)S(1)}, f32[8,16,1536]{2,1,0:T(8,128)S(1)}, f32[8,16,1536]{2,1,0:T(8,128)S(1)}) custom-call(s32[4,2]{1,0:T(4,128)S(1)} %copy.12.corners, s32[1,1]{1,0:T(1,128)S(6)} %copy.36.live, s32[1]{0:T(128)} %bitcast.1.parity, f32[512,1536]{1,0:T(8,128)S(1)} %copy-done.1, ...), custom_call_target="tpu_custom_call" | custom-call | flops 2000000000 | bytes 12000000 | tf_op jit(solution)/shard_map/patch_sums/pallas_call | solution.py:179
  93.3 1.9 %collective-permute-start.4 = (f32[8,32,1536]{2,1,0:T(8,128)S(1)}, f32[8,32,1536]{2,1,0:T(8,128)S(1)}, u32[]{:S(2)}, u32[]{:S(2)}) collective-permute-start(f32[8,32,1536]{2,1,0:T(8,128)S(1)} %get-tuple-element.36), channel_id=1, source_target_pairs={{0,1},{1,0},{2,3},{3,2},{4,5},{5,4},{6,7},{7,6},{8,9},{9,8},{10,11... | collective-permute-start | bytes 4718600 | tf_op jit(solution)/shard_map/ppermute | solution.py:248
  95.2 2.4 %collective-permute-start.5 = (f32[8,16,1536]{2,1,0:T(8,128)S(1)}, f32[8,16,1536]{2,1,0:T(8,128)S(1)}, u32[]{:S(2)}, u32[]{:S(2)}) collective-permute-start(f32[8,16,1536]{2,1,0:T(8,128)S(1)} %get-tuple-element.38), channel_id=1, source_target_pairs={{0,1},{1,0},{2,3},{3,2},{4,5},{5,4},{6,7},{7,6},{8,9},{9,8},{10,11... | collective-permute-start | bytes 2359304 | tf_op jit(solution)/shard_map/ppermute | solution.py:247
  97.6 2.1 %collective-permute-done.5 = f32[8,16,1536]{2,1,0:T(8,128)S(1)} collective-permute-done((f32[8,16,1536]{2,1,0:T(8,128)S(1)}, f32[8,16,1536]{2,1,0:T(8,128)S(1)}, u32[]{:S(2)}, u32[]{:S(2)}) %collective-permute-start.5) | collective-permute-done | bytes 786464 | tf_op jit(solution)/shard_map/ppermute | solution.py:247
  99.7 1.0 add.68
  100.7 1.4 add.67
  102.1 3.6 %all-to-all-start.1 = ((f32[8,16,1536]{2,1,0:T(8,128)}), f32[8,16,1536]{2,1,0:T(8,128)S(1)}, u32[]{:S(2)}, u32[]{:S(2)}) async-start(f32[8,16,1536]{2,1,0:T(8,128)} %add.68), calls=%async_computation.2 | async-start | bytes 1572864 | tf_op jit(solution)/shard_map/all_to_all | solution.py:260
  105.6 0.9 slice.107
  106.6 0.9 slice.108
  107.5 0.1 copy.21
  107.6 0.1 copy.15.corners
  107.6 0.1 copy.22
  107.7 7.8 %weight_rows.1 = f32[48,768]{1,0:T(8,128)S(1)} custom-call(s32[16,8]{1,0:T(8,128)S(1)} %copy.15.corners, s32[16]{0:T(128)S(1)} %convert_bitcast_fusion.1.live, s32[1]{0:T(128)} %bitcast.13.me, f32[2,256,256]{2,1,0:T(8,128)S(1)} %copy-done), custom_call_target="tpu_custom_call" | custom-call | flops 10000000 | bytes 1000000 | tf_op jit(solution)/shard_map/weight_rows/pallas_call | solution.py:199
  115.5 18.1 %all-to-all-done.1 = f32[8,16,1536]{2,1,0:T(8,128)S(1)} async-done(((f32[8,16,1536]{2,1,0:T(8,128)}), f32[8,16,1536]{2,1,0:T(8,128)S(1)}, u32[]{:S(2)}, u32[]{:S(2)}) %all-to-all-start.1) | async-done | bytes 786464 | tf_op jit(solution)/shard_map/all_to_all | solution.py:260
  133.7 1.3 collective-permute-start.7
  135.0 3.8 %collective-permute-start.6 = (f32[16,2304]{1,0:T(8,128)S(1)}, f32[16,2304]{1,0:T(8,128)S(1)}, u32[]{:S(2)}, u32[]{:S(2)}) collective-permute-start(f32[16,2304]{1,0:T(8,128)S(1)} %pad_maximum_fusion.5), channel_id=1, source_target_pairs={{0,64},{1,65},{2,66},{3,67},{4,68},{5,69},{6,70},{7,71},{16,80},{1... | collective-permute-start | bytes 442376 | tf_op jit(solution)/shard_map/ppermute | solution.py:218
  138.8 15.0 %collective-permute-done.7 = f32[16,2304]{1,0:T(8,128)S(1)} collective-permute-done((f32[16,2304]{1,0:T(8,128)S(1)}, f32[16,2304]{1,0:T(8,128)S(1)}, u32[]{:S(2)}, u32[]{:S(2)}) %collective-permute-start.7) | collective-permute-done | bytes 147488 | tf_op jit(solution)/shard_map/ppermute | solution.py:218
  153.8 3.3 %collective-permute-done.6 = f32[16,2304]{1,0:T(8,128)S(1)} collective-permute-done((f32[16,2304]{1,0:T(8,128)S(1)}, f32[16,2304]{1,0:T(8,128)S(1)}, u32[]{:S(2)}, u32[]{:S(2)}) %collective-permute-start.6) | collective-permute-done | bytes 147488 | tf_op jit(solution)/shard_map/ppermute | solution.py:218
  157.1 0.0 reduce-scatter.2.cloned.1.call-done
  157.2 0.9 pad_maximum_fusion.4
  158.1 0.1 bitcast_add_fusion
  158.2 2.2 %collective-permute-start.8 = (f32[32,768]{1,0:T(8,128)S(1)}, f32[32,768]{1,0:T(8,128)S(1)}, u32[]{:S(2)}, u32[]{:S(2)}) collective-permute-start(f32[32,768]{1,0:T(8,128)S(1)} %bitcast.77), channel_id=1, source_target_pairs={{0,16},{1,17},{2,18},{3,19},{4,20},{5,21},{6,22},{7,23},{8,24},{9,... | collective-permute-start | bytes 294920 | tf_op jit(solution)/shard_map/ppermute | solution.py:218
  160.4 4.3 %collective-permute-done.8 = f32[32,768]{1,0:T(8,128)S(1)} collective-permute-done((f32[32,768]{1,0:T(8,128)S(1)}, f32[32,768]{1,0:T(8,128)S(1)}, u32[]{:S(2)}, u32[]{:S(2)}) %collective-permute-start.8) | collective-permute-done | bytes 98336 | tf_op jit(solution)/shard_map/ppermute | solution.py:218
  164.8 0.7 maximum_bitcast_fusion
  (33 shorter events, 0.3 us)
Async XLA Ops:
  6.5 66.1 %all-gather.2.cloned.1.call-start = ((), (), s32[]{:S(2)}) async-start(), calls=%async_computation.3 | async-start | bytes 3342336 | tf_op jit(solution)/shard_map/all_gather | solution.py:233
  7.3 6.5 %collective-permute-start = (f32[32,512]{1,0:T(8,128)S(1)}, f32[32,512]{1,0:T(8,128)S(1)}, u32[]{:S(2)}, u32[]{:S(2)}) collective-permute-start(f32[32,512]{1,0:T(8,128)S(1)} %pad_maximum_fusion.6), channel_id=1, source_target_pairs={{16,0},{17,1},{18,2},{19,3},{20,4},{21,5},{22,6},{23,7},{24,8},{25... | collective-permute-start | bytes 196616 | tf_op jit(solution)/shard_map/ppermute | solution.py:218
  14.6 54.2 %copy-start.4 = (s32[1,1,4,2]{2,3,1,0:T(2,128)S(1)}, s32[1,1,4,2]{2,3,1,0:T(2,128)}, u32[]{:S(2)}) copy-start(s32[1,1,4,2]{2,3,1,0:T(2,128)} %param.12) | copy-start | bytes 100
  14.6 142.5 %reduce-scatter.2.cloned.1.call-start = ((), (), s32[]{:S(2)}) async-start(), calls=%async_computation.4 | async-start | bytes 1769472 | tf_op jit(solution)/shard_map/reduce_scatter | solution.py:252
  15.6 13.9 %collective-permute-start.1 = (f32[16,1536]{1,0:T(8,128)S(1)}, f32[16,1536]{1,0:T(8,128)S(1)}, u32[]{:S(2)}, u32[]{:S(2)}) collective-permute-start(f32[16,1536]{1,0:T(8,128)S(1)} %get-tuple-element.46), channel_id=1, source_target_pairs={{64,0},{65,1},{66,2},{67,3},{68,4},{69,5},{70,6},{71,7},{80,16},{8... | collective-permute-start | bytes 294920 | tf_op jit(solution)/shard_map/ppermute | solution.py:218
  25.3 6.2 %collective-permute-start.2 = (f32[16,1536]{1,0:T(8,128)S(1)}, f32[16,1536]{1,0:T(8,128)S(1)}, u32[]{:S(2)}, u32[]{:S(2)}) collective-permute-start(f32[16,1536]{1,0:T(8,128)S(1)} %get-tuple-element.45), channel_id=1, source_target_pairs={{64,14},{65,15},{66,12},{67,13},{68,10},{69,11},{70,8},{71,9},{80,... | collective-permute-start | bytes 294920 | tf_op jit(solution)/shard_map/ppermute | solution.py:218
  31.5 41.1 %copy-start = (f32[2,256,256]{2,1,0:T(8,128)S(1)}, f32[2,256,256]{2,1,0:T(8,128)}, u32[]{:S(2)}) copy-start(f32[2,256,256]{2,1,0:T(8,128)} %probe.3) | copy-start | bytes 1572868
  66.9 4.2 %collective-permute-start.3 = (f32[8,16,1536]{2,1,0:T(8,128)S(1)}, f32[8,16,1536]{2,1,0:T(8,128)S(1)}, u32[]{:S(2)}, u32[]{:S(2)}) collective-permute-start(f32[8,16,1536]{2,1,0:T(8,128)S(1)} %all_to_all.10.low_mine), channel_id=1, source_target_pairs={{0,1},{1,0},{2,3},{3,2},{4,5},{5,4},{6,7},{7,6},{8,9},{9,8},{10,11... | collective-permute-start | bytes 2359304 | tf_op jit(solution)/shard_map/ppermute | solution.py:241
  72.7 1.9 %copy-start.1 = (f32[512,1536]{1,0:T(8,128)S(1)}, f32[512,1536]{1,0:T(8,128)}, u32[]{:S(2)}) copy-start(f32[512,1536]{1,0:T(8,128)} %all-gather.2.cloned.1.call-done.own_hbm) | copy-start | bytes 9437188
  74.6 1.0 copy-start.2
  93.3 7.4 %collective-permute-start.4 = (f32[8,32,1536]{2,1,0:T(8,128)S(1)}, f32[8,32,1536]{2,1,0:T(8,128)S(1)}, u32[]{:S(2)}, u32[]{:S(2)}) collective-permute-start(f32[8,32,1536]{2,1,0:T(8,128)S(1)} %get-tuple-element.36), channel_id=1, source_target_pairs={{0,1},{1,0},{2,3},{3,2},{4,5},{5,4},{6,7},{7,6},{8,9},{9,8},{10,11... | collective-permute-start | bytes 4718600 | tf_op jit(solution)/shard_map/ppermute | solution.py:248
  95.2 4.5 %collective-permute-start.5 = (f32[8,16,1536]{2,1,0:T(8,128)S(1)}, f32[8,16,1536]{2,1,0:T(8,128)S(1)}, u32[]{:S(2)}, u32[]{:S(2)}) collective-permute-start(f32[8,16,1536]{2,1,0:T(8,128)S(1)} %get-tuple-element.38), channel_id=1, source_target_pairs={{0,1},{1,0},{2,3},{3,2},{4,5},{5,4},{6,7},{7,6},{8,9},{9,8},{10,11... | collective-permute-start | bytes 2359304 | tf_op jit(solution)/shard_map/ppermute | solution.py:247
  102.1 31.5 %all-to-all-start.1 = ((f32[8,16,1536]{2,1,0:T(8,128)}), f32[8,16,1536]{2,1,0:T(8,128)S(1)}, u32[]{:S(2)}, u32[]{:S(2)}) async-start(f32[8,16,1536]{2,1,0:T(8,128)} %add.68), calls=%async_computation.2 | async-start | bytes 1572864 | tf_op jit(solution)/shard_map/all_to_all | solution.py:260
  133.7 20.1 %collective-permute-start.7 = (f32[16,2304]{1,0:T(8,128)S(1)}, f32[16,2304]{1,0:T(8,128)S(1)}, u32[]{:S(2)}, u32[]{:S(2)}) collective-permute-start(f32[16,2304]{1,0:T(8,128)S(1)} %pad_maximum_fusion.5), channel_id=1, source_target_pairs={{8,70},{9,71},{10,68},{11,69},{12,66},{13,67},{14,64},{15,65},{24,... | collective-permute-start | bytes 442376 | tf_op jit(solution)/shard_map/ppermute | solution.py:218
  135.0 22.2 %collective-permute-start.6 = (f32[16,2304]{1,0:T(8,128)S(1)}, f32[16,2304]{1,0:T(8,128)S(1)}, u32[]{:S(2)}, u32[]{:S(2)}) collective-permute-start(f32[16,2304]{1,0:T(8,128)S(1)} %pad_maximum_fusion.5), channel_id=1, source_target_pairs={{0,64},{1,65},{2,66},{3,67},{4,68},{5,69},{6,70},{7,71},{16,80},{1... | collective-permute-start | bytes 442376 | tf_op jit(solution)/shard_map/ppermute | solution.py:218
  153.8 11.0 %copy-start.3 = (f32[1,2,32,512]{3,2,1,0:T(8,128)S(1)}, f32[1,2,32,512]{3,2,1,0:T(8,128)}, u32[]{:S(2)}) copy-start(f32[1,2,32,512]{3,2,1,0:T(8,128)} %param.9) | copy-start | bytes 393220
  158.2 6.5 %collective-permute-start.8 = (f32[32,768]{1,0:T(8,128)S(1)}, f32[32,768]{1,0:T(8,128)S(1)}, u32[]{:S(2)}, u32[]{:S(2)}) collective-permute-start(f32[32,768]{1,0:T(8,128)S(1)} %bitcast.77), channel_id=1, source_target_pairs={{0,16},{1,17},{2,18},{3,19},{4,20},{5,21},{6,22},{7,23},{8,24},{9,... | collective-permute-start | bytes 294920 | tf_op jit(solution)/shard_map/ppermute | solution.py:218
Sparse Core Ops, SparseCore 0:
  14.7 57.8 all-gather.1
  102.2 49.7 reduce-scatter.1

commit v3 on v2

--- a/solution.py
+++ b/solution.py
@@ -1,5 +1,6 @@
 import jax
 import jax.numpy as jnp
+import numpy as np
 from jax import lax
 from jax.experimental import pallas as pl
 from jax.experimental.pallas import tpu as pltpu
@@ -20,18 +21,14 @@
 
 
 def dft_blocks(side_len):
-    index_line = jnp.arange(side_len, dtype=jnp.int32)
+    index_line = np.arange(side_len)
     products = index_line[:, None] * index_line[None, :] % side_len
-    angles = 2.0 * 3.141592653589793 / side_len * products.astype(jnp.float32)
-    cos_part = jnp.cos(angles) / jnp.sqrt(jnp.float32(side_len))
-    sin_part = -jnp.sin(angles) / jnp.sqrt(jnp.float32(side_len))
-    left_table = jnp.concatenate(
-        [jnp.concatenate([cos_part, -sin_part], 1), jnp.concatenate([sin_part, cos_part], 1)], 0
-    )
-    right_table = jnp.concatenate(
-        [jnp.concatenate([cos_part, sin_part], 1), jnp.concatenate([-sin_part, cos_part], 1)], 0
-    )
-    return (left_table.astype(jnp.bfloat16), right_table.astype(jnp.bfloat16))
+    angles = (2.0 * np.pi / side_len) * products
+    cos_part = np.cos(angles) / np.sqrt(side_len)
+    sin_part = -np.sin(angles) / np.sqrt(side_len)
+    left_table = np.block([[cos_part, -sin_part], [sin_part, cos_part]])
+    right_table = np.block([[cos_part, sin_part], [-sin_part, cos_part]])
+    return tuple(jnp.asarray(table.astype(np.float32).astype(jnp.bfloat16)) for table in (left_table, right_table))
 
 
 def low_home(worker):
@@ -45,18 +42,19 @@
 
 
 def slots_kernel(
-    corners, live, parity, own_hbm, low_mine, low_other, probe, pattern, left, right,
-    keep_own, send_own, keep_low, send_low, cells, sums, wave, half, sem,
+    corners, live, me, own_hbm, low_mine, low_other, probe_hbm, pattern_hbm, left_hbm, right_hbm,
+    keep_own, send_own, keep_low, send_low,
+    cells, sums, wave, half, probe, pattern, left, right, sem,
 ):
-    core = parity[0]
-    fetches = [pltpu.make_async_copy(own_hbm, cells.at[0:TILE], sem.at[0])]
-    low_rows = []
+    core = me[0] % 2
+    pairs = [(own_hbm, cells.at[0:TILE]), (probe_hbm, probe), (left_hbm, left), (right_hbm, right),
+             (pattern_hbm, pattern)]
     for y in range(WORKERS // 2):
         mine = pl.multiple_of(low_row(2 * y + core), LOW)
         other = pl.multiple_of(low_row(2 * y + 1 - core), LOW)
-        low_rows.append((mine, other))
-        fetches.append(pltpu.make_async_copy(low_mine.at[y], cells.at[pl.ds(mine, LOW)], sem.at[1 + 2 * y]))
-        fetches.append(pltpu.make_async_copy(low_other.at[y], cells.at[pl.ds(other, LOW)], sem.at[2 + 2 * y]))
+        pairs.append((low_mine.at[y], cells.at[pl.ds(mine, LOW)]))
+        pairs.append((low_other.at[y], cells.at[pl.ds(other, LOW)]))
+    fetches = [pltpu.make_async_copy(source, target, sem.at[i]) for i, (source, target) in enumerate(pairs)]
     for copy in fetches:
         copy.start()
 
@@ -115,7 +113,8 @@
 
     copies = []
     for y in range(WORKERS // 2):
-        mine, other = low_rows[y]
+        mine = pl.multiple_of(low_row(2 * y + core), LOW)
+        other = pl.multiple_of(low_row(2 * y + 1 - core), LOW)
         own_mine = pl.multiple_of((2 * y + core) * OWN, OWN)
         own_other = pl.multiple_of((2 * y + 1 - core) * OWN, OWN)
         copies.append(pltpu.make_async_copy(sums.at[pl.ds(other, LOW)], send_low.at[y], sem.at[4 * y]))
@@ -173,26 +172,29 @@
     return pl.BlockSpec(memory_space=pl.ANY)
 
 
-def patch_sums(corners, live, parity, own_cells, low_mine, low_other, probe, patterns, left, right):
+def patch_sums(corners, live, me, own_cells, low_mine, low_other, probe, patterns, left, right):
     own_chunk = jax.ShapeDtypeStruct((WORKERS // 2, OWN, 2 * WIDE), jnp.float32)
     low_chunk = jax.ShapeDtypeStruct((WORKERS // 2, LOW, 2 * WIDE), jnp.float32)
     return pl.pallas_call(
         slots_kernel,
         out_shape=(own_chunk, own_chunk, low_chunk, low_chunk),
-        in_specs=[smem(), smem(), smem(), pl.BlockSpec(memory_space=pltpu.HBM), hbm(), hbm(),
-                  vmem(), vmem(), vmem(), vmem()],
+        in_specs=[smem()] * 3 + [hbm()] * 7,
         out_specs=(hbm(), hbm(), hbm(), hbm()),
         scratch_shapes=[
             pltpu.VMEM((WIDE, 2 * WIDE), jnp.float32),
             pltpu.VMEM((WIDE, 2 * WIDE), jnp.float32),
             pltpu.VMEM((2 * SIDE, SIDE), jnp.bfloat16),
             pltpu.VMEM((SIDE, 2 * SIDE), jnp.bfloat16),
-            pltpu.SemaphoreType.DMA((2 * WORKERS,)),
+            pltpu.VMEM((2, SIDE, SIDE), jnp.float32),
+            pltpu.VMEM((SLOTS, SIDE, SIDE), jnp.bfloat16),
+            pltpu.VMEM((2 * SIDE, 2 * SIDE), jnp.bfloat16),
+            pltpu.VMEM((2 * SIDE, 2 * SIDE), jnp.bfloat16),
+            pltpu.SemaphoreType.DMA((5 + 2 * WORKERS,)),
         ],
-        compiler_params=pltpu.CompilerParams(vmem_limit_bytes=40 * 2**20),
+        compiler_params=pltpu.CompilerParams(vmem_limit_bytes=61 * 2**20),
         cost_estimate=pl.CostEstimate(flops=2 * 10**9, bytes_accessed=12 * 10**6, transcendentals=0),
         name="patch_sums",
-    )(corners, live, parity, own_cells, low_mine, low_other, probe, patterns, left, right)
+    )(corners, live, me, own_cells, low_mine, low_other, probe, patterns, left, right)
 
 
 def weight_rows(corners, live, me, probe):
@@ -223,6 +225,12 @@
     me = lax.axis_index("pat").astype(jnp.int32)
     corners = offsets[0, 0]
 
+    mirrored = lambda worker: 2 * (7 - worker // 2) + worker % 2
+    first_half = lambda tile, worker: worker if worker < 8 else None
+    second_half = lambda tile, worker: mirrored(worker) if worker < 8 else None
+    mirrored = lambda worker: 2 * (7 - worker // 2) + worker % 2
+    first_half = lambda tile, worker: worker if worker < 8 else None
+    second_half = lambda tile, worker: mirrored(worker) if worker < 8 else None
     own_left = jnp.concatenate([own[0, :, :SIDE], own[1, :, :SIDE]], 1)
     from_right = moved(own_left, -1, lambda tile, worker: worker if tile % GRID_C else None)
     spare_re = jnp.zeros((OWN, 8), jnp.float32)
@@ -231,18 +239,17 @@
     shard = jnp.concatenate(
         [own[0], from_right[:, :SIDE - 8], spare_re, own[1], from_right[:, SIDE:]], 1)
     own_cells = lax.all_gather(shard, "pat", axis=0, tiled=True)
-    mirrored = lambda worker: 2 * (7 - worker // 2) + worker % 2
-    low_a = moved(shard[:LOW], -GRID_C, lambda tile, worker: worker if worker < 8 else None)
-    low_b = moved(shard[LOW:], -GRID_C, lambda tile, worker: mirrored(worker) if worker < 8 else None)
+    low = moved(shard[:LOW], -GRID_C, first_half) + moved(shard[LOW:], -GRID_C, second_half)
     same_core = [list(range(0, WORKERS, 2)), list(range(1, WORKERS, 2))]
     sibling = [(i, i ^ 1) for i in range(WORKERS)]
-    low_mine = lax.all_to_all(
-        jnp.broadcast_to(low_a + low_b, (WORKERS // 2, LOW, 2 * WIDE)), "pat", 0, 0, axis_index_groups=same_core)
+
+    low_mine = lax.all_gather(low, "pat", axis=0, tiled=True, axis_index_groups=same_core)
+    low_mine = low_mine.reshape(WORKERS // 2, LOW, 2 * WIDE)
     low_other = lax.ppermute(low_mine, "pat", sibling)
 
     left_table, right_table = dft_blocks(SIDE)
     keep_own, send_own, keep_low, send_low = patch_sums(
-        corners, live_count, (me % 2).reshape(1), own_cells, low_mine, low_other, probe_wave, amplitudes[0, 0],
+        corners, live_count, me.reshape(1), own_cells, low_mine, low_other, probe_wave, amplitudes[0, 0],
         left_table, right_table)
     other_low = lax.ppermute(send_low, "pat", sibling)
     other_own = lax.ppermute(send_own, "pat", sibling)
@@ -258,11 +265,11 @@
     weights = weight_rows(tile_corners, tile_live, me.reshape(1), probe_wave)
 
     summed_low = jnp.sum(lax.all_to_all(both_low, "pat", 0, 0, axis_index_groups=same_core), 0)
-    low = jnp.concatenate([summed_low, weights[OWN:]], 1)
-    down_a = moved(low, GRID_C, lambda tile, worker: worker if worker < 8 else None)
-    down_b = moved(low, GRID_C, lambda tile, worker: mirrored(worker) if worker >= 8 else None)
+    low_sums = jnp.concatenate([summed_low, weights[OWN:]], 1)
+    down_first = moved(low_sums, GRID_C, first_half)
+    down_second = moved(low_sums, GRID_C, lambda tile, worker: mirrored(worker) if worker >= 8 else None)
     upper_sum = (
-        jnp.concatenate([summed_own, weights[:OWN]], 1) + jnp.concatenate([down_a, down_b], 0)
+        jnp.concatenate([summed_own, weights[:OWN]], 1) + jnp.concatenate([down_first, down_second], 0)
     ).reshape(OWN, 3, WIDE)
     to_right = upper_sum[:, :, TILE:].reshape(OWN, 3 * SIDE)
     from_left = moved(to_right, 1, lambda tile, worker: worker if tile % GRID_C != GRID_C - 1 else None)

time: 173 us -> 162 us (0.936)
  starting transfers between devices: 32.2 us -> 47.1 us
  Pallas kernels: 25.5 us -> 15.6 us
  waiting for transfers between devices: 49.1 us -> 41.6 us
  blocking collectives: 35.4 us -> 29.2 us
    all_to_all x1 -> x0, blocking collectives: 35.4 us -> none  [local(): lax.all_to_all(jnp.broadcast_to(low_a + low_b, (WORKERS // 2, LOW, 2 * WI...]
    all_gather x0 -> x1, blocking collectives: none -> 29.2 us  [local(): lax.all_gather(low, 'pat', axis=0, tiled=True, axis_index_groups=same_core)]
    ppermute x6, starting transfers between devices: 22.4 us -> 32.8 us  [moved(): return lax.ppermute(value, ('obj', 'pat'), pairs)]
    pallas_call x1, Pallas kernels: 17.7 us -> 7.83 us  [patch_sums(): pl.pallas_call(slots_kernel, out_shape=(own_chunk, own_chunk, low_chunk,...]
    ppermute x6, waiting for transfers between devices: 27.4 us -> 20.7 us  [moved(): return lax.ppermute(value, ('obj', 'pat'), pairs)]
    all_to_all x1, starting transfers between devices: 3.56 us -> 6.58 us  [local(): lax.all_to_all(both_low, 'pat', 0, 0, axis_index_groups=same_core)]
    another operation x2 -> x0, other arithmetic: 2.1 us -> none
    unnamed x13 -> x15, local copies, waits for them, and re-layouts: 3.1 us -> 1.05 us
where the time goes in v3:
time: 162 us; the launch traced here: 161 us
  starting transfers between devices  47.1 us (29%)
  waiting for transfers between devices  41.6 us (26%)
  blocking collectives  29.2 us (18%)
  Pallas kernels  15.6 us (10%)
  between operations  14.3 us (9%)
  local copies, waits for them, and re-layouts  7.3 us (5%)
  other arithmetic  5.99 us (4%)
    ppermute x6, starting transfers between devices, moved(): return lax.ppermute(value, ('obj', 'pat'), pairs)  32.8 us
    all_gather x1, blocking collectives, local(): lax.all_gather(low, 'pat', axis=0, tiled=True, axis_index_groups=same_core)  29.2 us
    ppermute x6, waiting for transfers between devices, moved(): return lax.ppermute(value, ('obj', 'pat'), pairs)  20.7 us
    all_to_all x1, waiting for transfers between devices, local(): lax.all_to_all(both_low, 'pat', 0, 0, axis_index_groups=same_core)  16.9 us
    pallas_call x1, Pallas kernels, patch_sums(): pl.pallas_call(slots_kernel, out_shape=(own_chunk, own_chunk, low_chunk,...  7.83 us
    pallas_call x1, Pallas kernels, weight_rows(): pl.pallas_call(weight_kernel, out_shape=jax.ShapeDtypeStruct((ROWS, WIDE)...  7.78 us
    all_to_all x1, starting transfers between devices, local(): lax.all_to_all(both_low, 'pat', 0, 0, axis_index_groups=same_core)  6.58 us
    ppermute x1, starting transfers between devices, local(): other_own = lax.ppermute(send_own, 'pat', sibling)  3.8 us
  transfers between devices with their start and end apart: 12, of which 9 were waited for; matrix products, arithmetic and copies ran while one was open for 5% of the time, Pallas kernels for 5%

profile of v3, /device:TPU:68, one launch (start us, length us, event | category | flops | bytes accessed | tf_op | source)
XLA Modules:
  0.0 161.1 jit_solution(15824638453663568251)
XLA Ops:
  6.5 0.0 all-gather.2.cloned.1.call-start
  6.5 0.8 slice_bitcast_fusion.7
  7.3 1.9 %collective-permute-start = (f32[32,512]{1,0:T(8,128)S(1)}, f32[32,512]{1,0:T(8,128)S(1)}, u32[]{:S(2)}, u32[]{:S(2)}) collective-permute-start(f32[32,512]{1,0:T(8,128)S(1)} %pad_maximum_fusion.2), channel_id=1, source_target_pairs={{16,0},{17,1},{18,2},{19,3},{20,4},{21,5},{22,6},{23,7},{24,8},{25... | collective-permute-start | bytes 196616 | tf_op jit(solution)/shard_map/ppermute | solution.py:220
  9.3 0.9 slice_bitcast_fusion.4
  10.8 0.7 convert_element_type.29
  11.5 0.1 copy.13
  11.6 0.1 convert_element_type.30
  11.7 2.1 %collective-permute-done = f32[32,512]{1,0:T(8,128)S(1)} collective-permute-done((f32[32,512]{1,0:T(8,128)S(1)}, f32[32,512]{1,0:T(8,128)S(1)}, u32[]{:S(2)}, u32[]{:S(2)}) %collective-permute-start) | collective-permute-done | bytes 65568 | tf_op jit(solution)/shard_map/ppermute | solution.py:220
  13.9 0.8 concatenate.27
  14.6 0.0 all-gather.2.cloned.1.call-update
  14.6 0.0 reduce-scatter.2.cloned.1.call-start
  14.7 1.0 fusion.4
  15.7 9.6 %collective-permute-start.1 = (f32[16,1536]{1,0:T(8,128)S(1)}, f32[16,1536]{1,0:T(8,128)S(1)}, u32[]{:S(2)}, u32[]{:S(2)}) collective-permute-start(f32[16,1536]{1,0:T(8,128)S(1)} %get-tuple-element.44), channel_id=1, source_target_pairs={{64,0},{65,1},{66,2},{67,3},{68,4},{69,5},{70,6},{71,7},{80,16},{8... | collective-permute-start | bytes 294920 | tf_op jit(solution)/shard_map/ppermute | solution.py:220
  25.3 3.6 %collective-permute-start.2 = (f32[16,1536]{1,0:T(8,128)S(1)}, f32[16,1536]{1,0:T(8,128)S(1)}, u32[]{:S(2)}, u32[]{:S(2)}) collective-permute-start(f32[16,1536]{1,0:T(8,128)S(1)} %get-tuple-element.43), channel_id=1, source_target_pairs={{64,14},{65,15},{66,12},{67,13},{68,10},{69,11},{70,8},{71,9},{80,... | collective-permute-start | bytes 294920 | tf_op jit(solution)/shard_map/ppermute | solution.py:220
  28.9 0.7 collective-permute-done.1
  29.6 1.9 %collective-permute-done.2 = f32[16,1536]{1,0:T(8,128)S(1)} collective-permute-done((f32[16,1536]{1,0:T(8,128)S(1)}, f32[16,1536]{1,0:T(8,128)S(1)}, u32[]{:S(2)}, u32[]{:S(2)}) %collective-permute-start.2) | collective-permute-done | bytes 98336 | tf_op jit(solution)/shard_map/ppermute | solution.py:220
  31.5 29.2 %all_gather.7 = f32[128,1536]{1,0:T(8,128)S(1)} all-gather(f32[16,1536]{1,0:T(8,128)S(1)} %add.40), channel_id=1, replica_groups={{0,2,4,6,8,10,12,14},{1,3,5,7,9,11,13,15},{16,18,20,22,24,26,28,30},{17..., dimensions={0}, use_global_device_ids=true | all-gather | bytes 884736 | tf_op jit(solution)/shard_map/all_gather | solution.py:246
  60.7 1.9 %collective-permute-start.3 = (f32[8,16,1536]{2,1,0:T(8,128)S(1)}, f32[8,16,1536]{2,1,0:T(8,128)S(1)}, u32[]{:S(2)}, u32[]{:S(2)}) collective-permute-start(f32[8,16,1536]{2,1,0:T(8,128)S(1)} %bitcast.69), channel_id=1, source_target_pairs={{0,1},{1,0},{2,3},{3,2},{4,5},{5,4},{6,7},{7,6},{8,9},{9,8},{10,11... | collective-permute-start | bytes 2359304 | tf_op jit(solution)/shard_map/ppermute | solution.py:248
  62.6 0.7 copy.14.corners
  63.3 1.6 collective-permute-done.3.low_other
  64.8 0.9 copy-done.5
  65.7 7.8 %patch_sums.1 = (f32[8,32,1536]{2,1,0:T(8,128)}, f32[8,32,1536]{2,1,0:T(8,128)}, f32[8,16,1536]{2,1,0:T(8,128)}, f32[8,16,1536]{2,1,0:T(8,128)}) custom-call(s32[4,2]{1,0:T(4,128)} %copy.14.corners, s32[1,1]{1,0:T(1,128)S(6)} %copy.38.live, s32[1]{0:T(128)} %bitcast.1.me, f32[512,1536]{1,0:T(8,128)} %all-gather.2.cloned.1.call-done.own_hbm, ...), custom_call_target="tpu_custom_call" | custom-call | flops 2000000000 | bytes 12000000 | tf_op jit(solution)/shard_map/patch_sums/pallas_call | solution.py:178
  73.6 3.8 %collective-permute-start.4 = (f32[8,32,1536]{2,1,0:T(8,128)}, f32[8,32,1536]{2,1,0:T(8,128)S(1)}, u32[]{:S(2)}, u32[]{:S(2)}) collective-permute-start(f32[8,32,1536]{2,1,0:T(8,128)} %get-tuple-element.36), channel_id=1, source_target_pairs={{0,1},{1,0},{2,3},{3,2},{4,5},{5,4},{6,7},{7,6},{8,9},{9,8},{10,11... | collective-permute-start | bytes 4718600 | tf_op jit(solution)/shard_map/ppermute | solution.py:255
  77.4 1.9 %collective-permute-start.5 = (f32[8,16,1536]{2,1,0:T(8,128)}, f32[8,16,1536]{2,1,0:T(8,128)S(1)}, u32[]{:S(2)}, u32[]{:S(2)}) collective-permute-start(f32[8,16,1536]{2,1,0:T(8,128)} %get-tuple-element.38), channel_id=1, source_target_pairs={{0,1},{1,0},{2,3},{3,2},{4,5},{5,4},{6,7},{7,6},{8,9},{9,8},{10,11... | collective-permute-start | bytes 2359304 | tf_op jit(solution)/shard_map/ppermute | solution.py:254
  79.3 2.5 %collective-permute-done.5 = f32[8,16,1536]{2,1,0:T(8,128)S(1)} collective-permute-done((f32[8,16,1536]{2,1,0:T(8,128)}, f32[8,16,1536]{2,1,0:T(8,128)S(1)}, u32[]{:S(2)}, u32[]{:S(2)}) %collective-permute-start.5) | collective-permute-done | bytes 786464 | tf_op jit(solution)/shard_map/ppermute | solution.py:254
  81.8 2.1 %add.42 = f32[8,16,1536]{2,1,0:T(8,128)} add(f32[8,16,1536]{2,1,0:T(8,128)} %get-tuple-element.37, f32[8,16,1536]{2,1,0:T(8,128)S(1)} %collective-permute-done.5) | non-fusion elementwise | flops 196608 | bytes 2359296 | tf_op jit(solution)/shard_map/add | solution.py:257
  83.9 0.0 collective-permute-done.4
  83.9 1.4 add.41
  85.3 0.0 reduce-scatter.2.cloned.1.call-update
  85.3 6.6 %all-to-all-start = ((f32[8,16,1536]{2,1,0:T(8,128)}), f32[8,16,1536]{2,1,0:T(8,128)S(1)}, u32[]{:S(2)}, u32[]{:S(2)}) async-start(f32[8,16,1536]{2,1,0:T(8,128)} %add.42), calls=%async_computation.1 | async-start | bytes 1572864 | tf_op jit(solution)/shard_map/all_to_all | solution.py:267
  91.9 0.9 slice.107
  92.8 0.9 slice.108
  93.7 0.1 copy.23
  93.8 0.1 copy.17.corners
  93.9 0.1 copy.24
  94.0 0.0 copy-done
  94.0 7.8 %weight_rows.1 = f32[48,768]{1,0:T(8,128)S(1)} custom-call(s32[16,8]{1,0:T(8,128)S(1)} %copy.17.corners, s32[16]{0:T(128)S(1)} %convert_bitcast_fusion.1.live, s32[1]{0:T(128)} %bitcast.1.me, f32[2,256,256]{2,1,0:T(8,128)S(1)} %copy-done), custom_call_target="tpu_custom_call" | custom-call | flops 10000000 | bytes 1000000 | tf_op jit(solution)/shard_map/weight_rows/pallas_call | solution.py:201
  101.8 16.9 %all-to-all-done = f32[8,16,1536]{2,1,0:T(8,128)S(1)} async-done(((f32[8,16,1536]{2,1,0:T(8,128)}), f32[8,16,1536]{2,1,0:T(8,128)S(1)}, u32[]{:S(2)}, u32[]{:S(2)}) %all-to-all-start) | async-done | bytes 786464 | tf_op jit(solution)/shard_map/all_to_all | solution.py:267
  118.7 1.3 collective-permute-start.7
  120.0 13.3 %collective-permute-start.6 = (f32[16,2304]{1,0:T(8,128)S(1)}, f32[16,2304]{1,0:T(8,128)S(1)}, u32[]{:S(2)}, u32[]{:S(2)}) collective-permute-start(f32[16,2304]{1,0:T(8,128)S(1)} %pad_maximum_fusion.1), channel_id=1, source_target_pairs={{0,64},{1,65},{2,66},{3,67},{4,68},{5,69},{6,70},{7,71},{16,80},{1... | collective-permute-start | bytes 442376 | tf_op jit(solution)/shard_map/ppermute | solution.py:220
  133.3 7.4 %collective-permute-done.7 = f32[16,2304]{1,0:T(8,128)S(1)} collective-permute-done((f32[16,2304]{1,0:T(8,128)S(1)}, f32[16,2304]{1,0:T(8,128)S(1)}, u32[]{:S(2)}, u32[]{:S(2)}) %collective-permute-start.7) | collective-permute-done | bytes 147488 | tf_op jit(solution)/shard_map/ppermute | solution.py:220
  140.7 5.2 %collective-permute-done.6 = f32[16,2304]{1,0:T(8,128)S(1)} collective-permute-done((f32[16,2304]{1,0:T(8,128)S(1)}, f32[16,2304]{1,0:T(8,128)S(1)}, u32[]{:S(2)}, u32[]{:S(2)}) %collective-permute-start.6) | collective-permute-done | bytes 147488 | tf_op jit(solution)/shard_map/ppermute | solution.py:220
  145.9 0.0 reduce-scatter.2.cloned.1.call-done
  145.9 0.9 pad_maximum_fusion
  146.9 0.1 bitcast_add_fusion
  147.0 3.1 %collective-permute-start.8 = (f32[32,768]{1,0:T(8,128)S(1)}, f32[32,768]{1,0:T(8,128)S(1)}, u32[]{:S(2)}, u32[]{:S(2)}) collective-permute-start(f32[32,768]{1,0:T(8,128)S(1)} %bitcast.76), channel_id=1, source_target_pairs={{0,16},{1,17},{2,18},{3,19},{4,20},{5,21},{6,22},{7,23},{8,24},{9,... | collective-permute-start | bytes 294920 | tf_op jit(solution)/shard_map/ppermute | solution.py:220
  150.1 3.4 %collective-permute-done.8 = f32[32,768]{1,0:T(8,128)S(1)} collective-permute-done((f32[32,768]{1,0:T(8,128)S(1)}, f32[32,768]{1,0:T(8,128)S(1)}, u32[]{:S(2)}, u32[]{:S(2)}) %collective-permute-start.8) | collective-permute-done | bytes 98336 | tf_op jit(solution)/shard_map/ppermute | solution.py:220
  153.6 0.7 maximum_bitcast_fusion
  (31 shorter events, 0.3 us)
Async XLA Ops:
  6.5 56.1 %copy-start.4 = (s32[1,1,4,2]{2,3,1,0:T(2,128)S(1)}, s32[1,1,4,2]{2,3,1,0:T(2,128)}, u32[]{:S(2)}) copy-start(s32[1,1,4,2]{2,3,1,0:T(2,128)} %param.14) | copy-start | bytes 100
  6.5 58.3 %all-gather.2.cloned.1.call-start = ((), (), s32[]{:S(2)}) async-start(), calls=%async_computation.2 | async-start | bytes 3342336 | tf_op jit(solution)/shard_map/all_gather | solution.py:241
  7.3 6.5 %collective-permute-start = (f32[32,512]{1,0:T(8,128)S(1)}, f32[32,512]{1,0:T(8,128)S(1)}, u32[]{:S(2)}, u32[]{:S(2)}) collective-permute-start(f32[32,512]{1,0:T(8,128)S(1)} %pad_maximum_fusion.2), channel_id=1, source_target_pairs={{16,0},{17,1},{18,2},{19,3},{20,4},{21,5},{22,6},{23,7},{24,8},{25... | collective-permute-start | bytes 196616 | tf_op jit(solution)/shard_map/ppermute | solution.py:220
  14.6 131.3 %reduce-scatter.2.cloned.1.call-start = ((), (), s32[]{:S(2)}) async-start(), calls=%async_computation.3 | async-start | bytes 1769472 | tf_op jit(solution)/shard_map/reduce_scatter | solution.py:259
  15.7 13.9 %collective-permute-start.1 = (f32[16,1536]{1,0:T(8,128)S(1)}, f32[16,1536]{1,0:T(8,128)S(1)}, u32[]{:S(2)}, u32[]{:S(2)}) collective-permute-start(f32[16,1536]{1,0:T(8,128)S(1)} %get-tuple-element.44), channel_id=1, source_target_pairs={{64,0},{65,1},{66,2},{67,3},{68,4},{69,5},{70,6},{71,7},{80,16},{8... | collective-permute-start | bytes 294920 | tf_op jit(solution)/shard_map/ppermute | solution.py:220
  25.3 6.2 %collective-permute-start.2 = (f32[16,1536]{1,0:T(8,128)S(1)}, f32[16,1536]{1,0:T(8,128)S(1)}, u32[]{:S(2)}, u32[]{:S(2)}) collective-permute-start(f32[16,1536]{1,0:T(8,128)S(1)} %get-tuple-element.43), channel_id=1, source_target_pairs={{64,14},{65,15},{66,12},{67,13},{68,10},{69,11},{70,8},{71,9},{80,... | collective-permute-start | bytes 294920 | tf_op jit(solution)/shard_map/ppermute | solution.py:220
  60.7 4.2 %copy-start.3 = (f32[128,1536]{1,0:T(8,128)}, f32[128,1536]{1,0:T(8,128)S(1)}, u32[]{:S(2)}) copy-start(f32[128,1536]{1,0:T(8,128)S(1)} %all_gather.7) | copy-start | bytes 2359300
  60.7 4.2 %collective-permute-start.3 = (f32[8,16,1536]{2,1,0:T(8,128)S(1)}, f32[8,16,1536]{2,1,0:T(8,128)S(1)}, u32[]{:S(2)}, u32[]{:S(2)}) collective-permute-start(f32[8,16,1536]{2,1,0:T(8,128)S(1)} %bitcast.69), channel_id=1, source_target_pairs={{0,1},{1,0},{2,3},{3,2},{4,5},{5,4},{6,7},{7,6},{8,9},{9,8},{10,11... | collective-permute-start | bytes 2359304 | tf_op jit(solution)/shard_map/ppermute | solution.py:248
  64.8 0.9 copy-start.5
  73.6 10.3 %copy-start.1 = (f32[8,32,1536]{2,1,0:T(8,128)S(1)}, f32[8,32,1536]{2,1,0:T(8,128)}, u32[]{:S(2)}) copy-start(f32[8,32,1536]{2,1,0:T(8,128)} %get-tuple-element.35) | copy-start | bytes 4718596
  73.6 10.3 %collective-permute-start.4 = (f32[8,32,1536]{2,1,0:T(8,128)}, f32[8,32,1536]{2,1,0:T(8,128)S(1)}, u32[]{:S(2)}, u32[]{:S(2)}) collective-permute-start(f32[8,32,1536]{2,1,0:T(8,128)} %get-tuple-element.36), channel_id=1, source_target_pairs={{0,1},{1,0},{2,3},{3,2},{4,5},{5,4},{6,7},{7,6},{8,9},{9,8},{10,11... | collective-permute-start | bytes 4718600 | tf_op jit(solution)/shard_map/ppermute | solution.py:255
  77.4 4.4 %collective-permute-start.5 = (f32[8,16,1536]{2,1,0:T(8,128)}, f32[8,16,1536]{2,1,0:T(8,128)S(1)}, u32[]{:S(2)}, u32[]{:S(2)}) collective-permute-start(f32[8,16,1536]{2,1,0:T(8,128)} %get-tuple-element.38), channel_id=1, source_target_pairs={{0,1},{1,0},{2,3},{3,2},{4,5},{5,4},{6,7},{7,6},{8,9},{9,8},{10,11... | collective-permute-start | bytes 2359304 | tf_op jit(solution)/shard_map/ppermute | solution.py:254
  85.3 8.7 %copy-start = (f32[2,256,256]{2,1,0:T(8,128)S(1)}, f32[2,256,256]{2,1,0:T(8,128)}, u32[]{:S(2)}) copy-start(f32[2,256,256]{2,1,0:T(8,128)} %probe.1) | copy-start | bytes 1572868
  85.3 33.3 %all-to-all-start = ((f32[8,16,1536]{2,1,0:T(8,128)}), f32[8,16,1536]{2,1,0:T(8,128)S(1)}, u32[]{:S(2)}, u32[]{:S(2)}) async-start(f32[8,16,1536]{2,1,0:T(8,128)} %add.42), calls=%async_computation.1 | async-start | bytes 1572864 | tf_op jit(solution)/shard_map/all_to_all | solution.py:267
  118.7 22.0 %collective-permute-start.7 = (f32[16,2304]{1,0:T(8,128)S(1)}, f32[16,2304]{1,0:T(8,128)S(1)}, u32[]{:S(2)}, u32[]{:S(2)}) collective-permute-start(f32[16,2304]{1,0:T(8,128)S(1)} %pad_maximum_fusion.1), channel_id=1, source_target_pairs={{8,70},{9,71},{10,68},{11,69},{12,66},{13,67},{14,64},{15,65},{24,... | collective-permute-start | bytes 442376 | tf_op jit(solution)/shard_map/ppermute | solution.py:220
  120.0 25.9 %collective-permute-start.6 = (f32[16,2304]{1,0:T(8,128)S(1)}, f32[16,2304]{1,0:T(8,128)S(1)}, u32[]{:S(2)}, u32[]{:S(2)}) collective-permute-start(f32[16,2304]{1,0:T(8,128)S(1)} %pad_maximum_fusion.1), channel_id=1, source_target_pairs={{0,64},{1,65},{2,66},{3,67},{4,68},{5,69},{6,70},{7,71},{16,80},{1... | collective-permute-start | bytes 442376 | tf_op jit(solution)/shard_map/ppermute | solution.py:220
  140.7 12.8 %copy-start.2 = (f32[1,2,32,512]{3,2,1,0:T(8,128)S(1)}, f32[1,2,32,512]{3,2,1,0:T(8,128)}, u32[]{:S(2)}) copy-start(f32[1,2,32,512]{3,2,1,0:T(8,128)} %param.11) | copy-start | bytes 393220
  147.0 6.5 %collective-permute-start.8 = (f32[32,768]{1,0:T(8,128)S(1)}, f32[32,768]{1,0:T(8,128)S(1)}, u32[]{:S(2)}, u32[]{:S(2)}) collective-permute-start(f32[32,768]{1,0:T(8,128)S(1)} %bitcast.76), channel_id=1, source_target_pairs={{0,16},{1,17},{2,18},{3,19},{4,20},{5,21},{6,22},{7,23},{8,24},{9,... | collective-permute-start | bytes 294920 | tf_op jit(solution)/shard_map/ppermute | solution.py:220
Sparse Core Ops, SparseCore 0:
  14.8 48.4 all-gather.1
  85.4 51.2 reduce-scatter.1

commit v4 on v3

--- a/solution.py
+++ b/solution.py
@@ -66,50 +66,61 @@
     for copy in fetches:
         copy.wait()
 
-    def one(slot, _):
-        row = corners[slot, 0]
-        col = corners[slot, 1]
-        base = pl.multiple_of(col // 128 * 128, 128)
-        shift = col % 128
-        back = (SPAN - shift) % SPAN
-        for i in range(4):
-            here = slice(64 * i, 64 * i + 64)
-            rows = pl.ds(pl.multiple_of(row + 64 * i, 8), 64)
-            cell_re = pltpu.roll(cells[rows, pl.ds(base, SPAN)], back, 1)[:, :SIDE]
-            cell_im = pltpu.roll(cells[rows, pl.ds(pl.multiple_of(base + WIDE, 128), SPAN)], back, 1)[:, :SIDE]
-            probe_re = probe[0, here, :]
-            probe_im = probe[1, here, :]
-            wave[here, :] = (probe_re * cell_re - probe_im * cell_im).astype(jnp.bfloat16)
-            wave[64 * i + SIDE:64 * i + SIDE + 64, :] = (
-                probe_re * cell_im + probe_im * cell_re).astype(jnp.bfloat16)
+    def one(pair, _):
+        at = []
+        for e in range(2):
+            slot = 2 * pair + e
+            used = slot < live[0, 0]
+            row = jnp.where(used, corners[slot, 0], 0)
+            col = jnp.where(used, corners[slot, 1], 0)
+            base = pl.multiple_of(col // 128 * 128, 128)
+            at.append((used, row, base, pl.multiple_of(base + WIDE, 128), col % 128))
+        for e, (used, row, base_re, base_im, shift) in enumerate(at):
+            back = (SPAN - shift) % SPAN
+            columns = slice(SIDE * e, SIDE * e + SIDE)
+            for i in range(4):
+                here = slice(64 * i, 64 * i + 64)
+                rows = pl.ds(pl.multiple_of(row + 64 * i, 8), 64)
+                cell_re = pltpu.roll(cells[rows, pl.ds(base_re, SPAN)], back, 1)[:, :SIDE]
+                cell_im = pltpu.roll(cells[rows, pl.ds(base_im, SPAN)], back, 1)[:, :SIDE]
+                probe_re = probe[0, here, :]
+                probe_im = probe[1, here, :]
+                wave[here, columns] = (probe_re * cell_re - probe_im * cell_im).astype(jnp.bfloat16)
+                wave[64 * i + SIDE:64 * i + SIDE + 64, columns] = (
+                    probe_re * cell_im + probe_im * cell_re).astype(jnp.bfloat16)
         half_way = jnp.dot(left[...], wave[...], preferred_element_type=jnp.float32).astype(jnp.bfloat16)
-        half[:, :SIDE] = half_way[:SIDE]
-        half[:, SIDE:] = half_way[SIDE:]
+        for e in range(2):
+            half[SIDE * e:SIDE * e + SIDE, :SIDE] = half_way[:SIDE, SIDE * e:SIDE * e + SIDE]
+            half[SIDE * e:SIDE * e + SIDE, SIDE:] = half_way[SIDE:, SIDE * e:SIDE * e + SIDE]
         far = jnp.dot(half[...], right[...], preferred_element_type=jnp.float32)
         far_re = far[:, :SIDE]
         far_im = far[:, SIDE:]
-        ratio = pattern[slot].astype(jnp.float32) * lax.rsqrt(far_re * far_re + far_im * far_im + 0.01)
+        amplitude = pattern[pl.ds(2 * pair, 2)].reshape(2 * SIDE, SIDE).astype(jnp.float32)
+        ratio = amplitude * lax.rsqrt(far_re * far_re + far_im * far_im + 0.01)
         half[:, :SIDE] = (far_re * ratio).astype(jnp.bfloat16)
         half[:, SIDE:] = (far_im * ratio).astype(jnp.bfloat16)
         half_back = jnp.dot(half[...], left[...], preferred_element_type=jnp.float32).astype(jnp.bfloat16)
-        wave[:SIDE, :] = half_back[:, :SIDE]
-        wave[SIDE:, :] = half_back[:, SIDE:]
+        for e in range(2):
+            wave[:SIDE, SIDE * e:SIDE * e + SIDE] = half_back[SIDE * e:SIDE * e + SIDE, :SIDE]
+            wave[SIDE:, SIDE * e:SIDE * e + SIDE] = half_back[SIDE * e:SIDE * e + SIDE, SIDE:]
         near = jnp.dot(right[...], wave[...], preferred_element_type=jnp.float32)
-        for i in range(4):
-            here = slice(64 * i, 64 * i + 64)
-            rows = pl.ds(pl.multiple_of(row + 64 * i, 8), 64)
-            near_re = near[64 * i:64 * i + 64]
-            near_im = near[64 * i + SIDE:64 * i + SIDE + 64]
-            probe_re = probe[0, here, :]
-            probe_im = probe[1, here, :]
-            blank = jnp.zeros((64, 128), jnp.float32)
-            term_re = jnp.concatenate([probe_re * near_re + probe_im * near_im, blank], 1)
-            term_im = jnp.concatenate([probe_re * near_im - probe_im * near_re, blank], 1)
-            sums[rows, pl.ds(base, SPAN)] += pltpu.roll(term_re, shift, 1)
-            sums[rows, pl.ds(pl.multiple_of(base + WIDE, 128), SPAN)] += pltpu.roll(term_im, shift, 1)
+        for e, (used, row, base_re, base_im, shift) in enumerate(at):
+            columns = slice(SIDE * e, SIDE * e + SIDE)
+            for i in range(4):
+                here = slice(64 * i, 64 * i + 64)
+                rows = pl.ds(pl.multiple_of(row + 64 * i, 8), 64)
+                near_re = near[64 * i:64 * i + 64, columns]
+                near_im = near[64 * i + SIDE:64 * i + SIDE + 64, columns]
+                probe_re = probe[0, here, :]
+                probe_im = probe[1, here, :]
+                blank = jnp.zeros((64, 128), jnp.float32)
+                term_re = jnp.where(used, probe_re * near_re + probe_im * near_im, 0.0)
+                term_im = jnp.where(used, probe_re * near_im - probe_im * near_re, 0.0)
+                sums[rows, pl.ds(base_re, SPAN)] += pltpu.roll(jnp.concatenate([term_re, blank], 1), shift, 1)
+                sums[rows, pl.ds(base_im, SPAN)] += pltpu.roll(jnp.concatenate([term_im, blank], 1), shift, 1)
         return 0
 
-    lax.fori_loop(0, live[0, 0], one, 0)
+    lax.fori_loop(0, (live[0, 0] + 1) // 2, one, 0)
 
     copies = []
     for y in range(WORKERS // 2):
@@ -135,29 +146,25 @@
         probe_im = probe[1, here, :]
         padded[PAD + 64 * i:PAD + 64 * i + 64, 0:SIDE] = probe_re * probe_re + probe_im * probe_im
     weights[...] = jnp.zeros_like(weights)
-    worker = me[0]
-    own_first = worker * OWN
-    low_first = low_row(worker)
+    own_first = me[0] * OWN
 
     def one(index, _):
-        other = index // SLOTS
+        source = index // SLOTS
         slot = index % SLOTS
-        row = corners[other, 2 * slot]
-        used = slot < live[other]
-        col = jnp.where(used, corners[other, 2 * slot + 1], 0)
-        base = pl.multiple_of(col // 128 * 128, 128)
-        shift = col % 128
-
-        def part(first, count, at):
-            start = jnp.where(used, jnp.clip(first - row + PAD, 0, PAD + SIDE), 0)
-            piece = padded[pl.ds(pl.multiple_of(start, 8), count), :]
-            weights[at:at + count, pl.ds(base, SPAN)] += pltpu.roll(piece, shift, 1)
-
-        part(own_first, OWN, 0)
-        part(low_first, LOW, OWN)
+        used = slot < live[source]
+        row = corners[source, 2 * slot] - jnp.where(source < WORKERS, 0, TILE)
+        col = corners[source, 2 * slot + 1]
+        first = own_first - row
+
+        @pl.when(used & (first > -OWN) & (first < SIDE))
+        def _():
+            base = pl.multiple_of(col // 128 * 128, 128)
+            piece = padded[pl.ds(pl.multiple_of(first + PAD, 8), OWN), :]
+            weights[:, pl.ds(base, SPAN)] += pltpu.roll(piece, col % 128, 1)
+
         return 0
 
-    lax.fori_loop(0, WORKERS * SLOTS, one, 0)
+    lax.fori_loop(0, 2 * WORKERS * SLOTS, one, 0)
 
 
 def smem():
@@ -183,8 +190,8 @@
         scratch_shapes=[
             pltpu.VMEM((WIDE, 2 * WIDE), jnp.float32),
             pltpu.VMEM((WIDE, 2 * WIDE), jnp.float32),
-            pltpu.VMEM((2 * SIDE, SIDE), jnp.bfloat16),
-            pltpu.VMEM((SIDE, 2 * SIDE), jnp.bfloat16),
+            pltpu.VMEM((2 * SIDE, 2 * SIDE), jnp.bfloat16),
+            pltpu.VMEM((2 * SIDE, 2 * SIDE), jnp.bfloat16),
             pltpu.VMEM((2, SIDE, SIDE), jnp.float32),
             pltpu.VMEM((SLOTS, SIDE, SIDE), jnp.bfloat16),
             pltpu.VMEM((2 * SIDE, 2 * SIDE), jnp.bfloat16),
@@ -200,7 +207,7 @@
 def weight_rows(corners, live, me, probe):
     return pl.pallas_call(
         weight_kernel,
-        out_shape=jax.ShapeDtypeStruct((ROWS, WIDE), jnp.float32),
+        out_shape=jax.ShapeDtypeStruct((OWN, WIDE), jnp.float32),
         in_specs=[smem(), smem(), smem(), vmem()],
         out_specs=vmem(),
         scratch_shapes=[pltpu.VMEM((SIDE + 2 * PAD, SPAN), jnp.float32)],
@@ -225,9 +232,6 @@
     me = lax.axis_index("pat").astype(jnp.int32)
     corners = offsets[0, 0]
 
-    mirrored = lambda worker: 2 * (7 - worker // 2) + worker % 2
-    first_half = lambda tile, worker: worker if worker < 8 else None
-    second_half = lambda tile, worker: mirrored(worker) if worker < 8 else None
     mirrored = lambda worker: 2 * (7 - worker // 2) + worker % 2
     first_half = lambda tile, worker: worker if worker < 8 else None
     second_half = lambda tile, worker: mirrored(worker) if worker < 8 else None
@@ -255,32 +259,54 @@
     other_own = lax.ppermute(send_own, "pat", sibling)
     both_own = (keep_own + other_own).reshape(WORKERS // 2 * OWN, 2 * WIDE)
     both_low = keep_low + other_low
-    both_own, both_low = lax.optimization_barrier((both_own, both_low))
+    marks = own_cells.reshape(WORKERS, OWN, 2 * WIDE)[:, :2, WIDE - 8:WIDE].reshape(WORKERS, 16)
+    both_own, both_low, marks = lax.optimization_barrier((both_own, both_low, marks))
     summed_own = lax.psum_scatter(
         both_own, "pat", scatter_dimension=0, tiled=True, axis_index_groups=same_core)
 
-    by_tile = own_cells.reshape(WORKERS, OWN, 2 * WIDE)
-    tile_corners = by_tile[:, 0, WIDE - 8:WIDE].astype(jnp.int32)
-    tile_live = by_tile[:, 1, WIDE - 8].astype(jnp.int32)
-    weights = weight_rows(tile_corners, tile_live, me.reshape(1), probe_wave)
+    upper_marks = moved(jnp.pad(marks, ((0, 0), (0, 112))), GRID_C, lambda tile, worker: worker)
+    all_marks = jnp.concatenate([marks, upper_marks[:, :16]], 0).astype(jnp.int32)
+    weights = weight_rows(all_marks[:, :8], all_marks[:, 8], me.reshape(1), probe_wave)
 
     summed_low = jnp.sum(lax.all_to_all(both_low, "pat", 0, 0, axis_index_groups=same_core), 0)
-    low_sums = jnp.concatenate([summed_low, weights[OWN:]], 1)
-    down_first = moved(low_sums, GRID_C, first_half)
-    down_second = moved(low_sums, GRID_C, lambda tile, worker: mirrored(worker) if worker >= 8 else None)
-    upper_sum = (
-        jnp.concatenate([summed_own, weights[:OWN]], 1) + jnp.concatenate([down_first, down_second], 0)
-    ).reshape(OWN, 3, WIDE)
-    to_right = upper_sum[:, :, TILE:].reshape(OWN, 3 * SIDE)
-    from_left = moved(to_right, 1, lambda tile, worker: worker if tile % GRID_C != GRID_C - 1 else None)
-    total = upper_sum[:, :, :TILE] + jnp.pad(
-        from_left.reshape(OWN, 3, SIDE), ((0, 0), (0, 0), (0, TILE - SIDE)))
-    weight = total[:, 2]
+
+    def main_columns(rows, parts):
+        return jnp.concatenate([rows[:, part * WIDE:part * WIDE + TILE] for part in range(parts)], 1)
+
+    def right_columns(rows, parts):
+        return jnp.concatenate([rows[:, part * WIDE + TILE:(part + 1) * WIDE] for part in range(parts)], 1)
+
+    inside = lambda tile: tile % GRID_C != GRID_C - 1
+    direct = lambda worker: worker if worker < 8 else None
+    by_mirror = lambda worker: mirrored(worker) if worker >= 8 else None
+
+    def pushed_down(rows, pick):
+        below = moved(main_columns(rows, 2), GRID_C, lambda tile, worker: pick(worker))
+        corner = moved(right_columns(rows, 2), GRID_C + 1, lambda tile, worker: pick(worker) if inside(tile) else None)
+        return below, corner
+
+    def with_side(here, side):
+        parts = []
+        for part in range(here.shape[1] // TILE):
+            first, cut, last = part * TILE, part * TILE + SIDE, (part + 1) * TILE
+            parts += [here[:, first:cut] + side[:, part * SIDE:(part + 1) * SIDE], here[:, cut:last]]
+        return jnp.concatenate(parts, 1)
+
+    from_mirror = pushed_down(summed_low, by_mirror)
+    from_direct = pushed_down(summed_low, direct)
+    own_sums = jnp.concatenate([summed_own, weights], 1)
+    from_left = moved(right_columns(own_sums, 3), 1, lambda tile, worker: worker if inside(tile) else None)
+    main = main_columns(own_sums, 3)
+    lower, top = lax.optimization_barrier((with_side(main[LOW:, :2 * TILE] + from_mirror[0], from_mirror[1]), main[:LOW, :2 * TILE]))
+    top, lower = lax.optimization_barrier((top + from_direct[0], lower))
+    lower, top = lax.optimization_barrier((
+        with_side(lower, from_left[LOW:, :2 * SIDE]), with_side(top, from_left[:LOW, :2 * SIDE])))
+    weight = with_side(main[:, 2 * TILE:], from_left[:, 2 * SIDE:])
+    main = jnp.concatenate([with_side(top, from_direct[1]), lower], 0)
+
     over = 1.0 / (weight + 1.0)
-    return jnp.stack([
-        (total[:, 0] - weight * own[0]) * over,
-        (total[:, 1] - weight * own[1]) * over,
-    ])[None]
+    total = lambda part: main[:, part * TILE:(part + 1) * TILE]
+    return jnp.stack([(total(part) - weight * own[part]) * over for part in range(2)])[None]
 
 
 def solution(mesh):

time: 162 us -> 153 us (0.944)
  the two profiles are of different devices: /device:TPU:68 before, /device:TPU:1 now
where the time goes in v4:
time: 153 us; the launch traced here: 151 us
  starting transfers between devices  55.7 us (36%)
  blocking collectives  27.9 us (18%)
  waiting for transfers between devices  27.2 us (18%)
  between operations  14.4 us (9%)
  Pallas kernels  12.5 us (8%)
  local copies, waits for them, and re-layouts  7.79 us (5%)
  other arithmetic  5.34 us (3%)
    ppermute x9, starting transfers between devices, moved(): return lax.ppermute(value, ('obj', 'pat'), pairs)  37.9 us
    all_gather x1, blocking collectives, local(): lax.all_gather(low, 'pat', axis=0, tiled=True, axis_index_groups=same_core)  27.9 us
    ppermute x9, waiting for transfers between devices, moved(): return lax.ppermute(value, ('obj', 'pat'), pairs)  15.2 us
    all_to_all x1, waiting for transfers between devices, local(): lax.all_to_all(both_low, 'pat', 0, 0, axis_index_groups=same_core)  8.92 us
    pallas_call x1, Pallas kernels, patch_sums(): pl.pallas_call(slots_kernel, out_shape=(own_chunk, own_chunk, low_chunk,...  8.28 us
    ppermute x1, starting transfers between devices, local(): low_other = lax.ppermute(low_mine, 'pat', sibling)  7.64 us
    all_to_all x1, starting transfers between devices, local(): lax.all_to_all(both_low, 'pat', 0, 0, axis_index_groups=same_core)  5.65 us
    pallas_call x1, Pallas kernels, weight_rows(): pl.pallas_call(weight_kernel, out_shape=jax.ShapeDtypeStruct((OWN, WIDE),...  4.21 us
  transfers between devices with their start and end apart: 15, of which 9 were waited for; matrix products, arithmetic and copies ran while one was open for 6% of the time, Pallas kernels for 3%

profile of v4, /device:TPU:1, one launch (start us, length us, event | category | flops | bytes accessed | tf_op | source)
XLA Modules:
  0.0 150.8 jit_solution(1320493800750092581)
XLA Ops:
  6.5 0.8 slice_bitcast_fusion.3
  7.3 1.3 collective-permute-start
  8.6 0.9 slice_bitcast_fusion
  10.2 0.7 convert_element_type.22
  10.9 0.1 copy.10
  11.0 0.1 convert_element_type.23
  11.1 2.7 %collective-permute-done = f32[32,512]{1,0:T(8,128)S(1)} collective-permute-done((f32[32,512]{1,0:T(8,128)S(1)}, f32[32,512]{1,0:T(8,128)S(1)}, u32[]{:S(2)}, u32[]{:S(2)}) %collective-permute-start) | collective-permute-done | bytes 65568 | tf_op jit(solution)/shard_map/ppermute | solution.py:227
  13.8 0.8 concatenate.48
  14.6 0.0 all-gather.2.cloned.1.call-update
  14.6 0.0 reduce-scatter.2.cloned.1.call-start
  14.7 1.0 fusion.8
  15.6 1.3 collective-permute-start.1
  16.9 0.7 collective-permute-start.2
  17.6 10.1 %collective-permute-done.1 = f32[16,1536]{1,0:T(8,128)S(1)} collective-permute-done((f32[16,1536]{1,0:T(8,128)S(1)}, f32[16,1536]{1,0:T(8,128)S(1)}, u32[]{:S(2)}, u32[]{:S(2)}) %collective-permute-start.1) | collective-permute-done | bytes 98336 | tf_op jit(solution)/shard_map/ppermute | solution.py:227
  27.7 27.9 %all_gather.7 = f32[128,1536]{1,0:T(8,128)S(1)} all-gather(f32[16,1536]{1,0:T(8,128)S(1)} %add.55), channel_id=1, replica_groups={{0,2,4,6,8,10,12,14},{1,3,5,7,9,11,13,15},{16,18,20,22,24,26,28,30},{17..., dimensions={0}, use_global_device_ids=true | all-gather | bytes 884736 | tf_op jit(solution)/shard_map/all_gather | solution.py:250
  55.6 7.6 %collective-permute-start.3 = (f32[8,16,1536]{2,1,0:T(8,128)S(1)}, f32[8,16,1536]{2,1,0:T(8,128)S(1)}, u32[]{:S(2)}, u32[]{:S(2)}) collective-permute-start(f32[8,16,1536]{2,1,0:T(8,128)S(1)} %bitcast.32), channel_id=1, source_target_pairs={{0,1},{1,0},{2,3},{3,2},{4,5},{5,4},{6,7},{7,6},{8,9},{9,8},{10,11... | collective-permute-start | bytes 2359304 | tf_op jit(solution)/shard_map/ppermute | solution.py:252
  63.3 0.7 copy.11.corners
  64.0 1.2 collective-permute-done.3.low_other
  65.2 0.3 all-gather.2.cloned.1.call-done.own_hbm
  65.5 0.6 copy-done.5
  66.1 8.3 %patch_sums.1 = (f32[8,32,1536]{2,1,0:T(8,128)}, f32[8,32,1536]{2,1,0:T(8,128)}, f32[8,16,1536]{2,1,0:T(8,128)}, f32[8,16,1536]{2,1,0:T(8,128)}) custom-call(s32[4,2]{1,0:T(4,128)} %copy.11.corners, s32[1,1]{1,0:T(1,128)S(6)} %copy.17.live, s32[1]{0:T(128)} %bitcast.1.me, f32[512,1536]{1,0:T(8,128)} %all-gather.2.cloned.1.call-done.own_hbm, ...), custom_call_target="tpu_custom_call" | custom-call | flops 2000000000 | bytes 12000000 | tf_op jit(solution)/shard_map/patch_sums/pallas_call | solution.py:185
  74.4 2.4 %collective-permute-start.4 = (f32[8,32,1536]{2,1,0:T(8,128)}, f32[8,32,1536]{2,1,0:T(8,128)S(1)}, u32[]{:S(2)}, u32[]{:S(2)}) collective-permute-start(f32[8,32,1536]{2,1,0:T(8,128)} %get-tuple-element.43), channel_id=1, source_target_pairs={{0,1},{1,0},{2,3},{3,2},{4,5},{5,4},{6,7},{7,6},{8,9},{9,8},{10,11... | collective-permute-start | bytes 4718600 | tf_op jit(solution)/shard_map/ppermute | solution.py:259
  76.8 2.0 %collective-permute-start.5 = (f32[8,16,1536]{2,1,0:T(8,128)}, f32[8,16,1536]{2,1,0:T(8,128)}, u32[]{:S(2)}, u32[]{:S(2)}) collective-permute-start(f32[8,16,1536]{2,1,0:T(8,128)} %get-tuple-element.45), channel_id=1, source_target_pairs={{0,1},{1,0},{2,3},{3,2},{4,5},{5,4},{6,7},{7,6},{8,9},{9,8},{10,11... | collective-permute-start | bytes 2359304 | tf_op jit(solution)/shard_map/ppermute | solution.py:258
  78.9 0.9 slice.262
  79.8 0.1 copy.15
  79.9 1.5 collective-permute-done.5
  81.3 2.4 %add.57 = f32[8,16,1536]{2,1,0:T(8,128)} add(f32[8,16,1536]{2,1,0:T(8,128)} %get-tuple-element.44, f32[8,16,1536]{2,1,0:T(8,128)} %collective-permute-done.5) | non-fusion elementwise | flops 196608 | bytes 2359296 | tf_op jit(solution)/shard_map/add | solution.py:261
  83.7 1.4 add.56
  85.1 0.0 reduce-scatter.2.cloned.1.call-update
  85.1 5.6 %all-to-all-start = ((f32[8,16,1536]{2,1,0:T(8,128)}), f32[8,16,1536]{2,1,0:T(8,128)S(1)}, u32[]{:S(2)}, u32[]{:S(2)}) async-start(f32[8,16,1536]{2,1,0:T(8,128)} %add.57), calls=%async_computation.1 | async-start | bytes 1572864 | tf_op jit(solution)/shard_map/all_to_all | solution.py:271
  90.8 0.1 copy.14
  90.9 11.8 %collective-permute-start.9 = (f32[16,128]{1,0:T(8,128)S(1)}, f32[16,128]{1,0:T(8,128)S(1)}, u32[]{:S(2)}, u32[]{:S(2)}) collective-permute-start(f32[16,128]{1,0:T(8,128)S(1)} %pad.9), channel_id=1, source_target_pairs={{0,64},{1,65},{2,66},{3,67},{4,68},{5,69},{6,70},{7,71},{8,72},{9,... | collective-permute-start | bytes 24584 | tf_op jit(solution)/shard_map/ppermute | solution.py:227
  102.6 0.8 collective-permute-done.9
  103.4 0.2 slice_reduce_fusion.live
  103.6 4.2 %weight_rows.1 = f32[32,768]{1,0:T(8,128)S(1)} custom-call(s32[32,8]{1,0:T(8,128)S(1)} %bitcast.29, s32[32]{0:T(128)S(1)} %slice_reduce_fusion.live, s32[1]{0:T(128)} %bitcast.1.me, f32[2,256,256]{2,1,0:T(8,128)S(1)} %copy-done), custom_call_target="tpu_custom_call" | custom-call | flops 10000000 | bytes 1000000 | tf_op jit(solution)/shard_map/weight_rows/pallas_call | solution.py:208
  107.8 8.9 %all-to-all-done = f32[8,16,1536]{2,1,0:T(8,128)S(1)} async-done(((f32[8,16,1536]{2,1,0:T(8,128)}), f32[8,16,1536]{2,1,0:T(8,128)S(1)}, u32[]{:S(2)}, u32[]{:S(2)}) %all-to-all-start) | async-done | bytes 786464 | tf_op jit(solution)/shard_map/all_to_all | solution.py:271
  116.8 0.0 copy-start.2
  116.8 0.8 collective-permute-start.6
  117.6 14.6 %collective-permute-start.8 = (f32[16,1024]{1,0:T(8,128)S(1)}, f32[16,1024]{1,0:T(8,128)S(1)}, u32[]{:S(2)}, u32[]{:S(2)}) collective-permute-start(f32[16,1024]{1,0:T(8,128)S(1)} %pad_maximum_fusion.4), channel_id=1, source_target_pairs={{0,64},{1,65},{2,66},{3,67},{4,68},{5,69},{6,70},{7,71},{16,80},{1... | collective-permute-start | bytes 196616 | tf_op jit(solution)/shard_map/ppermute | solution.py:227
  132.3 0.7 collective-permute-start.7
  133.0 3.4 %collective-permute-start.11 = (f32[16,512]{1,0:T(8,128)S(1)}, f32[16,512]{1,0:T(8,128)S(1)}, u32[]{:S(2)}, u32[]{:S(2)}) collective-permute-start(f32[16,512]{1,0:T(8,128)S(1)} %pad_maximum_fusion.9), channel_id=1, source_target_pairs={{0,80},{1,81},{2,82},{3,83},{4,84},{5,85},{6,86},{7,87},{16,96},{1... | collective-permute-start | bytes 98312 | tf_op jit(solution)/shard_map/ppermute | solution.py:227
  136.3 0.0 reduce-scatter.2.cloned.1.call-done
  136.4 0.8 fusion.6
  137.2 3.5 %collective-permute-start.10 = (f32[32,768]{1,0:T(8,128)S(1)}, f32[32,768]{1,0:T(8,128)S(1)}, u32[]{:S(2)}, u32[]{:S(2)}) collective-permute-start(f32[32,768]{1,0:T(8,128)S(1)} %pad_maximum_fusion.1), channel_id=1, source_target_pairs={{0,16},{1,17},{2,18},{3,19},{4,20},{5,21},{6,22},{7,23},{8,24},{9,... | collective-permute-start | bytes 294920 | tf_op jit(solution)/shard_map/ppermute | solution.py:227
  140.6 0.9 fusion.7
  141.6 0.6 collective-permute-done.10
  142.3 0.9 collective-permute-done.11
  143.3 0.7 maximum_bitcast_fusion
  (42 shorter events, 0.3 us)
Async XLA Ops:
  6.5 56.8 %copy-start.4 = (s32[1,1,4,2]{2,3,1,0:T(2,128)S(1)}, s32[1,1,4,2]{2,3,1,0:T(2,128)}, u32[]{:S(2)}) copy-start(s32[1,1,4,2]{2,3,1,0:T(2,128)} %param.14) | copy-start | bytes 100
  6.5 59.0 %all-gather.2.cloned.1.call-start = ((), (), s32[]{:S(2)}) async-start(), calls=%async_computation.2 | async-start | bytes 3342336 | tf_op jit(solution)/shard_map/all_gather | solution.py:245
  7.3 6.5 %collective-permute-start = (f32[32,512]{1,0:T(8,128)S(1)}, f32[32,512]{1,0:T(8,128)S(1)}, u32[]{:S(2)}, u32[]{:S(2)}) collective-permute-start(f32[32,512]{1,0:T(8,128)S(1)} %pad_maximum_fusion.3), channel_id=1, source_target_pairs={{16,0},{17,1},{18,2},{19,3},{20,4},{21,5},{22,6},{23,7},{24,8},{25... | collective-permute-start | bytes 196616 | tf_op jit(solution)/shard_map/ppermute | solution.py:227
  14.6 121.8 %reduce-scatter.2.cloned.1.call-start = ((), (), s32[]{:S(2)}) async-start(), calls=%async_computation.3 | async-start | bytes 1769472 | tf_op jit(solution)/shard_map/reduce_scatter | solution.py:264
  15.6 12.1 %collective-permute-start.1 = (f32[16,1536]{1,0:T(8,128)S(1)}, f32[16,1536]{1,0:T(8,128)S(1)}, u32[]{:S(2)}, u32[]{:S(2)}) collective-permute-start(f32[16,1536]{1,0:T(8,128)S(1)} %get-tuple-element.62), channel_id=1, source_target_pairs={{64,0},{65,1},{66,2},{67,3},{68,4},{69,5},{70,6},{71,7},{80,16},{8... | collective-permute-start | bytes 294920 | tf_op jit(solution)/shard_map/ppermute | solution.py:227
  16.9 10.8 %collective-permute-start.2 = (f32[16,1536]{1,0:T(8,128)S(1)}, f32[16,1536]{1,0:T(8,128)S(1)}, u32[]{:S(2)}, u32[]{:S(2)}) collective-permute-start(f32[16,1536]{1,0:T(8,128)S(1)} %get-tuple-element.61), channel_id=1, source_target_pairs={{64,14},{65,15},{66,12},{67,13},{68,10},{69,11},{70,8},{71,9},{80,... | collective-permute-start | bytes 294920 | tf_op jit(solution)/shard_map/ppermute | solution.py:227
  55.6 9.9 %copy-start.3 = (f32[128,1536]{1,0:T(8,128)}, f32[128,1536]{1,0:T(8,128)S(1)}, u32[]{:S(2)}) copy-start(f32[128,1536]{1,0:T(8,128)S(1)} %all_gather.7) | copy-start | bytes 2359300
  55.6 9.5 %collective-permute-start.3 = (f32[8,16,1536]{2,1,0:T(8,128)S(1)}, f32[8,16,1536]{2,1,0:T(8,128)S(1)}, u32[]{:S(2)}, u32[]{:S(2)}) collective-permute-start(f32[8,16,1536]{2,1,0:T(8,128)S(1)} %bitcast.32), channel_id=1, source_target_pairs={{0,1},{1,0},{2,3},{3,2},{4,5},{5,4},{6,7},{7,6},{8,9},{9,8},{10,11... | collective-permute-start | bytes 2359304 | tf_op jit(solution)/shard_map/ppermute | solution.py:252
  65.2 0.9 copy-start.5
  74.4 9.3 %copy-start.1 = (f32[8,32,1536]{2,1,0:T(8,128)S(1)}, f32[8,32,1536]{2,1,0:T(8,128)}, u32[]{:S(2)}) copy-start(f32[8,32,1536]{2,1,0:T(8,128)} %get-tuple-element.42) | copy-start | bytes 4718596
  74.4 9.3 %collective-permute-start.4 = (f32[8,32,1536]{2,1,0:T(8,128)}, f32[8,32,1536]{2,1,0:T(8,128)S(1)}, u32[]{:S(2)}, u32[]{:S(2)}) collective-permute-start(f32[8,32,1536]{2,1,0:T(8,128)} %get-tuple-element.43), channel_id=1, source_target_pairs={{0,1},{1,0},{2,3},{3,2},{4,5},{5,4},{6,7},{7,6},{8,9},{9,8},{10,11... | collective-permute-start | bytes 4718600 | tf_op jit(solution)/shard_map/ppermute | solution.py:259
  76.8 4.5 %collective-permute-start.5 = (f32[8,16,1536]{2,1,0:T(8,128)}, f32[8,16,1536]{2,1,0:T(8,128)}, u32[]{:S(2)}, u32[]{:S(2)}) collective-permute-start(f32[8,16,1536]{2,1,0:T(8,128)} %get-tuple-element.45), channel_id=1, source_target_pairs={{0,1},{1,0},{2,3},{3,2},{4,5},{5,4},{6,7},{7,6},{8,9},{9,8},{10,11... | collective-permute-start | bytes 2359304 | tf_op jit(solution)/shard_map/ppermute | solution.py:258
  85.1 18.5 %copy-start = (f32[2,256,256]{2,1,0:T(8,128)S(1)}, f32[2,256,256]{2,1,0:T(8,128)}, u32[]{:S(2)}) copy-start(f32[2,256,256]{2,1,0:T(8,128)} %probe.1) | copy-start | bytes 1572868
  85.1 31.6 %all-to-all-start = ((f32[8,16,1536]{2,1,0:T(8,128)}), f32[8,16,1536]{2,1,0:T(8,128)S(1)}, u32[]{:S(2)}, u32[]{:S(2)}) async-start(f32[8,16,1536]{2,1,0:T(8,128)} %add.57), calls=%async_computation.1 | async-start | bytes 1572864 | tf_op jit(solution)/shard_map/all_to_all | solution.py:271
  90.9 12.5 %collective-permute-start.9 = (f32[16,128]{1,0:T(8,128)S(1)}, f32[16,128]{1,0:T(8,128)S(1)}, u32[]{:S(2)}, u32[]{:S(2)}) collective-permute-start(f32[16,128]{1,0:T(8,128)S(1)} %pad.9), channel_id=1, source_target_pairs={{0,64},{1,65},{2,66},{3,67},{4,68},{5,69},{6,70},{7,71},{8,72},{9,... | collective-permute-start | bytes 24584 | tf_op jit(solution)/shard_map/ppermute | solution.py:227
  116.8 26.4 %copy-start.2 = (f32[1,2,32,512]{3,2,1,0:T(8,128)S(1)}, f32[1,2,32,512]{3,2,1,0:T(8,128)}, u32[]{:S(2)}) copy-start(f32[1,2,32,512]{3,2,1,0:T(8,128)} %param.11) | copy-start | bytes 393220
  116.8 24.7 %collective-permute-start.6 = (f32[16,1024]{1,0:T(8,128)S(1)}, f32[16,1024]{1,0:T(8,128)S(1)}, u32[]{:S(2)}, u32[]{:S(2)}) collective-permute-start(f32[16,1024]{1,0:T(8,128)S(1)} %pad_maximum_fusion.4), channel_id=1, source_target_pairs={{8,70},{9,71},{10,68},{11,69},{12,66},{13,67},{14,64},{15,65},{24,... | collective-permute-start | bytes 196616 | tf_op jit(solution)/shard_map/ppermute | solution.py:227
  117.6 24.0 %collective-permute-start.8 = (f32[16,1024]{1,0:T(8,128)S(1)}, f32[16,1024]{1,0:T(8,128)S(1)}, u32[]{:S(2)}, u32[]{:S(2)}) collective-permute-start(f32[16,1024]{1,0:T(8,128)S(1)} %pad_maximum_fusion.4), channel_id=1, source_target_pairs={{0,64},{1,65},{2,66},{3,67},{4,68},{5,69},{6,70},{7,71},{16,80},{1... | collective-permute-start | bytes 196616 | tf_op jit(solution)/shard_map/ppermute | solution.py:227
  132.3 9.3 %collective-permute-start.7 = (f32[16,512]{1,0:T(8,128)S(1)}, f32[16,512]{1,0:T(8,128)S(1)}, u32[]{:S(2)}, u32[]{:S(2)}) collective-permute-start(f32[16,512]{1,0:T(8,128)S(1)} %pad_maximum_fusion.9), channel_id=1, source_target_pairs={{8,86},{9,87},{10,84},{11,85},{12,82},{13,83},{14,80},{15,81},{24,... | collective-permute-start | bytes 98312 | tf_op jit(solution)/shard_map/ppermute | solution.py:227
  133.0 10.2 %collective-permute-start.11 = (f32[16,512]{1,0:T(8,128)S(1)}, f32[16,512]{1,0:T(8,128)S(1)}, u32[]{:S(2)}, u32[]{:S(2)}) collective-permute-start(f32[16,512]{1,0:T(8,128)S(1)} %pad_maximum_fusion.9), channel_id=1, source_target_pairs={{0,80},{1,81},{2,82},{3,83},{4,84},{5,85},{6,86},{7,87},{16,96},{1... | collective-permute-start | bytes 98312 | tf_op jit(solution)/shard_map/ppermute | solution.py:227
  137.2 5.1 %collective-permute-start.10 = (f32[32,768]{1,0:T(8,128)S(1)}, f32[32,768]{1,0:T(8,128)S(1)}, u32[]{:S(2)}, u32[]{:S(2)}) collective-permute-start(f32[32,768]{1,0:T(8,128)S(1)} %pad_maximum_fusion.1), channel_id=1, source_target_pairs={{0,16},{1,17},{2,18},{3,19},{4,20},{5,21},{6,22},{7,23},{8,24},{9,... | collective-permute-start | bytes 294920 | tf_op jit(solution)/shard_map/ppermute | solution.py:227
Sparse Core Ops, SparseCore 0:
  14.7 50.7 all-gather.1
  85.3 47.1 reduce-scatter.1

commit v5 on v4

--- a/solution.py
+++ b/solution.py
@@ -167,6 +167,17 @@
     lax.fori_loop(0, 2 * WORKERS * SLOTS, one, 0)
 
 
+def low_kernel(parts, mirror_main, mirror_right, direct_main, direct_right):
+    total = parts[0]
+    for y in range(1, WORKERS // 2):
+        total = total + parts[y]
+    for main, right in ((mirror_main, mirror_right), (direct_main, direct_right)):
+        main[:, :TILE] = total[:, :TILE]
+        main[:, TILE:] = total[:, WIDE:WIDE + TILE]
+        right[:, :SIDE] = total[:, TILE:WIDE]
+        right[:, SIDE:] = total[:, WIDE + TILE:]
+
+
 def smem():
     return pl.BlockSpec(memory_space=pltpu.SMEM)
 
@@ -217,6 +228,19 @@
     )(corners, live, me, probe)
 
 
+def low_sums(parts):
+    return pl.pallas_call(
+        low_kernel,
+        out_shape=(
+            jax.ShapeDtypeStruct((LOW, 2 * TILE), jnp.float32), jax.ShapeDtypeStruct((LOW, 2 * SIDE), jnp.float32)) * 2,
+        in_specs=[vmem()],
+        out_specs=(vmem(), vmem()) * 2,
+        compiler_params=pltpu.CompilerParams(vmem_limit_bytes=8 * 2**20),
+        cost_estimate=pl.CostEstimate(flops=2 * 10**5, bytes_accessed=10**6, transcendentals=0),
+        name="low_sums",
+    )(parts)
+
+
 def moved(value, tile_step, pick):
     pairs = []
     for tile in range(TILES):
@@ -258,9 +282,9 @@
     other_low = lax.ppermute(send_low, "pat", sibling)
     other_own = lax.ppermute(send_own, "pat", sibling)
     both_own = (keep_own + other_own).reshape(WORKERS // 2 * OWN, 2 * WIDE)
+    marks = own_cells.reshape(WORKERS, OWN, 2 * WIDE)[:, :2, WIDE - 8:WIDE].reshape(WORKERS, 16)
+    both_own, other_low, marks = lax.optimization_barrier((both_own, other_low, marks))
     both_low = keep_low + other_low
-    marks = own_cells.reshape(WORKERS, OWN, 2 * WIDE)[:, :2, WIDE - 8:WIDE].reshape(WORKERS, 16)
-    both_own, both_low, marks = lax.optimization_barrier((both_own, both_low, marks))
     summed_own = lax.psum_scatter(
         both_own, "pat", scatter_dimension=0, tiled=True, axis_index_groups=same_core)
 
@@ -268,7 +292,7 @@
     all_marks = jnp.concatenate([marks, upper_marks[:, :16]], 0).astype(jnp.int32)
     weights = weight_rows(all_marks[:, :8], all_marks[:, 8], me.reshape(1), probe_wave)
 
-    summed_low = jnp.sum(lax.all_to_all(both_low, "pat", 0, 0, axis_index_groups=same_core), 0)
+    mirror_main, mirror_right, direct_main, direct_right = low_sums(lax.all_to_all(both_low, "pat", 0, 0, axis_index_groups=same_core))
 
     def main_columns(rows, parts):
         return jnp.concatenate([rows[:, part * WIDE:part * WIDE + TILE] for part in range(parts)], 1)
@@ -280,9 +304,9 @@
     direct = lambda worker: worker if worker < 8 else None
     by_mirror = lambda worker: mirrored(worker) if worker >= 8 else None
 
-    def pushed_down(rows, pick):
-        below = moved(main_columns(rows, 2), GRID_C, lambda tile, worker: pick(worker))
-        corner = moved(right_columns(rows, 2), GRID_C + 1, lambda tile, worker: pick(worker) if inside(tile) else None)
+    def pushed_down(main, right, pick):
+        below = moved(main, GRID_C, lambda tile, worker: pick(worker))
+        corner = moved(right, GRID_C + 1, lambda tile, worker: pick(worker) if inside(tile) else None)
         return below, corner
 
     def with_side(here, side):
@@ -292,8 +316,8 @@
             parts += [here[:, first:cut] + side[:, part * SIDE:(part + 1) * SIDE], here[:, cut:last]]
         return jnp.concatenate(parts, 1)
 
-    from_mirror = pushed_down(summed_low, by_mirror)
-    from_direct = pushed_down(summed_low, direct)
+    from_mirror = pushed_down(mirror_main, mirror_right, by_mirror)
+    from_direct = pushed_down(direct_main, direct_right, direct)
     own_sums = jnp.concatenate([summed_own, weights], 1)
     from_left = moved(right_columns(own_sums, 3), 1, lambda tile, worker: worker if inside(tile) else None)
     main = main_columns(own_sums, 3)

time: 153 us -> 154 us (level)
  waiting for transfers between devices: 27.2 us -> 28.8 us
    ppermute x9, waiting for transfers between devices: 15.2 us -> 16.7 us  [moved(): return lax.ppermute(value, ('obj', 'pat'), pairs)]
  transfers between devices with their start and end apart: 15 -> 15, of which waited for: 9 -> 9; matrix products, arithmetic and copies ran while one was open for 6% -> 7% of each run, Pallas kernels for 3% -> 3%
where the time goes in v5:
time: 154 us; the launch traced here: 153 us
  starting transfers between devices  55.1 us (36%)
  waiting for transfers between devices  28.8 us (19%)
  blocking collectives  27.9 us (18%)
  between operations  14.3 us (9%)
  Pallas kernels  12.4 us (8%)
  local copies, waits for them, and re-layouts  8.87 us (6%)
  other arithmetic  5.32 us (3%)
    ppermute x9, starting transfers between devices, moved(): return lax.ppermute(value, ('obj', 'pat'), pairs)  37.3 us
    all_gather x1, blocking collectives, local(): lax.all_gather(low, 'pat', axis=0, tiled=True, axis_index_groups=same_core)  27.9 us
    ppermute x9, waiting for transfers between devices, moved(): return lax.ppermute(value, ('obj', 'pat'), pairs)  16.7 us
    all_to_all x1, waiting for transfers between devices, local(): lax.all_to_all(both_low, 'pat', 0, 0, axis_index_groups=same_core)  10.3 us
    pallas_call x1, Pallas kernels, patch_sums(): pl.pallas_call(slots_kernel, out_shape=(own_chunk, own_chunk, low_chunk,...  8.28 us
    ppermute x1, starting transfers between devices, local(): low_other = lax.ppermute(low_mine, 'pat', sibling)  7.64 us
    all_to_all x1, starting transfers between devices, local(): lax.all_to_all(both_low, 'pat', 0, 0, axis_index_groups=same_core)  5.74 us
    pallas_call x1, Pallas kernels, weight_rows(): pl.pallas_call(weight_kernel, out_shape=jax.ShapeDtypeStruct((OWN, WIDE),...  4.04 us
  transfers between devices with their start and end apart: 15, of which 9 were waited for; matrix products, arithmetic and copies ran while one was open for 7% of the time, Pallas kernels for 3%

profile of v5, /device:TPU:1, one launch (start us, length us, event | category | flops | bytes accessed | tf_op | source)
XLA Modules:
  0.0 152.7 jit_solution(12640813272379827572)
XLA Ops:
  6.5 0.8 slice_bitcast_fusion.3
  7.3 1.3 collective-permute-start
  8.6 0.9 slice_bitcast_fusion
  10.2 0.7 convert_element_type.22
  10.9 0.1 copy.10
  11.0 0.1 convert_element_type.23
  11.1 2.7 %collective-permute-done = f32[32,512]{1,0:T(8,128)S(1)} collective-permute-done((f32[32,512]{1,0:T(8,128)S(1)}, f32[32,512]{1,0:T(8,128)S(1)}, u32[]{:S(2)}, u32[]{:S(2)}) %collective-permute-start) | collective-permute-done | bytes 65568 | tf_op jit(solution)/shard_map/ppermute | solution.py:251
  13.8 0.8 concatenate.40
  14.6 0.0 all-gather.2.cloned.1.call-update
  14.6 0.0 reduce-scatter.2.cloned.1.call-start
  14.7 1.0 fusion.8
  15.6 1.3 collective-permute-start.1
  16.9 0.7 collective-permute-start.2
  17.6 10.1 %collective-permute-done.1 = f32[16,1536]{1,0:T(8,128)S(1)} collective-permute-done((f32[16,1536]{1,0:T(8,128)S(1)}, f32[16,1536]{1,0:T(8,128)S(1)}, u32[]{:S(2)}, u32[]{:S(2)}) %collective-permute-start.1) | collective-permute-done | bytes 98336 | tf_op jit(solution)/shard_map/ppermute | solution.py:251
  27.7 27.9 %all_gather.7 = f32[128,1536]{1,0:T(8,128)S(1)} all-gather(f32[16,1536]{1,0:T(8,128)S(1)} %add.55), channel_id=1, replica_groups={{0,2,4,6,8,10,12,14},{1,3,5,7,9,11,13,15},{16,18,20,22,24,26,28,30},{17..., dimensions={0}, use_global_device_ids=true | all-gather | bytes 884736 | tf_op jit(solution)/shard_map/all_gather | solution.py:274
  55.6 7.6 %collective-permute-start.3 = (f32[8,16,1536]{2,1,0:T(8,128)S(1)}, f32[8,16,1536]{2,1,0:T(8,128)S(1)}, u32[]{:S(2)}, u32[]{:S(2)}) collective-permute-start(f32[8,16,1536]{2,1,0:T(8,128)S(1)} %bitcast.32), channel_id=1, source_target_pairs={{0,1},{1,0},{2,3},{3,2},{4,5},{5,4},{6,7},{7,6},{8,9},{9,8},{10,11... | collective-permute-start | bytes 2359304 | tf_op jit(solution)/shard_map/ppermute | solution.py:276
  63.3 0.7 copy.11.corners
  64.0 1.2 collective-permute-done.3.low_other
  65.2 0.3 all-gather.2.cloned.1.call-done.own_hbm
  65.5 0.6 copy-done.5
  66.1 8.3 %patch_sums.1 = (f32[8,32,1536]{2,1,0:T(8,128)}, f32[8,32,1536]{2,1,0:T(8,128)}, f32[8,16,1536]{2,1,0:T(8,128)}, f32[8,16,1536]{2,1,0:T(8,128)}) custom-call(s32[4,2]{1,0:T(4,128)} %copy.11.corners, s32[1,1]{1,0:T(1,128)S(6)} %copy.17.live, s32[1]{0:T(128)} %bitcast.1.me, f32[512,1536]{1,0:T(8,128)} %all-gather.2.cloned.1.call-done.own_hbm, ...), custom_call_target="tpu_custom_call" | custom-call | flops 2000000000 | bytes 12000000 | tf_op jit(solution)/shard_map/patch_sums/pallas_call | solution.py:196
  74.4 2.3 %collective-permute-start.4 = (f32[8,32,1536]{2,1,0:T(8,128)}, f32[8,32,1536]{2,1,0:T(8,128)S(1)}, u32[]{:S(2)}, u32[]{:S(2)}) collective-permute-start(f32[8,32,1536]{2,1,0:T(8,128)} %get-tuple-element.47), channel_id=1, source_target_pairs={{0,1},{1,0},{2,3},{3,2},{4,5},{5,4},{6,7},{7,6},{8,9},{9,8},{10,11... | collective-permute-start | bytes 4718600 | tf_op jit(solution)/shard_map/ppermute | solution.py:283
  76.7 2.0 %collective-permute-start.5 = (f32[8,16,1536]{2,1,0:T(8,128)}, f32[8,16,1536]{2,1,0:T(8,128)S(1)}, u32[]{:S(2)}, u32[]{:S(2)}) collective-permute-start(f32[8,16,1536]{2,1,0:T(8,128)} %get-tuple-element.48), channel_id=1, source_target_pairs={{0,1},{1,0},{2,3},{3,2},{4,5},{5,4},{6,7},{7,6},{8,9},{9,8},{10,11... | collective-permute-start | bytes 2359304 | tf_op jit(solution)/shard_map/ppermute | solution.py:282
  78.7 0.9 slice.242
  79.6 0.1 copy.15
  79.7 0.2 collective-permute-done.4
  79.9 2.8 %add.56 = f32[8,32,1536]{2,1,0:T(8,128)} add(f32[8,32,1536]{2,1,0:T(8,128)} %get-tuple-element.46, f32[8,32,1536]{2,1,0:T(8,128)S(1)} %collective-permute-done.4) | non-fusion elementwise | flops 393216 | bytes 4718592 | tf_op jit(solution)/shard_map/add | solution.py:284
  82.7 0.0 reduce-scatter.2.cloned.1.call-update
  82.7 1.1 copy-done.3
  83.8 1.0 add.57
  84.8 5.7 %all-to-all-start = ((f32[8,16,1536]{2,1,0:T(8,128)}), f32[8,16,1536]{2,1,0:T(8,128)S(1)}, u32[]{:S(2)}, u32[]{:S(2)}) async-start(f32[8,16,1536]{2,1,0:T(8,128)} %add.57), calls=%async_computation.1 | async-start | bytes 1572864 | tf_op jit(solution)/shard_map/all_to_all | solution.py:295
  90.6 0.1 copy.14
  90.6 11.8 %collective-permute-start.9 = (f32[16,128]{1,0:T(8,128)S(1)}, f32[16,128]{1,0:T(8,128)S(1)}, u32[]{:S(2)}, u32[]{:S(2)}) collective-permute-start(f32[16,128]{1,0:T(8,128)S(1)} %pad.9), channel_id=1, source_target_pairs={{0,64},{1,65},{2,66},{3,67},{4,68},{5,69},{6,70},{7,71},{8,72},{9,... | collective-permute-start | bytes 24584 | tf_op jit(solution)/shard_map/ppermute | solution.py:251
  102.4 0.8 collective-permute-done.9
  103.2 0.2 slice_reduce_fusion.live
  103.4 4.0 %weight_rows.1 = f32[32,768]{1,0:T(8,128)S(1)} custom-call(s32[32,8]{1,0:T(8,128)S(1)} %bitcast.29, s32[32]{0:T(128)S(1)} %slice_reduce_fusion.live, s32[1]{0:T(128)} %bitcast.1.me, f32[2,256,256]{2,1,0:T(8,128)S(1)} %copy-done), custom_call_target="tpu_custom_call" | custom-call | flops 10000000 | bytes 1000000 | tf_op jit(solution)/shard_map/weight_rows/pallas_call | solution.py:219
  107.5 10.3 %all-to-all-done.parts = f32[8,16,1536]{2,1,0:T(8,128)S(1)} async-done(((f32[8,16,1536]{2,1,0:T(8,128)}), f32[8,16,1536]{2,1,0:T(8,128)S(1)}, u32[]{:S(2)}, u32[]{:S(2)}) %all-to-all-start) | async-done | bytes 786464 | tf_op jit(solution)/shard_map/all_to_all | solution.py:295
  117.8 0.7 collective-permute-start.6
  118.5 0.7 collective-permute-start.7
  119.1 14.5 %collective-permute-start.8 = (f32[16,1024]{1,0:T(8,128)S(1)}, f32[16,1024]{1,0:T(8,128)S(1)}, u32[]{:S(2)}, u32[]{:S(2)}) collective-permute-start(f32[16,1024]{1,0:T(8,128)S(1)} %get-tuple-element.55), channel_id=1, source_target_pairs={{0,64},{1,65},{2,66},{3,67},{4,68},{5,69},{6,70},{7,71},{16,80},{1... | collective-permute-start | bytes 196616 | tf_op jit(solution)/shard_map/ppermute | solution.py:251
  133.6 3.0 %collective-permute-start.11 = (f32[16,512]{1,0:T(8,128)S(1)}, f32[16,512]{1,0:T(8,128)S(1)}, u32[]{:S(2)}, u32[]{:S(2)}) collective-permute-start(f32[16,512]{1,0:T(8,128)S(1)} %get-tuple-element.61), channel_id=1, source_target_pairs={{0,80},{1,81},{2,82},{3,83},{4,84},{5,85},{6,86},{7,87},{16,96},{1... | collective-permute-start | bytes 98312 | tf_op jit(solution)/shard_map/ppermute | solution.py:251
  136.6 0.0 reduce-scatter.2.cloned.1.call-done
  136.6 0.8 fusion.6
  137.4 3.6 %collective-permute-start.10 = (f32[32,768]{1,0:T(8,128)S(1)}, f32[32,768]{1,0:T(8,128)S(1)}, u32[]{:S(2)}, u32[]{:S(2)}) collective-permute-start(f32[32,768]{1,0:T(8,128)S(1)} %pad_maximum_fusion.1), channel_id=1, source_target_pairs={{0,16},{1,17},{2,18},{3,19},{4,20},{5,21},{6,22},{7,23},{8,24},{9,... | collective-permute-start | bytes 294920 | tf_op jit(solution)/shard_map/ppermute | solution.py:251
  141.0 0.9 fusion.7
  142.0 0.6 collective-permute-done.10
  142.6 2.5 %collective-permute-done.11 = f32[16,512]{1,0:T(8,128)S(1)} collective-permute-done((f32[16,512]{1,0:T(8,128)S(1)}, f32[16,512]{1,0:T(8,128)S(1)}, u32[]{:S(2)}, u32[]{:S(2)}) %collective-permute-start.11) | collective-permute-done | bytes 32800 | tf_op jit(solution)/shard_map/ppermute | solution.py:251
  145.2 0.7 maximum_bitcast_fusion
  (38 shorter events, 0.3 us)
Async XLA Ops:
  6.5 56.8 %copy-start.4 = (s32[1,1,4,2]{2,3,1,0:T(2,128)S(1)}, s32[1,1,4,2]{2,3,1,0:T(2,128)}, u32[]{:S(2)}) copy-start(s32[1,1,4,2]{2,3,1,0:T(2,128)} %param.14) | copy-start | bytes 100
  6.5 59.0 %all-gather.2.cloned.1.call-start = ((), (), s32[]{:S(2)}) async-start(), calls=%async_computation.2 | async-start | bytes 3342336 | tf_op jit(solution)/shard_map/all_gather | solution.py:269
  7.3 6.5 %collective-permute-start = (f32[32,512]{1,0:T(8,128)S(1)}, f32[32,512]{1,0:T(8,128)S(1)}, u32[]{:S(2)}, u32[]{:S(2)}) collective-permute-start(f32[32,512]{1,0:T(8,128)S(1)} %pad_maximum_fusion.3), channel_id=1, source_target_pairs={{16,0},{17,1},{18,2},{19,3},{20,4},{21,5},{22,6},{23,7},{24,8},{25... | collective-permute-start | bytes 196616 | tf_op jit(solution)/shard_map/ppermute | solution.py:251
  14.6 122.0 %reduce-scatter.2.cloned.1.call-start = ((), (), s32[]{:S(2)}) async-start(), calls=%async_computation.3 | async-start | bytes 1769472 | tf_op jit(solution)/shard_map/reduce_scatter | solution.py:288
  15.6 12.1 %collective-permute-start.1 = (f32[16,1536]{1,0:T(8,128)S(1)}, f32[16,1536]{1,0:T(8,128)S(1)}, u32[]{:S(2)}, u32[]{:S(2)}) collective-permute-start(f32[16,1536]{1,0:T(8,128)S(1)} %get-tuple-element.70), channel_id=1, source_target_pairs={{64,0},{65,1},{66,2},{67,3},{68,4},{69,5},{70,6},{71,7},{80,16},{8... | collective-permute-start | bytes 294920 | tf_op jit(solution)/shard_map/ppermute | solution.py:251
  16.9 10.8 %collective-permute-start.2 = (f32[16,1536]{1,0:T(8,128)S(1)}, f32[16,1536]{1,0:T(8,128)S(1)}, u32[]{:S(2)}, u32[]{:S(2)}) collective-permute-start(f32[16,1536]{1,0:T(8,128)S(1)} %get-tuple-element.69), channel_id=1, source_target_pairs={{64,14},{65,15},{66,12},{67,13},{68,10},{69,11},{70,8},{71,9},{80,... | collective-permute-start | bytes 294920 | tf_op jit(solution)/shard_map/ppermute | solution.py:251
  55.6 9.9 %copy-start.2 = (f32[128,1536]{1,0:T(8,128)}, f32[128,1536]{1,0:T(8,128)S(1)}, u32[]{:S(2)}) copy-start(f32[128,1536]{1,0:T(8,128)S(1)} %all_gather.7) | copy-start | bytes 2359300
  55.6 9.5 %collective-permute-start.3 = (f32[8,16,1536]{2,1,0:T(8,128)S(1)}, f32[8,16,1536]{2,1,0:T(8,128)S(1)}, u32[]{:S(2)}, u32[]{:S(2)}) collective-permute-start(f32[8,16,1536]{2,1,0:T(8,128)S(1)} %bitcast.32), channel_id=1, source_target_pairs={{0,1},{1,0},{2,3},{3,2},{4,5},{5,4},{6,7},{7,6},{8,9},{9,8},{10,11... | collective-permute-start | bytes 2359304 | tf_op jit(solution)/shard_map/ppermute | solution.py:276
  65.2 0.9 copy-start.5
  74.4 5.5 %collective-permute-start.4 = (f32[8,32,1536]{2,1,0:T(8,128)}, f32[8,32,1536]{2,1,0:T(8,128)S(1)}, u32[]{:S(2)}, u32[]{:S(2)}) collective-permute-start(f32[8,32,1536]{2,1,0:T(8,128)} %get-tuple-element.47), channel_id=1, source_target_pairs={{0,1},{1,0},{2,3},{3,2},{4,5},{5,4},{6,7},{7,6},{8,9},{9,8},{10,11... | collective-permute-start | bytes 4718600 | tf_op jit(solution)/shard_map/ppermute | solution.py:283
  76.7 6.0 %collective-permute-start.5 = (f32[8,16,1536]{2,1,0:T(8,128)}, f32[8,16,1536]{2,1,0:T(8,128)S(1)}, u32[]{:S(2)}, u32[]{:S(2)}) collective-permute-start(f32[8,16,1536]{2,1,0:T(8,128)} %get-tuple-element.48), channel_id=1, source_target_pairs={{0,1},{1,0},{2,3},{3,2},{4,5},{5,4},{6,7},{7,6},{8,9},{9,8},{10,11... | collective-permute-start | bytes 2359304 | tf_op jit(solution)/shard_map/ppermute | solution.py:282
  82.7 1.1 copy-start.3
  83.8 19.6 %copy-start = (f32[2,256,256]{2,1,0:T(8,128)S(1)}, f32[2,256,256]{2,1,0:T(8,128)}, u32[]{:S(2)}) copy-start(f32[2,256,256]{2,1,0:T(8,128)} %probe.1) | copy-start | bytes 1572868
  84.8 32.9 %all-to-all-start = ((f32[8,16,1536]{2,1,0:T(8,128)}), f32[8,16,1536]{2,1,0:T(8,128)S(1)}, u32[]{:S(2)}, u32[]{:S(2)}) async-start(f32[8,16,1536]{2,1,0:T(8,128)} %add.57), calls=%async_computation.1 | async-start | bytes 1572864 | tf_op jit(solution)/shard_map/all_to_all | solution.py:295
  90.6 12.6 %collective-permute-start.9 = (f32[16,128]{1,0:T(8,128)S(1)}, f32[16,128]{1,0:T(8,128)S(1)}, u32[]{:S(2)}, u32[]{:S(2)}) collective-permute-start(f32[16,128]{1,0:T(8,128)S(1)} %pad.9), channel_id=1, source_target_pairs={{0,64},{1,65},{2,66},{3,67},{4,68},{5,69},{6,70},{7,71},{8,72},{9,... | collective-permute-start | bytes 24584 | tf_op jit(solution)/shard_map/ppermute | solution.py:251
  107.5 37.7 %copy-start.1 = (f32[1,2,32,512]{3,2,1,0:T(8,128)S(1)}, f32[1,2,32,512]{3,2,1,0:T(8,128)}, u32[]{:S(2)}) copy-start(f32[1,2,32,512]{3,2,1,0:T(8,128)} %param.11) | copy-start | bytes 393220
  117.8 24.0 %collective-permute-start.6 = (f32[16,1024]{1,0:T(8,128)S(1)}, f32[16,1024]{1,0:T(8,128)S(1)}, u32[]{:S(2)}, u32[]{:S(2)}) collective-permute-start(f32[16,1024]{1,0:T(8,128)S(1)} %get-tuple-element.52), channel_id=1, source_target_pairs={{8,70},{9,71},{10,68},{11,69},{12,66},{13,67},{14,64},{15,65},{24,... | collective-permute-start | bytes 196616 | tf_op jit(solution)/shard_map/ppermute | solution.py:251
  118.5 23.4 %collective-permute-start.7 = (f32[16,512]{1,0:T(8,128)S(1)}, f32[16,512]{1,0:T(8,128)S(1)}, u32[]{:S(2)}, u32[]{:S(2)}) collective-permute-start(f32[16,512]{1,0:T(8,128)S(1)} %get-tuple-element.53), channel_id=1, source_target_pairs={{8,86},{9,87},{10,84},{11,85},{12,82},{13,83},{14,80},{15,81},{24,... | collective-permute-start | bytes 98312 | tf_op jit(solution)/shard_map/ppermute | solution.py:251
  119.1 22.8 %collective-permute-start.8 = (f32[16,1024]{1,0:T(8,128)S(1)}, f32[16,1024]{1,0:T(8,128)S(1)}, u32[]{:S(2)}, u32[]{:S(2)}) collective-permute-start(f32[16,1024]{1,0:T(8,128)S(1)} %get-tuple-element.55), channel_id=1, source_target_pairs={{0,64},{1,65},{2,66},{3,67},{4,68},{5,69},{6,70},{7,71},{16,80},{1... | collective-permute-start | bytes 196616 | tf_op jit(solution)/shard_map/ppermute | solution.py:251
  133.6 11.5 %collective-permute-start.11 = (f32[16,512]{1,0:T(8,128)S(1)}, f32[16,512]{1,0:T(8,128)S(1)}, u32[]{:S(2)}, u32[]{:S(2)}) collective-permute-start(f32[16,512]{1,0:T(8,128)S(1)} %get-tuple-element.61), channel_id=1, source_target_pairs={{0,80},{1,81},{2,82},{3,83},{4,84},{5,85},{6,86},{7,87},{16,96},{1... | collective-permute-start | bytes 98312 | tf_op jit(solution)/shard_map/ppermute | solution.py:251
  137.4 5.2 %collective-permute-start.10 = (f32[32,768]{1,0:T(8,128)S(1)}, f32[32,768]{1,0:T(8,128)S(1)}, u32[]{:S(2)}, u32[]{:S(2)}) collective-permute-start(f32[32,768]{1,0:T(8,128)S(1)} %pad_maximum_fusion.1), channel_id=1, source_target_pairs={{0,16},{1,17},{2,18},{3,19},{4,20},{5,21},{6,22},{7,23},{8,24},{9,... | collective-permute-start | bytes 294920 | tf_op jit(solution)/shard_map/ppermute | solution.py:251
Sparse Core Ops, SparseCore 0:
  14.7 50.7 all-gather.1
  82.8 48.5 reduce-scatter.1

commit v6 on v5

--- a/solution.py
+++ b/solution.py
@@ -47,13 +47,14 @@
     cells, sums, wave, half, probe, pattern, left, right, sem,
 ):
     core = me[0] % 2
-    pairs = [(own_hbm, cells.at[0:TILE]), (probe_hbm, probe), (left_hbm, left), (right_hbm, right),
-             (pattern_hbm, pattern)]
+    pairs = [(own_hbm, cells.at[0:TILE]), (probe_hbm, probe)]
     for y in range(WORKERS // 2):
         mine = pl.multiple_of(low_row(2 * y + core), LOW)
         other = pl.multiple_of(low_row(2 * y + 1 - core), LOW)
         pairs.append((low_mine.at[y], cells.at[pl.ds(mine, LOW)]))
         pairs.append((low_other.at[y], cells.at[pl.ds(other, LOW)]))
+    first_needs = len(pairs)
+    pairs += [(left_hbm, left), (right_hbm, right), (pattern_hbm, pattern)]
     fetches = [pltpu.make_async_copy(source, target, sem.at[i]) for i, (source, target) in enumerate(pairs)]
     for copy in fetches:
         copy.start()
@@ -63,48 +64,53 @@
         return 0
 
     lax.fori_loop(0, WIDE // 16, clear, 0)
-    for copy in fetches:
+    for copy in fetches[:first_needs]:
         copy.wait()
 
-    def one(pair, _):
-        at = []
-        for e in range(2):
-            slot = 2 * pair + e
-            used = slot < live[0, 0]
-            row = jnp.where(used, corners[slot, 0], 0)
-            col = jnp.where(used, corners[slot, 1], 0)
-            base = pl.multiple_of(col // 128 * 128, 128)
-            at.append((used, row, base, pl.multiple_of(base + WIDE, 128), col % 128))
-        for e, (used, row, base_re, base_im, shift) in enumerate(at):
-            back = (SPAN - shift) % SPAN
+    def place(slot):
+        used = slot < live[0, 0]
+        row = jnp.where(used, corners[slot, 0], 0)
+        col = jnp.where(used, corners[slot, 1], 0)
+        base = pl.multiple_of(col // 128 * 128, 128)
+        return used, row, base, pl.multiple_of(base + WIDE, 128), col % 128
+
+    def take(slot):
+        _, row, base_re, base_im, shift = place(slot)
+        back = (SPAN - shift) % SPAN
+        columns = slice(SIDE * slot, SIDE * slot + SIDE)
+        for i in range(4):
+            here = slice(64 * i, 64 * i + 64)
+            rows = pl.ds(pl.multiple_of(row + 64 * i, 8), 64)
+            cell_re = pltpu.roll(cells[rows, pl.ds(base_re, SPAN)], back, 1)[:, :SIDE]
+            cell_im = pltpu.roll(cells[rows, pl.ds(base_im, SPAN)], back, 1)[:, :SIDE]
+            probe_re = probe[0, here, :]
+            probe_im = probe[1, here, :]
+            wave[here, columns] = (probe_re * cell_re - probe_im * cell_im).astype(jnp.bfloat16)
+            wave[64 * i + SIDE:64 * i + SIDE + 64, columns] = (
+                probe_re * cell_im + probe_im * cell_re).astype(jnp.bfloat16)
+
+    def process(count):
+        every = slice(0, SIDE * count)
+        half_way = jnp.dot(left[...], wave[:, every], preferred_element_type=jnp.float32).astype(jnp.bfloat16)
+        for e in range(count):
             columns = slice(SIDE * e, SIDE * e + SIDE)
-            for i in range(4):
-                here = slice(64 * i, 64 * i + 64)
-                rows = pl.ds(pl.multiple_of(row + 64 * i, 8), 64)
-                cell_re = pltpu.roll(cells[rows, pl.ds(base_re, SPAN)], back, 1)[:, :SIDE]
-                cell_im = pltpu.roll(cells[rows, pl.ds(base_im, SPAN)], back, 1)[:, :SIDE]
-                probe_re = probe[0, here, :]
-                probe_im = probe[1, here, :]
-                wave[here, columns] = (probe_re * cell_re - probe_im * cell_im).astype(jnp.bfloat16)
-                wave[64 * i + SIDE:64 * i + SIDE + 64, columns] = (
-                    probe_re * cell_im + probe_im * cell_re).astype(jnp.bfloat16)
-        half_way = jnp.dot(left[...], wave[...], preferred_element_type=jnp.float32).astype(jnp.bfloat16)
-        for e in range(2):
-            half[SIDE * e:SIDE * e + SIDE, :SIDE] = half_way[:SIDE, SIDE * e:SIDE * e + SIDE]
-            half[SIDE * e:SIDE * e + SIDE, SIDE:] = half_way[SIDE:, SIDE * e:SIDE * e + SIDE]
-        far = jnp.dot(half[...], right[...], preferred_element_type=jnp.float32)
+            half[columns, :SIDE] = half_way[:SIDE, columns]
+            half[columns, SIDE:] = half_way[SIDE:, columns]
+        far = jnp.dot(half[every, :], right[...], preferred_element_type=jnp.float32)
         far_re = far[:, :SIDE]
         far_im = far[:, SIDE:]
-        amplitude = pattern[pl.ds(2 * pair, 2)].reshape(2 * SIDE, SIDE).astype(jnp.float32)
+        amplitude = pattern[0:count].reshape(count * SIDE, SIDE).astype(jnp.float32)
         ratio = amplitude * lax.rsqrt(far_re * far_re + far_im * far_im + 0.01)
-        half[:, :SIDE] = (far_re * ratio).astype(jnp.bfloat16)
-        half[:, SIDE:] = (far_im * ratio).astype(jnp.bfloat16)
-        half_back = jnp.dot(half[...], left[...], preferred_element_type=jnp.float32).astype(jnp.bfloat16)
-        for e in range(2):
-            wave[:SIDE, SIDE * e:SIDE * e + SIDE] = half_back[SIDE * e:SIDE * e + SIDE, :SIDE]
-            wave[SIDE:, SIDE * e:SIDE * e + SIDE] = half_back[SIDE * e:SIDE * e + SIDE, SIDE:]
-        near = jnp.dot(right[...], wave[...], preferred_element_type=jnp.float32)
-        for e, (used, row, base_re, base_im, shift) in enumerate(at):
+        half[every, :SIDE] = (far_re * ratio).astype(jnp.bfloat16)
+        half[every, SIDE:] = (far_im * ratio).astype(jnp.bfloat16)
+        half_back = jnp.dot(half[every, :], left[...], preferred_element_type=jnp.float32).astype(jnp.bfloat16)
+        for e in range(count):
+            columns = slice(SIDE * e, SIDE * e + SIDE)
+            wave[:SIDE, columns] = half_back[columns, :SIDE]
+            wave[SIDE:, columns] = half_back[columns, SIDE:]
+        near = jnp.dot(right[...], wave[:, every], preferred_element_type=jnp.float32)
+        for e in range(count):
+            used, row, base_re, base_im, shift = place(e)
             columns = slice(SIDE * e, SIDE * e + SIDE)
             for i in range(4):
                 here = slice(64 * i, 64 * i + 64)
@@ -118,9 +124,21 @@
                 term_im = jnp.where(used, probe_re * near_im - probe_im * near_re, 0.0)
                 sums[rows, pl.ds(base_re, SPAN)] += pltpu.roll(jnp.concatenate([term_re, blank], 1), shift, 1)
                 sums[rows, pl.ds(base_im, SPAN)] += pltpu.roll(jnp.concatenate([term_im, blank], 1), shift, 1)
-        return 0
-
-    lax.fori_loop(0, (live[0, 0] + 1) // 2, one, 0)
+
+    take(0)
+    take(1)
+    for copy in fetches[first_needs:]:
+        copy.wait()
+
+    @pl.when(live[0, 0] <= 2)
+    def _():
+        process(2)
+
+    @pl.when(live[0, 0] > 2)
+    def _():
+        take(2)
+        take(3)
+        process(SLOTS)
 
     copies = []
     for y in range(WORKERS // 2):
@@ -201,8 +219,8 @@
         scratch_shapes=[
             pltpu.VMEM((WIDE, 2 * WIDE), jnp.float32),
             pltpu.VMEM((WIDE, 2 * WIDE), jnp.float32),
-            pltpu.VMEM((2 * SIDE, 2 * SIDE), jnp.bfloat16),
-            pltpu.VMEM((2 * SIDE, 2 * SIDE), jnp.bfloat16),
+            pltpu.VMEM((2 * SIDE, SLOTS * SIDE), jnp.bfloat16),
+            pltpu.VMEM((SLOTS * SIDE, 2 * SIDE), jnp.bfloat16),
             pltpu.VMEM((2, SIDE, SIDE), jnp.float32),
             pltpu.VMEM((SLOTS, SIDE, SIDE), jnp.bfloat16),
             pltpu.VMEM((2 * SIDE, 2 * SIDE), jnp.bfloat16),

time: 154 us -> 152 us (0.987)
  starting transfers between devices: 55.1 us -> 51.6 us
    all_to_all x1, starting transfers between devices: 5.74 us -> 3.86 us  [local(): lax.all_to_all(both_low, 'pat', 0, 0, axis_index_groups=same_core)]
    ppermute x9, starting transfers between devices: 37.3 us -> 35.8 us  [moved(): return lax.ppermute(value, ('obj', 'pat'), pairs)]
where the time goes in v6:
time: 152 us; the launch traced here: 151 us
  starting transfers between devices  51.6 us (34%)
  waiting for transfers between devices  29.3 us (19%)
  blocking collectives  27.9 us (18%)
  between operations  14.3 us (9%)
  Pallas kernels  13.9 us (9%)
  local copies, waits for them, and re-layouts  8.87 us (6%)
  other arithmetic  5.32 us (4%)
    ppermute x9, starting transfers between devices, moved(): return lax.ppermute(value, ('obj', 'pat'), pairs)  35.8 us
    all_gather x1, blocking collectives, local(): lax.all_gather(low, 'pat', axis=0, tiled=True, axis_index_groups=same_core)  27.9 us
    ppermute x9, waiting for transfers between devices, moved(): return lax.ppermute(value, ('obj', 'pat'), pairs)  17 us
    all_to_all x1, waiting for transfers between devices, local(): lax.all_to_all(both_low, 'pat', 0, 0, axis_index_groups=same_core)  10.4 us
    pallas_call x1, Pallas kernels, patch_sums(): pl.pallas_call(slots_kernel, out_shape=(own_chunk, own_chunk, low_chunk,...  9.51 us
    ppermute x1, starting transfers between devices, local(): low_other = lax.ppermute(low_mine, 'pat', sibling)  7.64 us
    pallas_call x1, Pallas kernels, weight_rows(): pl.pallas_call(weight_kernel, out_shape=jax.ShapeDtypeStruct((OWN, WIDE),...  4.3 us
    all_to_all x1, starting transfers between devices, local(): lax.all_to_all(both_low, 'pat', 0, 0, axis_index_groups=same_core)  3.86 us
  transfers between devices with their start and end apart: 15, of which 9 were waited for; matrix products, arithmetic and copies ran while one was open for 7% of the time, Pallas kernels for 3%

profile of v6, /device:TPU:1, one launch (start us, length us, event | category | flops | bytes accessed | tf_op | source)
XLA Modules:
  0.0 151.2 jit_solution(14964998907648818501)
XLA Ops:
  6.5 0.8 slice_bitcast_fusion.3
  7.3 1.3 collective-permute-start
  8.6 0.9 slice_bitcast_fusion
  10.2 0.7 convert_element_type.22
  10.9 0.1 copy.10
  11.0 0.1 convert_element_type.23
  11.1 2.7 %collective-permute-done = f32[32,512]{1,0:T(8,128)S(1)} collective-permute-done((f32[32,512]{1,0:T(8,128)S(1)}, f32[32,512]{1,0:T(8,128)S(1)}, u32[]{:S(2)}, u32[]{:S(2)}) %collective-permute-start) | collective-permute-done | bytes 65568 | tf_op jit(solution)/shard_map/ppermute | solution.py:269
  13.8 0.8 concatenate.40
  14.6 0.0 all-gather.2.cloned.1.call-update
  14.6 0.0 reduce-scatter.2.cloned.1.call-start
  14.7 1.0 fusion.8
  15.6 1.3 collective-permute-start.1
  16.9 0.7 collective-permute-start.2
  17.6 10.1 %collective-permute-done.1 = f32[16,1536]{1,0:T(8,128)S(1)} collective-permute-done((f32[16,1536]{1,0:T(8,128)S(1)}, f32[16,1536]{1,0:T(8,128)S(1)}, u32[]{:S(2)}, u32[]{:S(2)}) %collective-permute-start.1) | collective-permute-done | bytes 98336 | tf_op jit(solution)/shard_map/ppermute | solution.py:269
  27.7 27.9 %all_gather.7 = f32[128,1536]{1,0:T(8,128)S(1)} all-gather(f32[16,1536]{1,0:T(8,128)S(1)} %add.55), channel_id=1, replica_groups={{0,2,4,6,8,10,12,14},{1,3,5,7,9,11,13,15},{16,18,20,22,24,26,28,30},{17..., dimensions={0}, use_global_device_ids=true | all-gather | bytes 884736 | tf_op jit(solution)/shard_map/all_gather | solution.py:292
  55.6 7.6 %collective-permute-start.3 = (f32[8,16,1536]{2,1,0:T(8,128)S(1)}, f32[8,16,1536]{2,1,0:T(8,128)S(1)}, u32[]{:S(2)}, u32[]{:S(2)}) collective-permute-start(f32[8,16,1536]{2,1,0:T(8,128)S(1)} %bitcast.32), channel_id=1, source_target_pairs={{0,1},{1,0},{2,3},{3,2},{4,5},{5,4},{6,7},{7,6},{8,9},{9,8},{10,11... | collective-permute-start | bytes 2359304 | tf_op jit(solution)/shard_map/ppermute | solution.py:294
  63.3 0.7 copy.11.corners
  64.0 1.2 collective-permute-done.3.low_other
  65.2 0.3 all-gather.2.cloned.1.call-done.own_hbm
  65.5 0.6 copy-done.5
  66.1 9.5 %patch_sums.1 = (f32[8,32,1536]{2,1,0:T(8,128)}, f32[8,32,1536]{2,1,0:T(8,128)}, f32[8,16,1536]{2,1,0:T(8,128)}, f32[8,16,1536]{2,1,0:T(8,128)}) custom-call(s32[4,2]{1,0:T(4,128)} %copy.11.corners, s32[1,1]{1,0:T(1,128)S(6)} %copy.17.live, s32[1]{0:T(128)} %bitcast.1.me, f32[512,1536]{1,0:T(8,128)} %all-gather.2.cloned.1.call-done.own_hbm, ...), custom_call_target="tpu_custom_call" | custom-call | flops 2000000000 | bytes 12000000 | tf_op jit(solution)/shard_map/patch_sums/pallas_call | solution.py:214
  75.6 1.9 %collective-permute-start.4 = (f32[8,32,1536]{2,1,0:T(8,128)}, f32[8,32,1536]{2,1,0:T(8,128)S(1)}, u32[]{:S(2)}, u32[]{:S(2)}) collective-permute-start(f32[8,32,1536]{2,1,0:T(8,128)} %get-tuple-element.47), channel_id=1, source_target_pairs={{0,1},{1,0},{2,3},{3,2},{4,5},{5,4},{6,7},{7,6},{8,9},{9,8},{10,11... | collective-permute-start | bytes 4718600 | tf_op jit(solution)/shard_map/ppermute | solution.py:301
  77.5 2.4 %collective-permute-start.5 = (f32[8,16,1536]{2,1,0:T(8,128)}, f32[8,16,1536]{2,1,0:T(8,128)S(1)}, u32[]{:S(2)}, u32[]{:S(2)}) collective-permute-start(f32[8,16,1536]{2,1,0:T(8,128)} %get-tuple-element.48), channel_id=1, source_target_pairs={{0,1},{1,0},{2,3},{3,2},{4,5},{5,4},{6,7},{7,6},{8,9},{9,8},{10,11... | collective-permute-start | bytes 2359304 | tf_op jit(solution)/shard_map/ppermute | solution.py:300
  80.0 0.9 slice.242
  80.9 0.1 copy.15
  80.9 0.2 collective-permute-done.4
  81.1 2.8 %add.56 = f32[8,32,1536]{2,1,0:T(8,128)} add(f32[8,32,1536]{2,1,0:T(8,128)} %get-tuple-element.46, f32[8,32,1536]{2,1,0:T(8,128)S(1)} %collective-permute-done.4) | non-fusion elementwise | flops 393216 | bytes 4718592 | tf_op jit(solution)/shard_map/add | solution.py:302
  83.9 0.0 reduce-scatter.2.cloned.1.call-update
  84.0 1.1 copy-done.3
  85.1 1.0 add.57
  86.1 3.9 %all-to-all-start = ((f32[8,16,1536]{2,1,0:T(8,128)}), f32[8,16,1536]{2,1,0:T(8,128)S(1)}, u32[]{:S(2)}, u32[]{:S(2)}) async-start(f32[8,16,1536]{2,1,0:T(8,128)} %add.57), calls=%async_computation.1 | async-start | bytes 1572864 | tf_op jit(solution)/shard_map/all_to_all | solution.py:313
  89.9 0.1 copy.14
  90.0 11.5 %collective-permute-start.9 = (f32[16,128]{1,0:T(8,128)S(1)}, f32[16,128]{1,0:T(8,128)S(1)}, u32[]{:S(2)}, u32[]{:S(2)}) collective-permute-start(f32[16,128]{1,0:T(8,128)S(1)} %pad.9), channel_id=1, source_target_pairs={{0,64},{1,65},{2,66},{3,67},{4,68},{5,69},{6,70},{7,71},{8,72},{9,... | collective-permute-start | bytes 24584 | tf_op jit(solution)/shard_map/ppermute | solution.py:269
  101.5 0.8 collective-permute-done.9
  102.3 0.2 slice_reduce_fusion.live
  102.5 4.3 %weight_rows.1 = f32[32,768]{1,0:T(8,128)S(1)} custom-call(s32[32,8]{1,0:T(8,128)S(1)} %bitcast.29, s32[32]{0:T(128)S(1)} %slice_reduce_fusion.live, s32[1]{0:T(128)} %bitcast.1.me, f32[2,256,256]{2,1,0:T(8,128)S(1)} %copy-done), custom_call_target="tpu_custom_call" | custom-call | flops 10000000 | bytes 1000000 | tf_op jit(solution)/shard_map/weight_rows/pallas_call | solution.py:237
  106.8 10.4 %all-to-all-done.parts = f32[8,16,1536]{2,1,0:T(8,128)S(1)} async-done(((f32[8,16,1536]{2,1,0:T(8,128)}), f32[8,16,1536]{2,1,0:T(8,128)S(1)}, u32[]{:S(2)}, u32[]{:S(2)}) %all-to-all-start) | async-done | bytes 786464 | tf_op jit(solution)/shard_map/all_to_all | solution.py:313
  117.3 0.7 collective-permute-start.6
  118.0 0.7 collective-permute-start.7
  118.6 14.0 %collective-permute-start.8 = (f32[16,1024]{1,0:T(8,128)S(1)}, f32[16,1024]{1,0:T(8,128)S(1)}, u32[]{:S(2)}, u32[]{:S(2)}) collective-permute-start(f32[16,1024]{1,0:T(8,128)S(1)} %get-tuple-element.55), channel_id=1, source_target_pairs={{0,64},{1,65},{2,66},{3,67},{4,68},{5,69},{6,70},{7,71},{16,80},{1... | collective-permute-start | bytes 196616 | tf_op jit(solution)/shard_map/ppermute | solution.py:269
  132.7 2.9 %collective-permute-start.11 = (f32[16,512]{1,0:T(8,128)S(1)}, f32[16,512]{1,0:T(8,128)S(1)}, u32[]{:S(2)}, u32[]{:S(2)}) collective-permute-start(f32[16,512]{1,0:T(8,128)S(1)} %get-tuple-element.61), channel_id=1, source_target_pairs={{0,80},{1,81},{2,82},{3,83},{4,84},{5,85},{6,86},{7,87},{16,96},{1... | collective-permute-start | bytes 98312 | tf_op jit(solution)/shard_map/ppermute | solution.py:269
  135.6 0.0 reduce-scatter.2.cloned.1.call-done
  135.6 0.8 fusion.6
  136.4 2.8 %collective-permute-start.10 = (f32[32,768]{1,0:T(8,128)S(1)}, f32[32,768]{1,0:T(8,128)S(1)}, u32[]{:S(2)}, u32[]{:S(2)}) collective-permute-start(f32[32,768]{1,0:T(8,128)S(1)} %pad_maximum_fusion.1), channel_id=1, source_target_pairs={{0,16},{1,17},{2,18},{3,19},{4,20},{5,21},{6,22},{7,23},{8,24},{9,... | collective-permute-start | bytes 294920 | tf_op jit(solution)/shard_map/ppermute | solution.py:269
  139.2 0.9 fusion.7
  140.2 0.6 collective-permute-done.10
  140.8 2.8 %collective-permute-done.11 = f32[16,512]{1,0:T(8,128)S(1)} collective-permute-done((f32[16,512]{1,0:T(8,128)S(1)}, f32[16,512]{1,0:T(8,128)S(1)}, u32[]{:S(2)}, u32[]{:S(2)}) %collective-permute-start.11) | collective-permute-done | bytes 32800 | tf_op jit(solution)/shard_map/ppermute | solution.py:269
  143.7 0.7 maximum_bitcast_fusion
  (38 shorter events, 0.3 us)
Async XLA Ops:
  6.5 56.8 %copy-start.4 = (s32[1,1,4,2]{2,3,1,0:T(2,128)S(1)}, s32[1,1,4,2]{2,3,1,0:T(2,128)}, u32[]{:S(2)}) copy-start(s32[1,1,4,2]{2,3,1,0:T(2,128)} %param.14) | copy-start | bytes 100
  6.5 59.0 %all-gather.2.cloned.1.call-start = ((), (), s32[]{:S(2)}) async-start(), calls=%async_computation.2 | async-start | bytes 3342336 | tf_op jit(solution)/shard_map/all_gather | solution.py:287
  7.3 6.5 %collective-permute-start = (f32[32,512]{1,0:T(8,128)S(1)}, f32[32,512]{1,0:T(8,128)S(1)}, u32[]{:S(2)}, u32[]{:S(2)}) collective-permute-start(f32[32,512]{1,0:T(8,128)S(1)} %pad_maximum_fusion.3), channel_id=1, source_target_pairs={{16,0},{17,1},{18,2},{19,3},{20,4},{21,5},{22,6},{23,7},{24,8},{25... | collective-permute-start | bytes 196616 | tf_op jit(solution)/shard_map/ppermute | solution.py:269
  14.6 121.0 %reduce-scatter.2.cloned.1.call-start = ((), (), s32[]{:S(2)}) async-start(), calls=%async_computation.3 | async-start | bytes 1769472 | tf_op jit(solution)/shard_map/reduce_scatter | solution.py:306
  15.6 12.1 %collective-permute-start.1 = (f32[16,1536]{1,0:T(8,128)S(1)}, f32[16,1536]{1,0:T(8,128)S(1)}, u32[]{:S(2)}, u32[]{:S(2)}) collective-permute-start(f32[16,1536]{1,0:T(8,128)S(1)} %get-tuple-element.70), channel_id=1, source_target_pairs={{64,0},{65,1},{66,2},{67,3},{68,4},{69,5},{70,6},{71,7},{80,16},{8... | collective-permute-start | bytes 294920 | tf_op jit(solution)/shard_map/ppermute | solution.py:269
  16.9 10.8 %collective-permute-start.2 = (f32[16,1536]{1,0:T(8,128)S(1)}, f32[16,1536]{1,0:T(8,128)S(1)}, u32[]{:S(2)}, u32[]{:S(2)}) collective-permute-start(f32[16,1536]{1,0:T(8,128)S(1)} %get-tuple-element.69), channel_id=1, source_target_pairs={{64,14},{65,15},{66,12},{67,13},{68,10},{69,11},{70,8},{71,9},{80,... | collective-permute-start | bytes 294920 | tf_op jit(solution)/shard_map/ppermute | solution.py:269
  55.6 9.9 %copy-start.2 = (f32[128,1536]{1,0:T(8,128)}, f32[128,1536]{1,0:T(8,128)S(1)}, u32[]{:S(2)}) copy-start(f32[128,1536]{1,0:T(8,128)S(1)} %all_gather.7) | copy-start | bytes 2359300
  55.6 9.5 %collective-permute-start.3 = (f32[8,16,1536]{2,1,0:T(8,128)S(1)}, f32[8,16,1536]{2,1,0:T(8,128)S(1)}, u32[]{:S(2)}, u32[]{:S(2)}) collective-permute-start(f32[8,16,1536]{2,1,0:T(8,128)S(1)} %bitcast.32), channel_id=1, source_target_pairs={{0,1},{1,0},{2,3},{3,2},{4,5},{5,4},{6,7},{7,6},{8,9},{9,8},{10,11... | collective-permute-start | bytes 2359304 | tf_op jit(solution)/shard_map/ppermute | solution.py:294
  65.2 0.9 copy-start.5
  75.6 5.5 %collective-permute-start.4 = (f32[8,32,1536]{2,1,0:T(8,128)}, f32[8,32,1536]{2,1,0:T(8,128)S(1)}, u32[]{:S(2)}, u32[]{:S(2)}) collective-permute-start(f32[8,32,1536]{2,1,0:T(8,128)} %get-tuple-element.47), channel_id=1, source_target_pairs={{0,1},{1,0},{2,3},{3,2},{4,5},{5,4},{6,7},{7,6},{8,9},{9,8},{10,11... | collective-permute-start | bytes 4718600 | tf_op jit(solution)/shard_map/ppermute | solution.py:301
  77.5 6.4 %collective-permute-start.5 = (f32[8,16,1536]{2,1,0:T(8,128)}, f32[8,16,1536]{2,1,0:T(8,128)S(1)}, u32[]{:S(2)}, u32[]{:S(2)}) collective-permute-start(f32[8,16,1536]{2,1,0:T(8,128)} %get-tuple-element.48), channel_id=1, source_target_pairs={{0,1},{1,0},{2,3},{3,2},{4,5},{5,4},{6,7},{7,6},{8,9},{9,8},{10,11... | collective-permute-start | bytes 2359304 | tf_op jit(solution)/shard_map/ppermute | solution.py:300
  83.9 1.1 copy-start.3
  85.1 17.4 %copy-start = (f32[2,256,256]{2,1,0:T(8,128)S(1)}, f32[2,256,256]{2,1,0:T(8,128)}, u32[]{:S(2)}) copy-start(f32[2,256,256]{2,1,0:T(8,128)} %probe.1) | copy-start | bytes 1572868
  86.1 31.2 %all-to-all-start = ((f32[8,16,1536]{2,1,0:T(8,128)}), f32[8,16,1536]{2,1,0:T(8,128)S(1)}, u32[]{:S(2)}, u32[]{:S(2)}) async-start(f32[8,16,1536]{2,1,0:T(8,128)} %add.57), calls=%async_computation.1 | async-start | bytes 1572864 | tf_op jit(solution)/shard_map/all_to_all | solution.py:313
  90.0 12.3 %collective-permute-start.9 = (f32[16,128]{1,0:T(8,128)S(1)}, f32[16,128]{1,0:T(8,128)S(1)}, u32[]{:S(2)}, u32[]{:S(2)}) collective-permute-start(f32[16,128]{1,0:T(8,128)S(1)} %pad.9), channel_id=1, source_target_pairs={{0,64},{1,65},{2,66},{3,67},{4,68},{5,69},{6,70},{7,71},{8,72},{9,... | collective-permute-start | bytes 24584 | tf_op jit(solution)/shard_map/ppermute | solution.py:269
  106.8 36.9 %copy-start.1 = (f32[1,2,32,512]{3,2,1,0:T(8,128)S(1)}, f32[1,2,32,512]{3,2,1,0:T(8,128)}, u32[]{:S(2)}) copy-start(f32[1,2,32,512]{3,2,1,0:T(8,128)} %param.11) | copy-start | bytes 393220
  117.3 22.8 %collective-permute-start.6 = (f32[16,1024]{1,0:T(8,128)S(1)}, f32[16,1024]{1,0:T(8,128)S(1)}, u32[]{:S(2)}, u32[]{:S(2)}) collective-permute-start(f32[16,1024]{1,0:T(8,128)S(1)} %get-tuple-element.52), channel_id=1, source_target_pairs={{8,70},{9,71},{10,68},{11,69},{12,66},{13,67},{14,64},{15,65},{24,... | collective-permute-start | bytes 196616 | tf_op jit(solution)/shard_map/ppermute | solution.py:269
  118.0 22.2 %collective-permute-start.7 = (f32[16,512]{1,0:T(8,128)S(1)}, f32[16,512]{1,0:T(8,128)S(1)}, u32[]{:S(2)}, u32[]{:S(2)}) collective-permute-start(f32[16,512]{1,0:T(8,128)S(1)} %get-tuple-element.53), channel_id=1, source_target_pairs={{8,86},{9,87},{10,84},{11,85},{12,82},{13,83},{14,80},{15,81},{24,... | collective-permute-start | bytes 98312 | tf_op jit(solution)/shard_map/ppermute | solution.py:269
  118.6 21.5 %collective-permute-start.8 = (f32[16,1024]{1,0:T(8,128)S(1)}, f32[16,1024]{1,0:T(8,128)S(1)}, u32[]{:S(2)}, u32[]{:S(2)}) collective-permute-start(f32[16,1024]{1,0:T(8,128)S(1)} %get-tuple-element.55), channel_id=1, source_target_pairs={{0,64},{1,65},{2,66},{3,67},{4,68},{5,69},{6,70},{7,71},{16,80},{1... | collective-permute-start | bytes 196616 | tf_op jit(solution)/shard_map/ppermute | solution.py:269
  132.7 10.9 %collective-permute-start.11 = (f32[16,512]{1,0:T(8,128)S(1)}, f32[16,512]{1,0:T(8,128)S(1)}, u32[]{:S(2)}, u32[]{:S(2)}) collective-permute-start(f32[16,512]{1,0:T(8,128)S(1)} %get-tuple-element.61), channel_id=1, source_target_pairs={{0,80},{1,81},{2,82},{3,83},{4,84},{5,85},{6,86},{7,87},{16,96},{1... | collective-permute-start | bytes 98312 | tf_op jit(solution)/shard_map/ppermute | solution.py:269
  136.4 4.4 %collective-permute-start.10 = (f32[32,768]{1,0:T(8,128)S(1)}, f32[32,768]{1,0:T(8,128)S(1)}, u32[]{:S(2)}, u32[]{:S(2)}) collective-permute-start(f32[32,768]{1,0:T(8,128)S(1)} %pad_maximum_fusion.1), channel_id=1, source_target_pairs={{0,16},{1,17},{2,18},{3,19},{4,20},{5,21},{6,22},{7,23},{8,24},{9,... | collective-permute-start | bytes 294920 | tf_op jit(solution)/shard_map/ppermute | solution.py:269
Sparse Core Ops, SparseCore 0:
  14.7 50.7 all-gather.1
  84.1 46.6 reduce-scatter.1

commit v7 on v6

--- a/solution.py
+++ b/solution.py
@@ -227,7 +227,7 @@
             pltpu.VMEM((2 * SIDE, 2 * SIDE), jnp.bfloat16),
             pltpu.SemaphoreType.DMA((5 + 2 * WORKERS,)),
         ],
-        compiler_params=pltpu.CompilerParams(vmem_limit_bytes=61 * 2**20),
+        compiler_params=pltpu.CompilerParams(vmem_limit_bytes=51 * 2**20),
         cost_estimate=pl.CostEstimate(flops=2 * 10**9, bytes_accessed=12 * 10**6, transcendentals=0),
         name="patch_sums",
     )(corners, live, me, own_cells, low_mine, low_other, probe, patterns, left, right)

time: 152 us -> 151 us (level)
  Pallas kernels: 13.9 us -> 11.6 us
  local copies, waits for them, and re-layouts: 8.87 us -> 6.78 us
    pallas_call x1, Pallas kernels: 9.51 us -> 7.55 us  [patch_sums(): pl.pallas_call(slots_kernel, out_shape=(own_chunk, own_chunk, low_chunk,...]
    all_to_all x1, waiting for transfers between devices: 10.4 us -> 12.3 us  [local(): lax.all_to_all(both_low, 'pat', 0, 0, axis_index_groups=same_core)]
    ppermute x9, waiting for transfers between devices: 17 us -> 15.3 us  [moved(): return lax.ppermute(value, ('obj', 'pat'), pairs)]
    unnamed x13 -> x15, local copies, waits for them, and re-layouts: 1.75 us -> 0.1 us
where the time goes in v7:
time: 151 us; the launch traced here: 149 us
  starting transfers between devices  51.9 us (34%)
  waiting for transfers between devices  30 us (20%)
  blocking collectives  27.9 us (18%)
  between operations  14.3 us (9%)
  Pallas kernels  11.6 us (8%)
  local copies, waits for them, and re-layouts  6.78 us (4%)
  other arithmetic  6.41 us (4%)
    ppermute x9, starting transfers between devices, moved(): return lax.ppermute(value, ('obj', 'pat'), pairs)  34.6 us
    all_gather x1, blocking collectives, local(): lax.all_gather(low, 'pat', axis=0, tiled=True, axis_index_groups=same_core)  27.9 us
    ppermute x9, waiting for transfers between devices, moved(): return lax.ppermute(value, ('obj', 'pat'), pairs)  15.3 us
    all_to_all x1, waiting for transfers between devices, local(): lax.all_to_all(both_low, 'pat', 0, 0, axis_index_groups=same_core)  12.3 us
    ppermute x1, starting transfers between devices, local(): low_other = lax.ppermute(low_mine, 'pat', sibling)  7.64 us
    pallas_call x1, Pallas kernels, patch_sums(): pl.pallas_call(slots_kernel, out_shape=(own_chunk, own_chunk, low_chunk,...  7.55 us
    all_to_all x1, starting transfers between devices, local(): lax.all_to_all(both_low, 'pat', 0, 0, axis_index_groups=same_core)  5.26 us
    pallas_call x1, Pallas kernels, weight_rows(): pl.pallas_call(weight_kernel, out_shape=jax.ShapeDtypeStruct((OWN, WIDE),...  4.04 us
  transfers between devices with their start and end apart: 15, of which 9 were waited for; matrix products, arithmetic and copies ran while one was open for 7% of the time, Pallas kernels for 3%

profile of v7, /device:TPU:1, one launch (start us, length us, event | category | flops | bytes accessed | tf_op | source)
XLA Modules:
  0.0 149.0 jit_solution(9305286546996420823)
XLA Ops:
  6.5 0.0 all-gather.2.cloned.1.call-start
  6.6 0.9 slice_bitcast_fusion.3
  7.5 1.3 collective-permute-start
  8.8 0.9 slice_bitcast_fusion
  10.4 0.7 convert_element_type.22
  11.0 0.1 copy.10
  11.1 0.1 convert_element_type.23
  11.3 2.7 %collective-permute-done = f32[32,512]{1,0:T(8,128)S(1)} collective-permute-done((f32[32,512]{1,0:T(8,128)S(1)}, f32[32,512]{1,0:T(8,128)S(1)}, u32[]{:S(2)}, u32[]{:S(2)}) %collective-permute-start) | collective-permute-done | bytes 65568 | tf_op jit(solution)/shard_map/ppermute | solution.py:269
  14.0 0.7 concatenate.40
  14.8 0.0 all-gather.2.cloned.1.call-update
  14.8 0.0 reduce-scatter.2.cloned.1.call-start
  14.8 1.0 fusion.8
  15.8 1.3 collective-permute-start.1
  17.1 0.7 collective-permute-start.2
  17.8 10.1 %collective-permute-done.1 = f32[16,1536]{1,0:T(8,128)S(1)} collective-permute-done((f32[16,1536]{1,0:T(8,128)S(1)}, f32[16,1536]{1,0:T(8,128)S(1)}, u32[]{:S(2)}, u32[]{:S(2)}) %collective-permute-start.1) | collective-permute-done | bytes 98336 | tf_op jit(solution)/shard_map/ppermute | solution.py:269
  27.9 27.9 %all_gather.7 = f32[128,1536]{1,0:T(8,128)S(1)} all-gather(f32[16,1536]{1,0:T(8,128)S(1)} %add.55), channel_id=1, replica_groups={{0,2,4,6,8,10,12,14},{1,3,5,7,9,11,13,15},{16,18,20,22,24,26,28,30},{17..., dimensions={0}, use_global_device_ids=true | all-gather | bytes 884736 | tf_op jit(solution)/shard_map/all_gather | solution.py:292
  55.8 7.6 %collective-permute-start.3 = (f32[8,16,1536]{2,1,0:T(8,128)S(1)}, f32[8,16,1536]{2,1,0:T(8,128)}, u32[]{:S(2)}, u32[]{:S(2)}) collective-permute-start(f32[8,16,1536]{2,1,0:T(8,128)S(1)} %bitcast.33), channel_id=1, source_target_pairs={{0,1},{1,0},{2,3},{3,2},{4,5},{5,4},{6,7},{7,6},{8,9},{9,8},{10,11... | collective-permute-start | bytes 2359304 | tf_op jit(solution)/shard_map/ppermute | solution.py:294
  63.5 0.1 copy.11.corners
  63.6 1.9 %collective-permute-done.3.low_other = f32[8,16,1536]{2,1,0:T(8,128)} collective-permute-done((f32[8,16,1536]{2,1,0:T(8,128)S(1)}, f32[8,16,1536]{2,1,0:T(8,128)}, u32[]{:S(2)}, u32[]{:S(2)}) %collective-permute-start.3) | collective-permute-done | bytes 786464 | tf_op jit(solution)/shard_map/ppermute | solution.py:294
  65.5 0.2 all-gather.2.cloned.1.call-done.own_hbm
  65.7 7.6 %patch_sums.1 = (f32[8,32,1536]{2,1,0:T(8,128)}, f32[8,32,1536]{2,1,0:T(8,128)}, f32[8,16,1536]{2,1,0:T(8,128)S(1)}, f32[8,16,1536]{2,1,0:T(8,128)}) custom-call(s32[4,2]{1,0:T(4,128)S(1)} %copy.11.corners, s32[1,1]{1,0:T(1,128)S(6)} %copy.17.live, s32[1]{0:T(128)} %bitcast.1.me, f32[512,1536]{1,0:T(8,128)} %all-gather.2.cloned.1.call-done.own_hbm, ...), custom_call_target="tpu_custom_call" | custom-call | flops 2000000000 | bytes 12000000 | tf_op jit(solution)/shard_map/patch_sums/pallas_call | solution.py:214
  73.3 2.2 %collective-permute-start.4 = (f32[8,32,1536]{2,1,0:T(8,128)}, f32[8,32,1536]{2,1,0:T(8,128)S(1)}, u32[]{:S(2)}, u32[]{:S(2)}) collective-permute-start(f32[8,32,1536]{2,1,0:T(8,128)} %get-tuple-element.47), channel_id=1, source_target_pairs={{0,1},{1,0},{2,3},{3,2},{4,5},{5,4},{6,7},{7,6},{8,9},{9,8},{10,11... | collective-permute-start | bytes 4718600 | tf_op jit(solution)/shard_map/ppermute | solution.py:301
  75.5 2.2 %collective-permute-start.5 = (f32[8,16,1536]{2,1,0:T(8,128)}, f32[8,16,1536]{2,1,0:T(8,128)}, u32[]{:S(2)}, u32[]{:S(2)}) collective-permute-start(f32[8,16,1536]{2,1,0:T(8,128)} %get-tuple-element.48), channel_id=1, source_target_pairs={{0,1},{1,0},{2,3},{3,2},{4,5},{5,4},{6,7},{7,6},{8,9},{9,8},{10,11... | collective-permute-start | bytes 2359304 | tf_op jit(solution)/shard_map/ppermute | solution.py:300
  77.6 0.9 slice.242
  78.6 0.1 copy.15
  78.6 0.2 collective-permute-done.4
  78.8 2.8 %add.56 = f32[8,32,1536]{2,1,0:T(8,128)} add(f32[8,32,1536]{2,1,0:T(8,128)} %get-tuple-element.46, f32[8,32,1536]{2,1,0:T(8,128)S(1)} %collective-permute-done.4) | non-fusion elementwise | flops 393216 | bytes 4718592 | tf_op jit(solution)/shard_map/add | solution.py:302
  81.6 0.0 reduce-scatter.2.cloned.1.call-update
  81.6 2.1 %add.57 = f32[8,16,1536]{2,1,0:T(8,128)} add(f32[8,16,1536]{2,1,0:T(8,128)S(1)} %get-tuple-element.50, f32[8,16,1536]{2,1,0:T(8,128)} %collective-permute-done.5) | non-fusion elementwise | flops 196608 | bytes 2359296 | tf_op jit(solution)/shard_map/add | solution.py:305
  83.7 5.3 %all-to-all-start = ((f32[8,16,1536]{2,1,0:T(8,128)}), f32[8,16,1536]{2,1,0:T(8,128)S(1)}, u32[]{:S(2)}, u32[]{:S(2)}) async-start(f32[8,16,1536]{2,1,0:T(8,128)} %add.57), calls=%async_computation.1 | async-start | bytes 1572864 | tf_op jit(solution)/shard_map/all_to_all | solution.py:313
  89.0 0.1 copy.14
  89.1 9.9 %collective-permute-start.9 = (f32[16,128]{1,0:T(8,128)S(1)}, f32[16,128]{1,0:T(8,128)S(1)}, u32[]{:S(2)}, u32[]{:S(2)}) collective-permute-start(f32[16,128]{1,0:T(8,128)S(1)} %pad.9), channel_id=1, source_target_pairs={{0,64},{1,65},{2,66},{3,67},{4,68},{5,69},{6,70},{7,71},{8,72},{9,... | collective-permute-start | bytes 24584 | tf_op jit(solution)/shard_map/ppermute | solution.py:269
  99.0 0.8 collective-permute-done.9
  99.8 0.2 slice_reduce_fusion.live
  100.0 4.0 %weight_rows.1 = f32[32,768]{1,0:T(8,128)S(1)} custom-call(s32[32,8]{1,0:T(8,128)S(1)} %bitcast.29, s32[32]{0:T(128)S(1)} %slice_reduce_fusion.live, s32[1]{0:T(128)} %bitcast.1.me, f32[2,256,256]{2,1,0:T(8,128)S(1)} %copy-done), custom_call_target="tpu_custom_call" | custom-call | flops 10000000 | bytes 1000000 | tf_op jit(solution)/shard_map/weight_rows/pallas_call | solution.py:237
  104.0 0.0 copy-start.4
  104.0 12.3 %all-to-all-done.parts = f32[8,16,1536]{2,1,0:T(8,128)S(1)} async-done(((f32[8,16,1536]{2,1,0:T(8,128)}), f32[8,16,1536]{2,1,0:T(8,128)S(1)}, u32[]{:S(2)}, u32[]{:S(2)}) %all-to-all-start) | async-done | bytes 786464 | tf_op jit(solution)/shard_map/all_to_all | solution.py:313
  116.4 0.7 collective-permute-start.6
  117.0 0.7 collective-permute-start.7
  117.7 11.6 %collective-permute-start.8 = (f32[16,1024]{1,0:T(8,128)S(1)}, f32[16,1024]{1,0:T(8,128)S(1)}, u32[]{:S(2)}, u32[]{:S(2)}) collective-permute-start(f32[16,1024]{1,0:T(8,128)S(1)} %get-tuple-element.55), channel_id=1, source_target_pairs={{0,64},{1,65},{2,66},{3,67},{4,68},{5,69},{6,70},{7,71},{16,80},{1... | collective-permute-start | bytes 196616 | tf_op jit(solution)/shard_map/ppermute | solution.py:269
  129.3 3.3 %collective-permute-start.11 = (f32[16,512]{1,0:T(8,128)S(1)}, f32[16,512]{1,0:T(8,128)S(1)}, u32[]{:S(2)}, u32[]{:S(2)}) collective-permute-start(f32[16,512]{1,0:T(8,128)S(1)} %get-tuple-element.61), channel_id=1, source_target_pairs={{0,80},{1,81},{2,82},{3,83},{4,84},{5,85},{6,86},{7,87},{16,96},{1... | collective-permute-start | bytes 98312 | tf_op jit(solution)/shard_map/ppermute | solution.py:269
  132.5 0.0 reduce-scatter.2.cloned.1.call-done
  132.6 0.8 fusion.6
  133.4 5.3 %collective-permute-start.10 = (f32[32,768]{1,0:T(8,128)S(1)}, f32[32,768]{1,0:T(8,128)S(1)}, u32[]{:S(2)}, u32[]{:S(2)}) collective-permute-start(f32[32,768]{1,0:T(8,128)S(1)} %pad_maximum_fusion.1), channel_id=1, source_target_pairs={{0,16},{1,17},{2,18},{3,19},{4,20},{5,21},{6,22},{7,23},{8,24},{9,... | collective-permute-start | bytes 294920 | tf_op jit(solution)/shard_map/ppermute | solution.py:269
  138.7 0.9 fusion.7
  139.7 0.6 collective-permute-done.10
  140.4 1.0 collective-permute-done.11
  141.5 0.7 maximum_bitcast_fusion
  (40 shorter events, 0.3 us)
Async XLA Ops:
  6.5 59.2 %copy-start.2 = (bf16[512,512]{1,0:T(8,128)(2,1)S(1)}, bf16[512,512]{1,0:T(8,128)(2,1)}, u32[]{:S(2)}) copy-start(bf16[512,512]{1,0:T(8,128)(2,1)} %constant.69.clone.left_hbm) | copy-start | bytes 1572868
  6.5 59.2 %copy-start.3 = (bf16[512,512]{1,0:T(8,128)(2,1)S(1)}, bf16[512,512]{1,0:T(8,128)(2,1)}, u32[]{:S(2)}) copy-start(bf16[512,512]{1,0:T(8,128)(2,1)} %constant.70.clone.right_hbm) | copy-start | bytes 1572868
  6.5 56.9 %copy-start.6 = (s32[1,1,4,2]{2,3,1,0:T(2,128)S(1)}, s32[1,1,4,2]{2,3,1,0:T(2,128)}, u32[]{:S(2)}) copy-start(s32[1,1,4,2]{2,3,1,0:T(2,128)} %param.14) | copy-start | bytes 100
  6.5 59.2 %copy-start.1 = (bf16[1,1,4,256,256]{4,3,2,1,0:T(8,128)(2,1)S(1)}, bf16[1,1,4,256,256]{4,3,2,1,0:T(8,128)(2,1)}, u32[]{:S(2)}) copy-start(bf16[1,1,4,256,256]{4,3,2,1,0:T(8,128)(2,1)} %param.13) | copy-start | bytes 1572868
  6.5 59.2 %copy-start = (f32[2,256,256]{2,1,0:T(8,128)S(1)}, f32[2,256,256]{2,1,0:T(8,128)}, u32[]{:S(2)}) copy-start(f32[2,256,256]{2,1,0:T(8,128)} %probe.1) | copy-start | bytes 1572868
  6.5 59.2 %all-gather.2.cloned.1.call-start = ((), (), s32[]{:S(2)}) async-start(), calls=%async_computation.2 | async-start | bytes 3342336 | tf_op jit(solution)/shard_map/all_gather | solution.py:287
  7.5 6.5 %collective-permute-start = (f32[32,512]{1,0:T(8,128)S(1)}, f32[32,512]{1,0:T(8,128)S(1)}, u32[]{:S(2)}, u32[]{:S(2)}) collective-permute-start(f32[32,512]{1,0:T(8,128)S(1)} %pad_maximum_fusion.3), channel_id=1, source_target_pairs={{16,0},{17,1},{18,2},{19,3},{20,4},{21,5},{22,6},{23,7},{24,8},{25... | collective-permute-start | bytes 196616 | tf_op jit(solution)/shard_map/ppermute | solution.py:269
  14.8 117.8 %reduce-scatter.2.cloned.1.call-start = ((), (), s32[]{:S(2)}) async-start(), calls=%async_computation.3 | async-start | bytes 1769472 | tf_op jit(solution)/shard_map/reduce_scatter | solution.py:306
  15.8 12.1 %collective-permute-start.1 = (f32[16,1536]{1,0:T(8,128)S(1)}, f32[16,1536]{1,0:T(8,128)S(1)}, u32[]{:S(2)}, u32[]{:S(2)}) collective-permute-start(f32[16,1536]{1,0:T(8,128)S(1)} %get-tuple-element.70), channel_id=1, source_target_pairs={{64,0},{65,1},{66,2},{67,3},{68,4},{69,5},{70,6},{71,7},{80,16},{8... | collective-permute-start | bytes 294920 | tf_op jit(solution)/shard_map/ppermute | solution.py:269
  17.1 10.8 %collective-permute-start.2 = (f32[16,1536]{1,0:T(8,128)S(1)}, f32[16,1536]{1,0:T(8,128)S(1)}, u32[]{:S(2)}, u32[]{:S(2)}) collective-permute-start(f32[16,1536]{1,0:T(8,128)S(1)} %get-tuple-element.69), channel_id=1, source_target_pairs={{64,14},{65,15},{66,12},{67,13},{68,10},{69,11},{70,8},{71,9},{80,... | collective-permute-start | bytes 294920 | tf_op jit(solution)/shard_map/ppermute | solution.py:269
  55.8 9.9 %copy-start.5 = (f32[128,1536]{1,0:T(8,128)}, f32[128,1536]{1,0:T(8,128)S(1)}, u32[]{:S(2)}) copy-start(f32[128,1536]{1,0:T(8,128)S(1)} %all_gather.7) | copy-start | bytes 2359300
  55.8 9.7 %collective-permute-start.3 = (f32[8,16,1536]{2,1,0:T(8,128)S(1)}, f32[8,16,1536]{2,1,0:T(8,128)}, u32[]{:S(2)}, u32[]{:S(2)}) collective-permute-start(f32[8,16,1536]{2,1,0:T(8,128)S(1)} %bitcast.33), channel_id=1, source_target_pairs={{0,1},{1,0},{2,3},{3,2},{4,5},{5,4},{6,7},{7,6},{8,9},{9,8},{10,11... | collective-permute-start | bytes 2359304 | tf_op jit(solution)/shard_map/ppermute | solution.py:294
  73.3 5.5 %collective-permute-start.4 = (f32[8,32,1536]{2,1,0:T(8,128)}, f32[8,32,1536]{2,1,0:T(8,128)S(1)}, u32[]{:S(2)}, u32[]{:S(2)}) collective-permute-start(f32[8,32,1536]{2,1,0:T(8,128)} %get-tuple-element.47), channel_id=1, source_target_pairs={{0,1},{1,0},{2,3},{3,2},{4,5},{5,4},{6,7},{7,6},{8,9},{9,8},{10,11... | collective-permute-start | bytes 4718600 | tf_op jit(solution)/shard_map/ppermute | solution.py:301
  75.5 6.1 %collective-permute-start.5 = (f32[8,16,1536]{2,1,0:T(8,128)}, f32[8,16,1536]{2,1,0:T(8,128)}, u32[]{:S(2)}, u32[]{:S(2)}) collective-permute-start(f32[8,16,1536]{2,1,0:T(8,128)} %get-tuple-element.48), channel_id=1, source_target_pairs={{0,1},{1,0},{2,3},{3,2},{4,5},{5,4},{6,7},{7,6},{8,9},{9,8},{10,11... | collective-permute-start | bytes 2359304 | tf_op jit(solution)/shard_map/ppermute | solution.py:300
  83.7 32.6 %all-to-all-start = ((f32[8,16,1536]{2,1,0:T(8,128)}), f32[8,16,1536]{2,1,0:T(8,128)S(1)}, u32[]{:S(2)}, u32[]{:S(2)}) async-start(f32[8,16,1536]{2,1,0:T(8,128)} %add.57), calls=%async_computation.1 | async-start | bytes 1572864 | tf_op jit(solution)/shard_map/all_to_all | solution.py:313
  89.1 10.7 %collective-permute-start.9 = (f32[16,128]{1,0:T(8,128)S(1)}, f32[16,128]{1,0:T(8,128)S(1)}, u32[]{:S(2)}, u32[]{:S(2)}) collective-permute-start(f32[16,128]{1,0:T(8,128)S(1)} %pad.9), channel_id=1, source_target_pairs={{0,64},{1,65},{2,66},{3,67},{4,68},{5,69},{6,70},{7,71},{8,72},{9,... | collective-permute-start | bytes 24584 | tf_op jit(solution)/shard_map/ppermute | solution.py:269
  104.0 37.4 %copy-start.4 = (f32[1,2,32,512]{3,2,1,0:T(8,128)S(1)}, f32[1,2,32,512]{3,2,1,0:T(8,128)}, u32[]{:S(2)}) copy-start(f32[1,2,32,512]{3,2,1,0:T(8,128)} %param.11) | copy-start | bytes 393220
  116.4 23.2 %collective-permute-start.6 = (f32[16,1024]{1,0:T(8,128)S(1)}, f32[16,1024]{1,0:T(8,128)S(1)}, u32[]{:S(2)}, u32[]{:S(2)}) collective-permute-start(f32[16,1024]{1,0:T(8,128)S(1)} %get-tuple-element.52), channel_id=1, source_target_pairs={{8,70},{9,71},{10,68},{11,69},{12,66},{13,67},{14,64},{15,65},{24,... | collective-permute-start | bytes 196616 | tf_op jit(solution)/shard_map/ppermute | solution.py:269
  117.0 22.6 %collective-permute-start.7 = (f32[16,512]{1,0:T(8,128)S(1)}, f32[16,512]{1,0:T(8,128)S(1)}, u32[]{:S(2)}, u32[]{:S(2)}) collective-permute-start(f32[16,512]{1,0:T(8,128)S(1)} %get-tuple-element.53), channel_id=1, source_target_pairs={{8,86},{9,87},{10,84},{11,85},{12,82},{13,83},{14,80},{15,81},{24,... | collective-permute-start | bytes 98312 | tf_op jit(solution)/shard_map/ppermute | solution.py:269
  117.7 22.0 %collective-permute-start.8 = (f32[16,1024]{1,0:T(8,128)S(1)}, f32[16,1024]{1,0:T(8,128)S(1)}, u32[]{:S(2)}, u32[]{:S(2)}) collective-permute-start(f32[16,1024]{1,0:T(8,128)S(1)} %get-tuple-element.55), channel_id=1, source_target_pairs={{0,64},{1,65},{2,66},{3,67},{4,68},{5,69},{6,70},{7,71},{16,80},{1... | collective-permute-start | bytes 196616 | tf_op jit(solution)/shard_map/ppermute | solution.py:269
  129.3 12.1 %collective-permute-start.11 = (f32[16,512]{1,0:T(8,128)S(1)}, f32[16,512]{1,0:T(8,128)S(1)}, u32[]{:S(2)}, u32[]{:S(2)}) collective-permute-start(f32[16,512]{1,0:T(8,128)S(1)} %get-tuple-element.61), channel_id=1, source_target_pairs={{0,80},{1,81},{2,82},{3,83},{4,84},{5,85},{6,86},{7,87},{16,96},{1... | collective-permute-start | bytes 98312 | tf_op jit(solution)/shard_map/ppermute | solution.py:269
  133.4 7.0 %collective-permute-start.10 = (f32[32,768]{1,0:T(8,128)S(1)}, f32[32,768]{1,0:T(8,128)S(1)}, u32[]{:S(2)}, u32[]{:S(2)}) collective-permute-start(f32[32,768]{1,0:T(8,128)S(1)} %pad_maximum_fusion.1), channel_id=1, source_target_pairs={{0,16},{1,17},{2,18},{3,19},{4,20},{5,21},{6,22},{7,23},{8,24},{9,... | collective-permute-start | bytes 294920 | tf_op jit(solution)/shard_map/ppermute | solution.py:269
Sparse Core Ops, SparseCore 0:
  14.9 50.7 all-gather.1
  81.7 48.7 reduce-scatter.1
